TPU v7x, 32 devices: a whole 2x2x4 slice. The times are simulated.
32 devices in a mesh: grp: 4 (over y, x), row: 8 (over z, core).
Axes of the slice: x: 2, y: 2, z: 4, core: 2. Of those that a mesh axis runs over, the one named last changes fastest.
Arguments:
- coarse_blocks: bfloat16 [2048, 64, 512], P(('grp', 'row'))
- smoother: bfloat16 [2048, 4096], P(('grp', 'row'))
- residual: bfloat16 [2048, 512], P(('grp', 'row')), may hold values from -6 to 6
- dest: int32 [2048, 1], P(('grp', 'row')), may hold values from 0 to 31, as said below
- band_cols: int32 [2048, 8], P(('grp', 'row')), may hold values from 0 to 511, as said below
- band_mask: int32 [2048, 8], P(('grp', 'row')), may hold values from 0 to 1, as said below
Outputs:
- smoothed: float32 [2048, 512], P(('grp', 'row'))
Inputs may be any that keep to these rules, and one draw needn't show every extreme that they name: `dest`: at most 2 of the rows of one device have the same owner, and in every draw some owners receive exactly 2 rows from every device. `band_cols`: every entry names the slot index, within the owner's subgroup, of a row whose owner is in the same subgroup: owner's row index * 64 + source device * 2 + its rank among that source's rows to that owner. The first entry names the row itself. `band_mask`: the first entry of every row is 1.
All inputs are finite; a program needn't handle non-finite values.
Results may differ from a plain program's by a relative error of at most 0.0035.
Values may be sent and summed in bfloat16 or wider, within the bound.
No kernel may reach another device: no remote copies, remote signals or barrier semaphores. Data moves between devices by JAX's collectives and lax.ppermute only.
A program may use at most 192 MiB of HBM per device.

v0:
```python
import jax
import jax.numpy as jnp
from jax import lax
from jax.sharding import PartitionSpec as P

NRHS = 8
CAP = 2
SWEEPS = 3


def local(coarse_blocks, smoother, residual, dest, band_cols, band_mask):
    groups = lax.axis_size("grp")
    members = lax.axis_size("row")
    devices = groups * members
    row_count = dest.shape[0]
    block_size = coarse_blocks.shape[1]
    band_count = band_cols.shape[1]
    slot_count = devices * CAP
    target = dest[:, 0]
    onehot = (target[:, None] == jnp.arange(devices, dtype=jnp.int32)[None, :]).astype(jnp.int32)
    within = jnp.sum((jnp.cumsum(onehot, axis=0) - 1) * onehot, axis=1)
    slot_of_row = target * CAP + within
    matches = (slot_of_row[None, :] == jnp.arange(slot_count, dtype=jnp.int32)[:, None]).astype(
        jnp.int32
    )
    picked = jnp.sum(matches * jnp.arange(row_count, dtype=jnp.int32)[None, :], axis=1)
    live_slot = jnp.sum(matches, axis=1).astype(jnp.bfloat16)
    keep_mask = band_mask.astype(jnp.bfloat16)
    masked = (
        coarse_blocks.reshape(row_count, block_size, band_count, block_size)
        * keep_mask[:, None, :, None]
    ).reshape(row_count, block_size, band_count * block_size)
    send_blocks = (jnp.take(masked, picked, axis=0) * live_slot[:, None, None]).reshape(
        devices, CAP, block_size, band_count * block_size
    )
    send_smooth = (jnp.take(smoother, picked, axis=0) * live_slot[:, None]).reshape(
        devices, CAP, block_size * block_size
    )
    send_right = (jnp.take(residual, picked, axis=0) * live_slot[:, None]).reshape(
        devices, CAP, NRHS * block_size
    )
    send_index = jnp.take(band_cols, picked, axis=0).reshape(devices, CAP, band_count)
    got_blocks, got_smooth, got_right = (
        lax.all_to_all(send_blocks, ("grp", "row"), split_axis=0, concat_axis=0, tiled=True),
        lax.all_to_all(send_smooth, ("grp", "row"), split_axis=0, concat_axis=0, tiled=True),
        lax.all_to_all(send_right, ("grp", "row"), split_axis=0, concat_axis=0, tiled=True),
    )
    got_index = lax.all_to_all(send_index, ("grp", "row"), split_axis=0, concat_axis=0, tiled=True)
    blocks = got_blocks.reshape(slot_count, block_size, band_count, block_size)
    smooth = got_smooth.reshape(slot_count, block_size, block_size)
    right_side = got_right.reshape(slot_count, NRHS, block_size).astype(jnp.float32)
    columns = got_index.reshape(slot_count, band_count)
    solution = jnp.zeros((slot_count, NRHS, block_size), jnp.float32)
    for sweep_index in range(SWEEPS):
        if sweep_index == 0:
            defect = right_side
        else:
            rounded = solution.astype(jnp.bfloat16).reshape(slot_count, NRHS * block_size)
            gathered = lax.all_gather(rounded, "row", axis=0, tiled=True)
            values = jnp.take(gathered, columns, axis=0).reshape(
                slot_count, band_count, NRHS, block_size
            )
            applied = jnp.einsum(
                "sibk,sbrk->sri", blocks, values, preferred_element_type=jnp.float32
            )
            defect = right_side - applied
        solution = solution + jnp.einsum(
            "sik,srk->sri", smooth, defect.astype(jnp.bfloat16), preferred_element_type=jnp.float32
        )
    return solution.reshape(slot_count, NRHS * block_size)


def solution(mesh):
    in_specs = (
        P(("grp", "row"), None, None),
        P(("grp", "row"), None),
        P(("grp", "row"), None),
        P(("grp", "row"), None),
        P(("grp", "row"), None),
        P(("grp", "row"), None),
    )
    out_specs = P(("grp", "row"), None)
    return jax.shard_map(local, mesh=mesh, in_specs=in_specs, out_specs=out_specs, check_vma=False)
```

profile of v0, /device:TPU:0, one launch (start us, length us, event | category | flops | bytes accessed | tf_op | source)
XLA Modules:
  0.0 196.6 jit_solution(16266320316438950809)
XLA Ops:
  0.0 0.8 fusion.30
  0.9 0.8 select_reduce_fusion.1
  1.7 0.7 multiply_add_fusion
  2.6 0.8 copy.13
  3.4 0.6 gather_fusion.2
  4.0 0.7 broadcast_select_fusion.2
  4.7 7.3 %all-to-all-start.2 = ((s32[32,2,8]{2,1,0:T(2,128)}), s32[32,2,8]{2,1,0:T(2,128)S(1)}, u32[]{:S(2)}, u32[]{:S(2)}) async-start(s32[32,2,8]{2,1,0:T(2,128)} %broadcast_select_fusion.2), calls=%async_computation.2 | async-start | bytes 65536 | tf_op jit(solution)/shard_map/all_to_all | solution.py:48
  12.2 1.6 gather_fusion
  13.8 0.8 fusion.29
  14.6 0.9 gather_fusion.1
  15.8 3.5 %all-to-all-done.2 = s32[32,2,8]{2,1,0:T(2,128)S(1)} async-done(((s32[32,2,8]{2,1,0:T(2,128)}), s32[32,2,8]{2,1,0:T(2,128)S(1)}, u32[]{:S(2)}, u32[]{:S(2)}) %all-to-all-start.2) | async-done | bytes 2080 | tf_op jit(solution)/shard_map/all_to_all | solution.py:48
  19.3 2.6 %all-to-all-start = ((bf16[32,2,512]{2,1,0:T(2,128)(2,1)}), bf16[32,2,512]{2,1,0:T(2,128)(2,1)S(1)}, u32[]{:S(2)}, u32[]{:S(2)}) async-start(bf16[32,2,512]{2,1,0:T(2,128)(2,1)} %fusion.29), calls=%async_computation | async-start | bytes 131072 | tf_op jit(solution)/shard_map/all_to_all | solution.py:46
  21.9 1.6 fusion.26
  23.4 5.8 %all-to-all-done = bf16[32,2,512]{2,1,0:T(2,128)(2,1)S(1)} async-done(((bf16[32,2,512]{2,1,0:T(2,128)(2,1)}), bf16[32,2,512]{2,1,0:T(2,128)(2,1)S(1)}, u32[]{:S(2)}, u32[]{:S(2)}) %all-to-all-start) | async-done | bytes 65568 | tf_op jit(solution)/shard_map/all_to_all | solution.py:46
  29.2 2.6 %all-to-all-start.1 = ((bf16[32,2,4096]{2,1,0:T(2,128)(2,1)}), bf16[32,2,4096]{2,1,0:T(2,128)(2,1)S(1)}, u32[]{:S(2)}, u32[]{:S(2)}) async-start(bf16[32,2,4096]{2,1,0:T(2,128)(2,1)} %fusion.26), calls=%async_computation.1 | async-start | bytes 1048576 | tf_op jit(solution)/shard_map/all_to_all | solution.py:45
  32.3 4.4 %broadcast_multiply_fusion = bf16[64,64,512]{2,1,0:T(8,128)(2,1)} fusion(bf16[64,64,512]{2,1,0:T(8,128)(2,1)} %param.8, bf16[64,512]{1,0:T(8,128)(2,1)S(1)} %mul.71), kind=kLoop, calls=%fused_computation.11 | loop fusion | flops 2097152 | bytes 8454144 | tf_op jit(solution)/shard_map/mul | solution.py:30
  36.7 5.0 %gather_fusion.3 = bf16[64,64,512]{2,1,0:T(8,128)(2,1)} fusion(bf16[64,64,512]{2,1,0:T(8,128)(2,1)} %broadcast_multiply_fusion, s32[1024]{0:T(1024)S(1)} %pad_clamp_fusion.1), kind=kCustom, calls=%fused_computation.5 | custom fusion | bytes 8388864 | tf_op jit(solution)/shard_map/jit(_take)/gather | solution.py:33
  41.6 4.6 %select_multiply_fusion = bf16[32,2,64,512]{3,2,1,0:T(8,128)(2,1)} fusion(bf16[32,2,64,512]{3,2,1,0:T(8,128)(2,1)} %bitcast.41, pred[32,2]{1,0:T(8,128)(4,1)S(1)} %compare_and_fusion.1, bf16[32,2]{1,0:T(8,128)(2,1)S(1)} %convert_element_type.42), kind=kLoop, calls=%fused_computation.10 | loop fusion | flops 4194304 | bytes 8388800 | tf_op jit(solution)/shard_map/mul | solution.py:33
  46.3 1.9 all-to-all-done.1
  48.2 4.0 %all-to-all-start.3 = ((bf16[32,2,64,512]{3,2,1,0:T(8,128)(2,1)}), bf16[32,2,64,512]{3,2,1,0:T(8,128)(2,1)}, u32[]{:S(2)}, u32[]{:S(2)}) async-start(bf16[32,2,64,512]{3,2,1,0:T(8,128)(2,1)} %select_multiply_fusion), calls=%async_computation.3 | async-start | bytes 8388608 | tf_op jit(solution)/shard_map/all_to_all | solution.py:44
  52.5 0.7 reshape.106
  53.2 1.4 fusion.32
  54.7 99.2 %all_gather.6 = bf16[512,512]{1,0:T(8,128)(2,1)S(1)} all-gather(bf16[64,512]{1,0:T(8,128)(2,1)S(1)} %reshape.107), channel_id=1, replica_groups=mesh['grp'=4,'row'=8] {'row'}, dimensions={0}, use_global_device_ids=true | all-gather | bytes 589824 | tf_op jit(solution)/shard_map/all_gather | solution.py:59
  153.9 2.0 gather_fusion.4
  156.0 0.5 reshape.109
  156.5 11.2 %reshape.110 = bf16[64,64,8,64]{3,2,1,0:T(8,128)(2,1)} reshape(bf16[32,2,64,512]{3,2,1,0:T(8,128)(2,1)} %all-to-all-done.3) | data formatting | bytes 8388608 | tf_op jit(solution)/shard_map/reshape | solution.py:49
  167.8 5.1 %fusion.33 = (bf16[64,8,64]{2,1,0:T(8,128)(2,1)S(1)}, f32[64,8,64]{2,1,0:T(8,128)S(1)}) fusion(f32[64,8,64]{2,1,0:T(8,128)S(1)} %copy-done.1, bf16[64,64,64]{2,1,0:T(8,128)(2,1)S(1)} %reshape.106, bf16[64,8,8,64]{3,2,1,0:T(8,128)(2,1)S(1)} %reshape.109, bf16[64,64,8,64]{3,2,1,0:T(8,128)(2,1)} %reshape.110, bf16[64,8,64]{2,1,0:T(8,128)(2,1)S(1)} %reshape.105), kind=kOutput, calls=%fused_computation.45 | convolution fusion | flops 37912576 | bytes 5636096 | tf_op jit(solution)/shard_map/sik,srk->sri/dot_general | solution.py:67
  173.1 14.9 %all_gather.7 = bf16[512,512]{1,0:T(8,128)(2,1)S(1)} all-gather(bf16[64,512]{1,0:T(8,128)(2,1)S(1)} %reshape.111), channel_id=1, replica_groups=mesh['grp'=4,'row'=8] {'row'}, dimensions={0}, use_global_device_ids=true | all-gather | bytes 589824 | tf_op jit(solution)/shard_map/all_gather | solution.py:59
  188.0 2.0 gather_fusion.5
  190.1 0.5 reshape.112
  190.6 5.1 %convolution_add_fusion = f32[64,8,64]{2,1,0:T(8,128)S(1)} fusion(f32[64,8,64]{2,1,0:T(8,128)S(1)} %get-tuple-element.11, bf16[64,64,64]{2,1,0:T(8,128)(2,1)S(1)} %reshape.106, bf16[64,8,8,64]{3,2,1,0:T(8,128)(2,1)S(1)} %reshape.112, bf16[64,64,8,64]{3,2,1,0:T(8,128)(2,1)} %reshape.110, bf16[64,8,64]{2,1,0:T(8,128)(2,1)S(1)} %reshape.105), kind=kOutput, calls=%fused_computation.14 | convolution fusion | flops 37879808 | bytes 5570560 | tf_op jit(solution)/shard_map/sik,srk->sri/dot_general | solution.py:67
  195.8 0.8 reshape.113
  (30 shorter events, 2.0 us)
Async XLA Ops:
  0.0 14.6 %copy-start = (bf16[64,4096]{1,0:T(8,128)(2,1)S(1)}, bf16[64,4096]{1,0:T(8,128)(2,1)}, u32[]{:S(2)}) copy-start(bf16[64,4096]{1,0:T(8,128)(2,1)} %param.9) | copy-start | bytes 1572868
  4.7 14.5 %all-to-all-start.2 = ((s32[32,2,8]{2,1,0:T(2,128)}), s32[32,2,8]{2,1,0:T(2,128)S(1)}, u32[]{:S(2)}, u32[]{:S(2)}) async-start(s32[32,2,8]{2,1,0:T(2,128)} %broadcast_select_fusion.2), calls=%async_computation.2 | async-start | bytes 65536 | tf_op jit(solution)/shard_map/all_to_all | solution.py:48
  13.7 18.1 %copy-start.2 = (s32[64,8]{0,1:T(8,128)S(1)}, s32[64,8]{0,1:T(8,128)}, u32[]{:S(2)}) copy-start(s32[64,8]{0,1:T(8,128)} %param.13) | copy-start | bytes 6148
  19.3 10.0 %all-to-all-start = ((bf16[32,2,512]{2,1,0:T(2,128)(2,1)}), bf16[32,2,512]{2,1,0:T(2,128)(2,1)S(1)}, u32[]{:S(2)}, u32[]{:S(2)}) async-start(bf16[32,2,512]{2,1,0:T(2,128)(2,1)} %fusion.29), calls=%async_computation | async-start | bytes 131072 | tf_op jit(solution)/shard_map/all_to_all | solution.py:46
  29.2 19.0 %all-to-all-start.1 = ((bf16[32,2,4096]{2,1,0:T(2,128)(2,1)}), bf16[32,2,4096]{2,1,0:T(2,128)(2,1)S(1)}, u32[]{:S(2)}, u32[]{:S(2)}) async-start(bf16[32,2,4096]{2,1,0:T(2,128)(2,1)} %fusion.26), calls=%async_computation.1 | async-start | bytes 1048576 | tf_op jit(solution)/shard_map/all_to_all | solution.py:45
  48.2 108.3 %all-to-all-start.3 = ((bf16[32,2,64,512]{3,2,1,0:T(8,128)(2,1)}), bf16[32,2,64,512]{3,2,1,0:T(8,128)(2,1)}, u32[]{:S(2)}, u32[]{:S(2)}) async-start(bf16[32,2,64,512]{3,2,1,0:T(8,128)(2,1)} %select_multiply_fusion), calls=%async_computation.3 | async-start | bytes 8388608 | tf_op jit(solution)/shard_map/all_to_all | solution.py:44
  156.5 11.3 %copy-start.1 = (f32[64,8,64]{2,1,0:T(8,128)S(1)}, f32[64,8,64]{2,1,0:T(8,128)}, u32[]{:S(2)}) copy-start(f32[64,8,64]{2,1,0:T(8,128)} %get-tuple-element.9) | copy-start | bytes 393220
where the time goes:
time: 197 us
  blocking collectives  114 us (58%)
  local copies, waits for them, and re-layouts  27.9 us (14%)
  starting transfers between devices  16.5 us (8%)
  other arithmetic  14.9 us (8%)
  matrix products  11.6 us (6%)
  waiting for transfers between devices  11.3 us (6%)
    all_gather x2, blocking collectives, local(): gathered = lax.all_gather(rounded, 'row', axis=0, tiled=True)  114 us
    dot_general x3, matrix products, local(): jnp.einsum('sik,srk->sri', smooth, defect.astype(jnp.bfloat16), preferred...  11.6 us
    reshape x1, local copies, waits for them, and re-layouts, local(): blocks = got_blocks.reshape(slot_count, block_size, band_count, block_size)  11.2 us
    all_to_all x1, starting transfers between devices, local(): lax.all_to_all(send_index, ('grp', 'row'), split_axis=0, concat_axis=0, t...  7.3 us
    all_to_all x1, waiting for transfers between devices, local(): lax.all_to_all(send_right, ('grp', 'row'), split_axis=0, concat_axis=0, t...  5.84 us
    gather x1, local copies, waits for them, and re-layouts, local(): jnp.take(masked, picked, axis=0) * live_slot[:, None, None]  4.97 us
    mul x1, other arithmetic, local(): jnp.take(masked, picked, axis=0) * live_slot[:, None, None]  4.61 us
    mul x1, other arithmetic, local(): coarse_blocks.reshape(row_count, block_size, band_count, block_size)  4.42 us
  transfers between devices with their start and end apart: 4, of which 3 were waited for; matrix products, arithmetic and copies ran while one was open for 13% of the time, Pallas kernels for 0%

commit v1 on v0

v1 whole, which is shorter than its diff:
```python
import functools

import jax
import jax.numpy as jnp
from jax import lax
from jax.experimental import pallas as pl
from jax.experimental.pallas import tpu as pltpu
from jax.sharding import PartitionSpec as P

NRHS = 8
CAP = 2
LANES = 128
CHUNKS = 4
VMEM_LIMIT = 48 * 1024 * 1024

TRANSPOSED = (((1,), (1,)), ((), ()))


def first_sweep(full, dest_ref, smooth_ref, right_ref, perm_ref, starts_ref, x_ref, xb_ref, rp_ref, sbd_ref, count):
    rows = dest_ref.shape[0]
    owners = starts_ref.shape[0]
    pairs = x_ref.shape[0]
    block = smooth_ref.shape[1]

    def clear(owner, carry):
        count[owner] = 0
        return carry

    lax.fori_loop(0, owners, clear, 0)
    if full:

        def start(owner, carry):
            starts_ref[owner] = owner * CAP
            return carry

        lax.fori_loop(0, owners, start, 0)
    else:

        def tally(row, carry):
            count[dest_ref[row]] = count[dest_ref[row]] + 1
            return carry

        lax.fori_loop(0, rows, tally, 0)

        def start(owner, total):
            starts_ref[owner] = total
            following = total + count[owner]
            count[owner] = 0
            return following

        lax.fori_loop(0, owners, start, jnp.int32(0))

    def place(row, carry):
        owner = dest_ref[row]
        rank = count[owner]
        count[owner] = rank + 1
        perm_ref[starts_ref[owner] + rank] = row
        return carry

    lax.fori_loop(0, rows, place, 0)

    zero = jnp.zeros((block, block), jnp.bfloat16)
    for pair in range(pairs):
        low, high = perm_ref[2 * pair], perm_ref[2 * pair + 1]
        both = jnp.concatenate(
            [
                jnp.concatenate([smooth_ref[low], zero], axis=1),
                jnp.concatenate([zero, smooth_ref[high]], axis=1),
            ],
            axis=0,
        )
        right = jnp.concatenate([right_ref[low], right_ref[high]], axis=1)
        x = lax.dot_general(right, both, TRANSPOSED, preferred_element_type=jnp.float32)
        sbd_ref[pair] = both
        rp_ref[pair] = right
        x_ref[pair] = x
        xb_ref[pair] = x.astype(jnp.bfloat16)


def later_sweep(piece_count, with_rounded, *refs):
    perm_ref, index_ref = refs[:2]
    pieces = refs[2 : 2 + piece_count]
    blocks_hbm, sbd_ref, rp_ref, x_ref = refs[2 + piece_count : 6 + piece_count]
    refs = refs[6 + piece_count :]
    out_ref = refs[0]
    rounded_ref = refs[1] if with_rounded else None
    tiles, blocks, tile_sem, block_sem = refs[2 if with_rounded else 1 :]
    pairs = x_ref.shape[0]
    rows, block, width = blocks.shape
    bands = width // block
    piece_tiles = pieces[0].shape[0]
    part = rows // CHUNKS

    tile_copies = [
        pltpu.make_async_copy(piece, tiles.at[pl.ds(number * piece_tiles, piece_tiles)], tile_sem.at[number])
        for number, piece in enumerate(pieces)
    ]
    block_copies = [
        pltpu.make_async_copy(
            blocks_hbm.at[pl.ds(number * part, part)], blocks.at[pl.ds(number * part, part)], block_sem.at[number]
        )
        for number in range(CHUNKS)
    ]
    for copy in tile_copies + block_copies:
        copy.start()
    tiles[piece_count * piece_tiles] = jnp.zeros((NRHS, LANES), jnp.bfloat16)
    for copy in tile_copies + block_copies:
        copy.wait()

    lower = lax.broadcasted_iota(jnp.int32, (NRHS, LANES), 1) < block

    def fetch(row, band):
        entry = index_ref[row * bands + band]
        tile = tiles[lax.shift_right_logical(entry, 1)].astype(jnp.float32)
        return pltpu.roll(tile, (entry & 1) * block, 1)

    def values(row):
        return [
            jnp.where(lower, fetch(row, 2 * half), fetch(row, 2 * half + 1)) for half in range(bands // 2)
        ]

    for pair in range(pairs):
        low, high = perm_ref[2 * pair], perm_ref[2 * pair + 1]
        gathered = jnp.concatenate(
            [
                jnp.concatenate(values(low), axis=1),
                jnp.concatenate(values(high), axis=1),
            ],
            axis=0,
        ).astype(jnp.bfloat16)
        weights = jnp.concatenate([blocks[low], blocks[high]], axis=0)
        applied = lax.dot_general(gathered, weights, TRANSPOSED, preferred_element_type=jnp.float32)
        image = jnp.where(lower, applied[:NRHS], applied[NRHS:])
        defect = (rp_ref[pair].astype(jnp.float32) - image).astype(jnp.bfloat16)
        x = x_ref[pair] + lax.dot_general(
            defect, sbd_ref[pair], TRANSPOSED, preferred_element_type=jnp.float32
        )
        out_ref[pair] = x
        if with_rounded:
            rounded_ref[pair] = x.astype(jnp.bfloat16)


def local(coarse_blocks, smoother, residual, dest, band_cols, band_mask):
    groups = lax.axis_size("grp")
    members = lax.axis_size("row")
    devices = groups * members
    rows, block, width = coarse_blocks.shape
    bands = band_cols.shape[1]
    pairs = rows // 2
    full = rows == devices * CAP
    smem = pl.BlockSpec(memory_space=pltpu.SMEM)
    vmem = pl.BlockSpec(memory_space=pltpu.VMEM)
    anywhere = pl.BlockSpec(memory_space=pl.ANY)
    tile_shape = (pairs, NRHS, LANES)
    params = pltpu.CompilerParams(vmem_limit_bytes=VMEM_LIMIT)

    perm, starts, x, rounded, right, smooth = pl.pallas_call(
        functools.partial(first_sweep, full),
        out_shape=(
            jax.ShapeDtypeStruct((rows,), jnp.int32),
            jax.ShapeDtypeStruct((devices,), jnp.int32),
            jax.ShapeDtypeStruct(tile_shape, jnp.float32),
            jax.ShapeDtypeStruct(tile_shape, jnp.bfloat16),
            jax.ShapeDtypeStruct(tile_shape, jnp.bfloat16),
            jax.ShapeDtypeStruct((pairs, 2 * block, 2 * block), jnp.bfloat16),
        ),
        in_specs=[smem, vmem, vmem],
        out_specs=(smem, smem, vmem, vmem, vmem, vmem),
        scratch_shapes=[pltpu.SMEM((devices,), jnp.int32)],
        compiler_params=params,
        name="first_sweep",
    )(dest.reshape(rows), smoother.reshape(rows, block, block), residual.reshape(rows, NRHS, block))

    row_bits = [1 << bit for bit in range(members.bit_length() - 2, 0, -1)]
    slots = devices * CAP
    member = band_cols // slots
    source = (band_cols % slots) // CAP
    rank = band_cols % CAP
    owner = (dest // members) * members + member
    if full:
        position = owner * CAP + rank
    else:
        table = lax.all_gather(starts, ("grp", "row"), axis=0, tiled=True)
        position = jnp.take(table, source * devices + owner, mode="clip") + rank
    relative_row = (source % members) ^ lax.axis_index("row")
    relative_group = (source // members) ^ lax.axis_index("grp")
    piece = (relative_row & 1) * groups + relative_group
    within = jnp.zeros_like(piece)
    for order, bit in enumerate(row_bits):
        within = within + ((relative_row // bit) & 1) * (1 << order)
    tile = (piece * (members // 2) + within) * pairs + position // 2
    swap = (position ^ jnp.arange(bands, dtype=jnp.int32)[None, :]) & 1
    dead = devices * pairs
    index = jnp.where(band_mask != 0, tile * 2 + swap, dead * 2).reshape(rows * bands)

    def exchange(value, axis, size, distance):
        return lax.ppermute(value, axis, [(place, place ^ distance) for place in range(size)])

    def everywhere(value):
        for bit in row_bits:
            value = jnp.concatenate([value, exchange(value, "row", members, bit)], axis=0)
        near = [value] + [exchange(value, "grp", groups, distance) for distance in range(1, groups)]
        return near + [exchange(part, "row", members, 1) for part in near]

    def sweep(x, rounded, last):
        pieces = everywhere(rounded)
        outs = [jax.ShapeDtypeStruct(tile_shape, jnp.float32)]
        if not last:
            outs.append(jax.ShapeDtypeStruct(tile_shape, jnp.bfloat16))
        return pl.pallas_call(
            functools.partial(later_sweep, len(pieces), not last),
            out_shape=tuple(outs),
            in_specs=[smem, smem] + [anywhere] * (len(pieces) + 1) + [vmem] * 3,
            out_specs=tuple([vmem] * len(outs)),
            scratch_shapes=[
                pltpu.VMEM((devices * pairs + 1, NRHS, LANES), jnp.bfloat16),
                pltpu.VMEM((rows, block, width), jnp.bfloat16),
                pltpu.SemaphoreType.DMA((len(pieces),)),
                pltpu.SemaphoreType.DMA((CHUNKS,)),
            ],
            compiler_params=params,
            name="later_sweep",
        )(perm, index, *pieces, coarse_blocks, smooth, right, x)

    x, rounded = sweep(x, rounded, False)
    (x,) = sweep(x, rounded, True)

    if not full:
        flat = x.reshape(pairs, NRHS, 2, block).transpose(0, 2, 1, 3).reshape(rows, NRHS * block)
        following = jnp.concatenate([starts[1:], jnp.full((1,), rows, jnp.int32)])
        wanted = starts[:, None] + jnp.arange(CAP, dtype=jnp.int32)[None, :]
        live = wanted < following[:, None]
        flat = jnp.where(
            live.reshape(slots, 1), jnp.take(flat, wanted.reshape(slots), axis=0, mode="clip"), 0.0
        )
        x = flat.reshape(devices, CAP, NRHS, block).transpose(0, 2, 1, 3).reshape(devices, NRHS, CAP * block)
    got = lax.all_to_all(x, ("grp", "row"), split_axis=0, concat_axis=0, tiled=True)
    got = got.reshape(devices, NRHS, CAP, block).transpose(0, 2, 1, 3)
    return got.reshape(slots, NRHS * block)


def solution(mesh):
    in_specs = (
        P(("grp", "row"), None, None),
        P(("grp", "row"), None),
        P(("grp", "row"), None),
        P(("grp", "row"), None),
        P(("grp", "row"), None),
        P(("grp", "row"), None),
    )
    out_specs = P(("grp", "row"), None)
    return jax.shard_map(local, mesh=mesh, in_specs=in_specs, out_specs=out_specs, check_vma=False)
```

time: 197 us -> 95.1 us (0.48)
  blocking collectives: 114 us -> 14.8 us
  waiting for transfers between devices: 11.3 us -> 35.6 us
  local copies, waits for them, and re-layouts: 27.9 us -> 4.91 us
  Pallas kernels: 0 us -> 21 us
  other arithmetic: 14.9 us -> 0.79 us
  matrix products: 11.6 us -> 0 us
    all_gather x2 -> x0, blocking collectives: 114 us -> none  [local(): gathered = lax.all_gather(rounded, 'row', axis=0, tiled=True)]
    ppermute x0 -> x18, waiting for transfers between devices: none -> 35.6 us  [exchange(): lax.ppermute(value, axis, [(place, place ^ distance) for place in range(s...]
    pallas_call x0 -> x3, Pallas kernels: none -> 21 us  [the longest x2 18.1 us: sweep(): pl.pallas_call(functools.partial(later_sweep, len(pieces), not last), out...]
    ppermute x0 -> x18, starting transfers between devices: none -> 17.6 us  [exchange(): lax.ppermute(value, axis, [(place, place ^ distance) for place in range(s...]
    all_to_all x4 -> x0, starting transfers between devices: 16.5 us -> none  [the longest x1 7.3 us: local(): lax.all_to_all(send_index, ('grp', 'row'), split_axis=0, concat_axis=0, t...]
    all_to_all x0 -> x1, blocking collectives: none -> 14.8 us  [local(): lax.all_to_all(x, ('grp', 'row'), split_axis=0, concat_axis=0, tiled=True)]
    gather x8 -> x0, local copies, waits for them, and re-layouts: 12.3 us -> none  [the longest x1 4.97 us: local(): jnp.take(masked, picked, axis=0) * live_slot[:, None, None]]
    dot_general x3 -> x0, matrix products: 11.6 us -> none  [local(): jnp.einsum('sik,srk->sri', smooth, defect.astype(jnp.bfloat16), preferred...]
  transfers between devices with their start and end apart: 4 -> 18, of which waited for: 3 -> 14; matrix products, arithmetic and copies ran while one was open for 13% -> 1% of each run, Pallas kernels for 0% -> 0%
where the time goes in v1:
time: 95.1 us; the launch traced here: 94.8 us
  waiting for transfers between devices  35.6 us (37%)
  Pallas kernels  21 us (22%)
  starting transfers between devices  17.6 us (19%)
  blocking collectives  14.8 us (16%)
  local copies, waits for them, and re-layouts  4.91 us (5%)
    ppermute x18, waiting for transfers between devices, exchange(): lax.ppermute(value, axis, [(place, place ^ distance) for place in range(s...  35.6 us
    pallas_call x2, Pallas kernels, sweep(): pl.pallas_call(functools.partial(later_sweep, len(pieces), not last), out...  18.1 us
    ppermute x18, starting transfers between devices, exchange(): lax.ppermute(value, axis, [(place, place ^ distance) for place in range(s...  17.6 us
    all_to_all x1, blocking collectives, local(): lax.all_to_all(x, ('grp', 'row'), split_axis=0, concat_axis=0, tiled=True)  14.8 us
    pallas_call x1, Pallas kernels, local(): pl.pallas_call(functools.partial(first_sweep, full), out_shape=(jax.Shape...  2.85 us
    reshape x1, local copies, waits for them, and re-layouts, local(): smoother.reshape(rows, block, block)  2.06 us
  transfers between devices with their start and end apart: 18, of which 14 were waited for; matrix products, arithmetic and copies ran while one was open for 1% of the time, Pallas kernels for 0%

profile of v1, /device:TPU:0, one launch (start us, length us, event | category | flops | bytes accessed | tf_op | source)
XLA Modules:
  0.0 94.8 jit_solution(18362689121749740454)
XLA Ops:
  0.0 1.0 %reshape.20.right_ref = bf16[64,8,64]{2,1,0:T(8,128)(2,1)S(1)} reshape(bf16[64,512]{1,0:T(8,128)(2,1)} %param.8) | data formatting | bytes 131072 | tf_op jit(solution)/shard_map/reshape | solution.py:172
  1.0 2.1 %reshape.19.smooth_ref = bf16[64,64,64]{2,1,0:T(8,128)(2,1)S(1)} reshape(bf16[64,4096]{1,0:T(8,128)(2,1)} %param.7) | data formatting | bytes 1048576 | tf_op jit(solution)/shard_map/reshape | solution.py:172
  3.1 0.6 copy-done
  3.7 2.9 %first_sweep.1 = (s32[64]{0:T(128)S(1)}, s32[32]{0:T(128)}, f32[32,8,128]{2,1,0:T(8,128)S(1)}, bf16[32,8,128]{2,1,0:T(8,128)(2,1)S(1)}, bf16[32,8,128]{2,1,0:T(8...) custom-call(s32[64]{0:T(128)S(1)} %bitcast.6, bf16[64,64,64]{2,1,0:T(8,128)(2,1)S(1)} %reshape.19.smooth_ref, ...), custom_call_target="tpu_custom_call" | custom-call | tf_op jit(solution)/shard_map/first_sweep/pallas_call | solution.py:157
  6.6 4.1 %collective-permute-start = (bf16[32,8,128]{2,1,0:T(8,128)(2,1)S(1)}, bf16[32,8,128]{2,1,0:T(8,128)(2,1)S(1)}, u32[]{:S(2)}, u32[]{:S(2)}) collective-permute-start(bf16[32,8,128]{2,1,0:T(8,128)(2,1)S(1)} %get-tuple-element.13), channel_id=1, source_target_pairs={{0,4},{1,5},{2,6},{3,7},{4,0},{5,1},{6,2},{7,3},{8,12},{9,13},{10,... | collective-permute-start | bytes 196616 | tf_op jit(solution)/shard_map/ppermute | solution.py:197
  10.7 3.6 %collective-permute-done = bf16[32,8,128]{2,1,0:T(8,128)(2,1)S(1)} collective-permute-done((bf16[32,8,128]{2,1,0:T(8,128)(2,1)S(1)}, bf16[32,8,128]{2,1,0:T(8,128)(2,1)S(1)}, u32[]{:S(2)}, u32[]{:S(2)}) %collective-permute-start) | collective-permute-done | bytes 65568 | tf_op jit(solution)/shard_map/ppermute | solution.py:197
  14.3 0.6 collective-permute-start.1
  15.0 4.4 %collective-permute-done.1 = bf16[64,8,128]{2,1,0:T(8,128)(2,1)S(1)} collective-permute-done((bf16[64,8,128]{2,1,0:T(8,128)(2,1)S(1)}, bf16[64,8,128]{2,1,0:T(8,128)(2,1)S(1)}, u32[]{:S(2)}, u32[]{:S(2)}) %collective-permute-start.1) | collective-permute-done | bytes 131104 | tf_op jit(solution)/shard_map/ppermute | solution.py:197
  19.4 2.7 %collective-permute-start.4 = (bf16[128,8,128]{2,1,0:T(8,128)(2,1)S(1)}, bf16[128,8,128]{2,1,0:T(8,128)(2,1)S(1)}, u32[]{:S(2)}, u32[]{:S(2)}) collective-permute-start(bf16[128,8,128]{2,1,0:T(8,128)(2,1)S(1)} %constant_dynamic-update-slice_fusion.refs_2_), channel_id=1, source_target_pairs={{0,24},{8,16},{16,8},{24,0},{1,25},{9,17},{17,9},{25,1},{2,26},{10... | collective-permute-start | bytes 786440 | tf_op jit(solution)/shard_map/ppermute | solution.py:197
  22.1 0.5 collective-permute-start.3
  22.6 0.3 collective-permute-start.2
  22.9 5.7 %collective-permute-done.4.refs_5_ = bf16[128,8,128]{2,1,0:T(8,128)(2,1)S(1)} collective-permute-done((bf16[128,8,128]{2,1,0:T(8,128)(2,1)S(1)}, bf16[128,8,128]{2,1,0:T(8,128)(2,1)S(1)}, u32[]{:S(2)}, u32[]{:S(2)}) %collective-permute-start.4) | collective-permute-done | bytes 262176 | tf_op jit(solution)/shard_map/ppermute | solution.py:197
  28.7 2.7 %collective-permute-done.3.refs_4_ = bf16[128,8,128]{2,1,0:T(8,128)(2,1)S(1)} collective-permute-done((bf16[128,8,128]{2,1,0:T(8,128)(2,1)S(1)}, bf16[128,8,128]{2,1,0:T(8,128)(2,1)S(1)}, u32[]{:S(2)}, u32[]{:S(2)}) %collective-permute-start.3) | collective-permute-done | bytes 262176 | tf_op jit(solution)/shard_map/ppermute | solution.py:197
  31.5 0.4 collective-permute-start.6
  31.9 0.7 fusion.10
  32.9 0.4 collective-permute-done.6.refs_7_
  33.3 9.1 %later_sweep.2 = (f32[32,8,128]{2,1,0:T(8,128)S(1)}, bf16[32,8,128]{2,1,0:T(8,128)(2,1)S(1)}) custom-call(s32[64]{0:T(128)S(1)} %get-tuple-element.12.refs_0_, s32[512]{0:T(512)S(1)} %reshape.21.refs_1_, bf16[128,8,128]{2,1,0:T(8,128)(2,1)S(1)} %constant_dynamic-update-slice_fusion.refs_2_, bf16[128,8,128]{2,1,0:T(8,128)(2,1)S(1)} %collective-permute-done.2.refs_3_, ...), custom_call_target="tpu_custom_call" | custom-call | tf_op jit(solution)/shard_map/later_sweep/pallas_call | solution.py:210
  42.4 4.3 %collective-permute-start.9 = (bf16[32,8,128]{2,1,0:T(8,128)(2,1)S(1)}, bf16[32,8,128]{2,1,0:T(8,128)(2,1)S(1)}, u32[]{:S(2)}, u32[]{:S(2)}) collective-permute-start(bf16[32,8,128]{2,1,0:T(8,128)(2,1)S(1)} %get-tuple-element.17), channel_id=1, source_target_pairs={{0,4},{1,5},{2,6},{3,7},{4,0},{5,1},{6,2},{7,3},{8,12},{9,13},{10,... | collective-permute-start | bytes 196616 | tf_op jit(solution)/shard_map/ppermute | solution.py:197
  46.6 3.8 %collective-permute-done.9 = bf16[32,8,128]{2,1,0:T(8,128)(2,1)S(1)} collective-permute-done((bf16[32,8,128]{2,1,0:T(8,128)(2,1)S(1)}, bf16[32,8,128]{2,1,0:T(8,128)(2,1)S(1)}, u32[]{:S(2)}, u32[]{:S(2)}) %collective-permute-start.9) | collective-permute-done | bytes 65568 | tf_op jit(solution)/shard_map/ppermute | solution.py:197
  50.4 0.7 collective-permute-start.10
  51.2 4.3 %collective-permute-done.10 = bf16[64,8,128]{2,1,0:T(8,128)(2,1)S(1)} collective-permute-done((bf16[64,8,128]{2,1,0:T(8,128)(2,1)S(1)}, bf16[64,8,128]{2,1,0:T(8,128)(2,1)S(1)}, u32[]{:S(2)}, u32[]{:S(2)}) %collective-permute-start.10) | collective-permute-done | bytes 131104 | tf_op jit(solution)/shard_map/ppermute | solution.py:197
  55.5 1.8 %collective-permute-start.13 = (bf16[128,8,128]{2,1,0:T(8,128)(2,1)S(1)}, bf16[128,8,128]{2,1,0:T(8,128)(2,1)S(1)}, u32[]{:S(2)}, u32[]{:S(2)}) collective-permute-start(bf16[128,8,128]{2,1,0:T(8,128)(2,1)S(1)} %constant_dynamic-update-slice_fusion.3.refs_2_), channel_id=1, source_target_pairs={{0,24},{8,16},{16,8},{24,0},{1,25},{9,17},{17,9},{25,1},{2,26},{10... | collective-permute-start | bytes 786440 | tf_op jit(solution)/shard_map/ppermute | solution.py:197
  57.3 1.2 %collective-permute-start.12 = (bf16[128,8,128]{2,1,0:T(8,128)(2,1)S(1)}, bf16[128,8,128]{2,1,0:T(8,128)(2,1)S(1)}, u32[]{:S(2)}, u32[]{:S(2)}) collective-permute-start(bf16[128,8,128]{2,1,0:T(8,128)(2,1)S(1)} %constant_dynamic-update-slice_fusion.3.refs_2_), channel_id=1, source_target_pairs={{0,16},{8,24},{16,0},{24,8},{1,17},{9,25},{17,1},{25,9},{2,18},{10... | collective-permute-start | bytes 786440 | tf_op jit(solution)/shard_map/ppermute | solution.py:197
  58.5 0.5 collective-permute-start.11
  59.1 6.3 %collective-permute-done.13.refs_5_ = bf16[128,8,128]{2,1,0:T(8,128)(2,1)S(1)} collective-permute-done((bf16[128,8,128]{2,1,0:T(8,128)(2,1)S(1)}, bf16[128,8,128]{2,1,0:T(8,128)(2,1)S(1)}, u32[]{:S(2)}, u32[]{:S(2)}) %collective-permute-start.13) | collective-permute-done | bytes 262176 | tf_op jit(solution)/shard_map/ppermute | solution.py:197
  65.3 2.7 %collective-permute-done.12.refs_4_ = bf16[128,8,128]{2,1,0:T(8,128)(2,1)S(1)} collective-permute-done((bf16[128,8,128]{2,1,0:T(8,128)(2,1)S(1)}, bf16[128,8,128]{2,1,0:T(8,128)(2,1)S(1)}, u32[]{:S(2)}, u32[]{:S(2)}) %collective-permute-start.12) | collective-permute-done | bytes 262176 | tf_op jit(solution)/shard_map/ppermute | solution.py:197
  68.2 0.4 collective-permute-start.15
  68.6 1.0 %collective-permute-done.16.refs_8_ = bf16[128,8,128]{2,1,0:T(8,128)(2,1)S(1)} collective-permute-done((bf16[128,8,128]{2,1,0:T(8,128)(2,1)S(1)}, bf16[128,8,128]{2,1,0:T(8,128)(2,1)S(1)}, u32[]{:S(2)}, u32[]{:S(2)}) %collective-permute-start.16) | collective-permute-done | bytes 262176 | tf_op jit(solution)/shard_map/ppermute | solution.py:197
  69.6 0.4 collective-permute-done.15.refs_7_
  70.0 9.1 %later_sweep.3 = f32[32,8,128]{2,1,0:T(8,128)S(1)} custom-call(s32[64]{0:T(128)S(1)} %get-tuple-element.12.refs_0_, s32[512]{0:T(512)S(1)} %reshape.21.refs_1_, bf16[128,8,128]{2,1,0:T(8,128)(2,1)S(1)} %constant_dynamic-update-slice_fusion.3.refs_2_, bf16[128,8,128]{2,1,0:T(8,128)(2,1)S(1)} %collective-permute-done.11.refs_3_, ...), custom_call_target="tpu_custom_call" | custom-call | tf_op jit(solution)/shard_map/later_sweep/pallas_call | solution.py:210
  79.0 14.8 %all_to_all.5 = f32[32,8,128]{2,1,0:T(8,128)S(1)} all-to-all(f32[32,8,128]{2,1,0:T(8,128)S(1)} %later_sweep.3), channel_id=1, replica_groups=mesh['grp'=4,'row'=8] {'grp','row'}, dimensions={0} | all-to-all | bytes 262144 | tf_op jit(solution)/shard_map/all_to_all | solution.py:237
  94.0 0.8 reshape.23
  (27 shorter events, 0.8 us)
Async XLA Ops:
  3.0 0.7 copy-start
  6.6 7.8 %collective-permute-start = (bf16[32,8,128]{2,1,0:T(8,128)(2,1)S(1)}, bf16[32,8,128]{2,1,0:T(8,128)(2,1)S(1)}, u32[]{:S(2)}, u32[]{:S(2)}) collective-permute-start(bf16[32,8,128]{2,1,0:T(8,128)(2,1)S(1)} %get-tuple-element.13), channel_id=1, source_target_pairs={{0,4},{1,5},{2,6},{3,7},{4,0},{5,1},{6,2},{7,3},{8,12},{9,13},{10,... | collective-permute-start | bytes 196616 | tf_op jit(solution)/shard_map/ppermute | solution.py:197
  14.3 5.0 %collective-permute-start.1 = (bf16[64,8,128]{2,1,0:T(8,128)(2,1)S(1)}, bf16[64,8,128]{2,1,0:T(8,128)(2,1)S(1)}, u32[]{:S(2)}, u32[]{:S(2)}) collective-permute-start(bf16[64,8,128]{2,1,0:T(8,128)(2,1)S(1)} %pad_maximum_fusion), channel_id=1, source_target_pairs={{0,2},{1,3},{2,0},{3,1},{4,6},{5,7},{6,4},{7,5},{8,10},{9,11},{10,... | collective-permute-start | bytes 393224 | tf_op jit(solution)/shard_map/ppermute | solution.py:197
  19.4 9.3 %collective-permute-start.4 = (bf16[128,8,128]{2,1,0:T(8,128)(2,1)S(1)}, bf16[128,8,128]{2,1,0:T(8,128)(2,1)S(1)}, u32[]{:S(2)}, u32[]{:S(2)}) collective-permute-start(bf16[128,8,128]{2,1,0:T(8,128)(2,1)S(1)} %constant_dynamic-update-slice_fusion.refs_2_), channel_id=1, source_target_pairs={{0,24},{8,16},{16,8},{24,0},{1,25},{9,17},{17,9},{25,1},{2,26},{10... | collective-permute-start | bytes 786440 | tf_op jit(solution)/shard_map/ppermute | solution.py:197
  22.1 9.3 %collective-permute-start.3 = (bf16[128,8,128]{2,1,0:T(8,128)(2,1)S(1)}, bf16[128,8,128]{2,1,0:T(8,128)(2,1)S(1)}, u32[]{:S(2)}, u32[]{:S(2)}) collective-permute-start(bf16[128,8,128]{2,1,0:T(8,128)(2,1)S(1)} %constant_dynamic-update-slice_fusion.refs_2_), channel_id=1, source_target_pairs={{0,16},{8,24},{16,0},{24,8},{1,17},{9,25},{17,1},{25,9},{2,18},{10... | collective-permute-start | bytes 786440 | tf_op jit(solution)/shard_map/ppermute | solution.py:197
  22.6 8.9 %collective-permute-start.2 = (bf16[128,8,128]{2,1,0:T(8,128)(2,1)S(1)}, bf16[128,8,128]{2,1,0:T(8,128)(2,1)S(1)}, u32[]{:S(2)}, u32[]{:S(2)}) collective-permute-start(bf16[128,8,128]{2,1,0:T(8,128)(2,1)S(1)} %constant_dynamic-update-slice_fusion.refs_2_), channel_id=1, source_target_pairs={{0,8},{8,0},{16,24},{24,16},{1,9},{9,1},{17,25},{25,17},{2,10},{10... | collective-permute-start | bytes 786440 | tf_op jit(solution)/shard_map/ppermute | solution.py:197
  22.9 9.9 %collective-permute-start.5 = (bf16[128,8,128]{2,1,0:T(8,128)(2,1)S(1)}, bf16[128,8,128]{2,1,0:T(8,128)(2,1)S(1)}, u32[]{:S(2)}, u32[]{:S(2)}) collective-permute-start(bf16[128,8,128]{2,1,0:T(8,128)(2,1)S(1)} %constant_dynamic-update-slice_fusion.refs_2_), channel_id=1, source_target_pairs={{0,1},{1,0},{2,3},{3,2},{4,5},{5,4},{6,7},{7,6},{8,9},{9,8},{10,11... | collective-permute-start | bytes 786440 | tf_op jit(solution)/shard_map/ppermute | solution.py:197
  28.7 4.2 %collective-permute-start.8 = (bf16[128,8,128]{2,1,0:T(8,128)(2,1)S(1)}, bf16[128,8,128]{2,1,0:T(8,128)(2,1)S(1)}, u32[]{:S(2)}, u32[]{:S(2)}) collective-permute-start(bf16[128,8,128]{2,1,0:T(8,128)(2,1)S(1)} %collective-permute-done.4.refs_5_), channel_id=1, source_target_pairs={{0,1},{1,0},{2,3},{3,2},{4,5},{5,4},{6,7},{7,6},{8,9},{9,8},{10,11... | collective-permute-start | bytes 786440 | tf_op jit(solution)/shard_map/ppermute | solution.py:197
  31.4 1.5 %collective-permute-start.7 = (bf16[128,8,128]{2,1,0:T(8,128)(2,1)S(1)}, bf16[128,8,128]{2,1,0:T(8,128)(2,1)S(1)}, u32[]{:S(2)}, u32[]{:S(2)}) collective-permute-start(bf16[128,8,128]{2,1,0:T(8,128)(2,1)S(1)} %collective-permute-done.3.refs_4_), channel_id=1, source_target_pairs={{0,1},{1,0},{2,3},{3,2},{4,5},{5,4},{6,7},{7,6},{8,9},{9,8},{10,11... | collective-permute-start | bytes 786440 | tf_op jit(solution)/shard_map/ppermute | solution.py:197
  31.5 1.8 %collective-permute-start.6 = (bf16[128,8,128]{2,1,0:T(8,128)(2,1)S(1)}, bf16[128,8,128]{2,1,0:T(8,128)(2,1)S(1)}, u32[]{:S(2)}, u32[]{:S(2)}) collective-permute-start(bf16[128,8,128]{2,1,0:T(8,128)(2,1)S(1)} %collective-permute-done.2.refs_3_), channel_id=1, source_target_pairs={{0,1},{1,0},{2,3},{3,2},{4,5},{5,4},{6,7},{7,6},{8,9},{9,8},{10,11... | collective-permute-start | bytes 786440 | tf_op jit(solution)/shard_map/ppermute | solution.py:197
  42.4 8.1 %collective-permute-start.9 = (bf16[32,8,128]{2,1,0:T(8,128)(2,1)S(1)}, bf16[32,8,128]{2,1,0:T(8,128)(2,1)S(1)}, u32[]{:S(2)}, u32[]{:S(2)}) collective-permute-start(bf16[32,8,128]{2,1,0:T(8,128)(2,1)S(1)} %get-tuple-element.17), channel_id=1, source_target_pairs={{0,4},{1,5},{2,6},{3,7},{4,0},{5,1},{6,2},{7,3},{8,12},{9,13},{10,... | collective-permute-start | bytes 196616 | tf_op jit(solution)/shard_map/ppermute | solution.py:197
  50.4 5.0 %collective-permute-start.10 = (bf16[64,8,128]{2,1,0:T(8,128)(2,1)S(1)}, bf16[64,8,128]{2,1,0:T(8,128)(2,1)S(1)}, u32[]{:S(2)}, u32[]{:S(2)}) collective-permute-start(bf16[64,8,128]{2,1,0:T(8,128)(2,1)S(1)} %pad_maximum_fusion.1), channel_id=1, source_target_pairs={{0,2},{1,3},{2,0},{3,1},{4,6},{5,7},{6,4},{7,5},{8,10},{9,11},{10,... | collective-permute-start | bytes 393224 | tf_op jit(solution)/shard_map/ppermute | solution.py:197
  55.5 9.8 %collective-permute-start.13 = (bf16[128,8,128]{2,1,0:T(8,128)(2,1)S(1)}, bf16[128,8,128]{2,1,0:T(8,128)(2,1)S(1)}, u32[]{:S(2)}, u32[]{:S(2)}) collective-permute-start(bf16[128,8,128]{2,1,0:T(8,128)(2,1)S(1)} %constant_dynamic-update-slice_fusion.3.refs_2_), channel_id=1, source_target_pairs={{0,24},{8,16},{16,8},{24,0},{1,25},{9,17},{17,9},{25,1},{2,26},{10... | collective-permute-start | bytes 786440 | tf_op jit(solution)/shard_map/ppermute | solution.py:197
  57.3 10.7 %collective-permute-start.12 = (bf16[128,8,128]{2,1,0:T(8,128)(2,1)S(1)}, bf16[128,8,128]{2,1,0:T(8,128)(2,1)S(1)}, u32[]{:S(2)}, u32[]{:S(2)}) collective-permute-start(bf16[128,8,128]{2,1,0:T(8,128)(2,1)S(1)} %constant_dynamic-update-slice_fusion.3.refs_2_), channel_id=1, source_target_pairs={{0,16},{8,24},{16,0},{24,8},{1,17},{9,25},{17,1},{25,9},{2,18},{10... | collective-permute-start | bytes 786440 | tf_op jit(solution)/shard_map/ppermute | solution.py:197
  58.5 9.6 %collective-permute-start.11 = (bf16[128,8,128]{2,1,0:T(8,128)(2,1)S(1)}, bf16[128,8,128]{2,1,0:T(8,128)(2,1)S(1)}, u32[]{:S(2)}, u32[]{:S(2)}) collective-permute-start(bf16[128,8,128]{2,1,0:T(8,128)(2,1)S(1)} %constant_dynamic-update-slice_fusion.3.refs_2_), channel_id=1, source_target_pairs={{0,8},{8,0},{16,24},{24,16},{1,9},{9,1},{17,25},{25,17},{2,10},{10... | collective-permute-start | bytes 786440 | tf_op jit(solution)/shard_map/ppermute | solution.py:197
  59.0 9.5 %collective-permute-start.14 = (bf16[128,8,128]{2,1,0:T(8,128)(2,1)S(1)}, bf16[128,8,128]{2,1,0:T(8,128)(2,1)S(1)}, u32[]{:S(2)}, u32[]{:S(2)}) collective-permute-start(bf16[128,8,128]{2,1,0:T(8,128)(2,1)S(1)} %constant_dynamic-update-slice_fusion.3.refs_2_), channel_id=1, source_target_pairs={{0,1},{1,0},{2,3},{3,2},{4,5},{5,4},{6,7},{7,6},{8,9},{9,8},{10,11... | collective-permute-start | bytes 786440 | tf_op jit(solution)/shard_map/ppermute | solution.py:197
  65.3 3.2 %collective-permute-start.17 = (bf16[128,8,128]{2,1,0:T(8,128)(2,1)S(1)}, bf16[128,8,128]{2,1,0:T(8,128)(2,1)S(1)}, u32[]{:S(2)}, u32[]{:S(2)}) collective-permute-start(bf16[128,8,128]{2,1,0:T(8,128)(2,1)S(1)} %collective-permute-done.13.refs_5_), channel_id=1, source_target_pairs={{0,1},{1,0},{2,3},{3,2},{4,5},{5,4},{6,7},{7,6},{8,9},{9,8},{10,11... | collective-permute-start | bytes 786440 | tf_op jit(solution)/shard_map/ppermute | solution.py:197
  68.1 1.5 %collective-permute-start.16 = (bf16[128,8,128]{2,1,0:T(8,128)(2,1)S(1)}, bf16[128,8,128]{2,1,0:T(8,128)(2,1)S(1)}, u32[]{:S(2)}, u32[]{:S(2)}) collective-permute-start(bf16[128,8,128]{2,1,0:T(8,128)(2,1)S(1)} %collective-permute-done.12.refs_4_), channel_id=1, source_target_pairs={{0,1},{1,0},{2,3},{3,2},{4,5},{5,4},{6,7},{7,6},{8,9},{9,8},{10,11... | collective-permute-start | bytes 786440 | tf_op jit(solution)/shard_map/ppermute | solution.py:197
  68.2 1.8 %collective-permute-start.15 = (bf16[128,8,128]{2,1,0:T(8,128)(2,1)S(1)}, bf16[128,8,128]{2,1,0:T(8,128)(2,1)S(1)}, u32[]{:S(2)}, u32[]{:S(2)}) collective-permute-start(bf16[128,8,128]{2,1,0:T(8,128)(2,1)S(1)} %collective-permute-done.11.refs_3_), channel_id=1, source_target_pairs={{0,1},{1,0},{2,3},{3,2},{4,5},{5,4},{6,7},{7,6},{8,9},{9,8},{10,11... | collective-permute-start | bytes 786440 | tf_op jit(solution)/shard_map/ppermute | solution.py:197

commit v2 on v1

--- a/solution.py
+++ b/solution.py
@@ -10,31 +10,54 @@
 NRHS = 8
 CAP = 2
 LANES = 128
-CHUNKS = 4
-VMEM_LIMIT = 48 * 1024 * 1024
+VMEM_LIMIT = 32 * 1024 * 1024
 
 TRANSPOSED = (((1,), (1,)), ((), ()))
-
-
-def first_sweep(full, dest_ref, smooth_ref, right_ref, perm_ref, starts_ref, x_ref, xb_ref, rp_ref, sbd_ref, count):
+PLAIN = (((1,), (0,)), ((), ()))
+SUB = 8
+
+
+def spread_rows(source_ref, spread_ref, copies):
+    rows, width = source_ref.shape
+    tiles = width // LANES
+    for top in range(rows // SUB):
+        values = source_ref[top * SUB : (top + 1) * SUB, :].astype(jnp.float32)
+        for place, (tile, turned) in enumerate(copies):
+            piece = values[:, tile * LANES : (tile + 1) * LANES]
+            if turned:
+                piece = pltpu.roll(piece, LANES // 2, 1)
+            spread_ref[pl.ds((top * len(copies) + place) * SUB, SUB), :] = piece
+
+
+def spread_row(spread_ref, row, tiles, first, count):
+    start = (row // SUB) * (tiles * SUB) + first * SUB + row % SUB
+    return spread_ref[pl.ds(start, count, stride=SUB), :]
+
+
+def smooth_copies(width):
+    return [(tile, False) for tile in range(width // LANES)]
+
+
+def right_copies(width):
+    plain = [(tile, False) for tile in range(width // LANES)]
+    turned = [(tile, True) for tile in range(width // LANES)]
+    return plain + turned + plain
+
+
+def sort_rows(full, dest_ref, perm_ref, starts_ref, count):
     rows = dest_ref.shape[0]
     owners = starts_ref.shape[0]
-    pairs = x_ref.shape[0]
-    block = smooth_ref.shape[1]
-
-    def clear(owner, carry):
-        count[owner] = 0
-        return carry
-
-    lax.fori_loop(0, owners, clear, 0)
     if full:
-
-        def start(owner, carry):
+        for owner in range(owners):
+            count[owner] = owner * CAP
             starts_ref[owner] = owner * CAP
+    else:
+
+        def clear(owner, carry):
+            count[owner] = 0
             return carry
 
-        lax.fori_loop(0, owners, start, 0)
-    else:
+        lax.fori_loop(0, owners, clear, 0)
 
         def tally(row, carry):
             count[dest_ref[row]] = count[dest_ref[row]] + 1
@@ -43,68 +66,148 @@
         lax.fori_loop(0, rows, tally, 0)
 
         def start(owner, total):
+            following = total + count[owner]
             starts_ref[owner] = total
-            following = total + count[owner]
-            count[owner] = 0
+            count[owner] = total
             return following
 
         lax.fori_loop(0, owners, start, jnp.int32(0))
-
-    def place(row, carry):
+    for row in range(rows):
         owner = dest_ref[row]
-        rank = count[owner]
-        count[owner] = rank + 1
-        perm_ref[starts_ref[owner] + rank] = row
-        return carry
-
-    lax.fori_loop(0, rows, place, 0)
-
-    zero = jnp.zeros((block, block), jnp.bfloat16)
+        position = count[owner]
+        count[owner] = position + 1
+        perm_ref[position] = row
+
+
+def first_sweep(
+    full, dest_hbm, smooth_hbm, right_hbm, perm_ref, starts_ref, xb_ref,
+    dest_ref, count, smooth_ref, right_ref, smooth_spread, right_spread, collected, sems,
+):
+    copies = [
+        pltpu.make_async_copy(dest_hbm, dest_ref, sems.at[0]),
+        pltpu.make_async_copy(right_hbm, right_ref, sems.at[1]),
+        pltpu.make_async_copy(smooth_hbm, smooth_ref, sems.at[2]),
+    ]
+    for copy in copies:
+        copy.start()
+    rows, smooth_width = smooth_ref.shape
+    block = LANES // 2
+    half = smooth_width // LANES
+    quad = LANES // half
+    lanes = lax.broadcasted_iota(jnp.int32, (2 * SUB, LANES), 1)
+    lower = lanes[:SUB] < block
+    width = quad * block
+    held = lax.broadcasted_iota(jnp.int32, (width, width), 0)
+    wanted = lax.broadcasted_iota(jnp.int32, (width, width), 1)
+    placed = ((held % LANES) // half) * block + 2 * (held % half) + held // LANES
+    order = jnp.where(placed == wanted, 1.0, 0.0).astype(jnp.bfloat16)
+
+    copies[0].wait()
+    sort_rows(full, dest_ref, perm_ref, starts_ref, count)
+    copies[1].wait()
+    copied = right_copies(right_ref.shape[1])
+    spread_rows(right_ref, right_spread, copied)
+    copies[2].wait()
+    spread_rows(smooth_ref, smooth_spread, smooth_copies(smooth_width))
+
+    for group in range(rows // quad):
+        weights, values = [], []
+        for member in range(quad):
+            row = perm_ref[quad * group + member]
+            weights.append(spread_row(smooth_spread, row, half, 0, half))
+            straight = spread_row(right_spread, row, len(copied), 0, SUB)
+            crossed = spread_row(right_spread, row, len(copied), SUB // 2, SUB)
+            values += [jnp.where(lower, straight, 0.0), jnp.where(lower, 0.0, crossed)]
+        products = lax.dot_general(
+            jnp.concatenate(values, axis=0).astype(jnp.bfloat16),
+            jnp.concatenate(weights, axis=0).astype(jnp.bfloat16),
+            TRANSPOSED,
+            preferred_element_type=jnp.float32,
+        )
+        own = products[: 2 * SUB]
+        for member in range(1, quad):
+            own = jnp.where(
+                lanes // half == member, products[2 * SUB * member : 2 * SUB * (member + 1)], own
+            )
+        collected[pl.ds(group * SUB, SUB), :LANES] = own[:SUB]
+        collected[pl.ds(group * SUB, SUB), LANES:] = own[SUB:]
+    ordered = lax.dot_general(
+        collected[...].astype(jnp.bfloat16), order, PLAIN, preferred_element_type=jnp.float32
+    ).astype(jnp.bfloat16)
+    for group in range(rows // quad):
+        for pair in range(quad // 2):
+            xb_ref[group * (quad // 2) + pair] = ordered[
+                group * SUB : (group + 1) * SUB, pair * LANES : (pair + 1) * LANES
+            ]
+
+
+def prepare(
+    perm_ref, smooth_hbm, right_hbm, blocks_hbm, x_ref, rp_ref, sbd_ref, blocks_ref,
+    smooth_ref, right_ref, smooth_spread, right_spread, widened, sems,
+):
+    copies = [
+        pltpu.make_async_copy(right_hbm, right_ref, sems.at[0]),
+        pltpu.make_async_copy(smooth_hbm, smooth_ref, sems.at[1]),
+        pltpu.make_async_copy(blocks_hbm, blocks_ref, sems.at[2]),
+    ]
+    for copy in copies:
+        copy.start()
+    rows, smooth_width = smooth_ref.shape
+    block = LANES // 2
+    half = smooth_width // LANES
+    pairs = rows // 2
+    lower = lax.broadcasted_iota(jnp.int32, (SUB, LANES), 1) < block
+    low_half = lax.broadcasted_iota(jnp.int32, (half, LANES), 1) < block
+    copies[0].wait()
+    copied = right_copies(right_ref.shape[1])
+    spread_rows(right_ref, right_spread, copied)
+    copies[1].wait()
+    spread_rows(smooth_ref, smooth_spread, smooth_copies(smooth_width))
     for pair in range(pairs):
         low, high = perm_ref[2 * pair], perm_ref[2 * pair + 1]
-        both = jnp.concatenate(
-            [
-                jnp.concatenate([smooth_ref[low], zero], axis=1),
-                jnp.concatenate([zero, smooth_ref[high]], axis=1),
-            ],
-            axis=0,
+        rp_ref[pair] = jnp.where(
+            lower,
+            spread_row(right_spread, low, len(copied), 0, SUB),
+            spread_row(right_spread, high, len(copied), SUB // 2, SUB),
+        ).astype(jnp.bfloat16)
+        base = pair * LANES
+        for number, row in enumerate((low, high)):
+            straight = spread_row(smooth_spread, row, half, 0, half)
+            turned = pltpu.roll(straight, block, 1)
+            first, second = (straight, turned) if number == 0 else (turned, straight)
+            keep = low_half if number == 0 else jnp.logical_not(low_half)
+            widened[pl.ds(base + number * block, half, stride=2), :] = jnp.where(keep, first, 0.0)
+            widened[pl.ds(base + number * block + 1, half, stride=2), :] = jnp.where(keep, second, 0.0)
+    for pair in range(pairs):
+        sbd_ref[pair] = widened[pl.ds(pair * LANES, LANES), :].astype(jnp.bfloat16)
+    for pair in range(pairs):
+        x_ref[pair] = lax.dot_general(
+            rp_ref[pair], sbd_ref[pair], TRANSPOSED, preferred_element_type=jnp.float32
         )
-        right = jnp.concatenate([right_ref[low], right_ref[high]], axis=1)
-        x = lax.dot_general(right, both, TRANSPOSED, preferred_element_type=jnp.float32)
-        sbd_ref[pair] = both
-        rp_ref[pair] = right
-        x_ref[pair] = x
-        xb_ref[pair] = x.astype(jnp.bfloat16)
+    copies[2].wait()
 
 
 def later_sweep(piece_count, with_rounded, *refs):
     perm_ref, index_ref = refs[:2]
     pieces = refs[2 : 2 + piece_count]
-    blocks_hbm, sbd_ref, rp_ref, x_ref = refs[2 + piece_count : 6 + piece_count]
+    blocks, sbd_ref, rp_ref, x_ref = refs[2 + piece_count : 6 + piece_count]
     refs = refs[6 + piece_count :]
     out_ref = refs[0]
     rounded_ref = refs[1] if with_rounded else None
-    tiles, blocks, tile_sem, block_sem = refs[2 if with_rounded else 1 :]
+    tiles, defects, tile_sem = refs[2 if with_rounded else 1 :]
     pairs = x_ref.shape[0]
-    rows, block, width = blocks.shape
+    _, block, width = blocks.shape
     bands = width // block
     piece_tiles = pieces[0].shape[0]
-    part = rows // CHUNKS
 
     tile_copies = [
         pltpu.make_async_copy(piece, tiles.at[pl.ds(number * piece_tiles, piece_tiles)], tile_sem.at[number])
         for number, piece in enumerate(pieces)
     ]
-    block_copies = [
-        pltpu.make_async_copy(
-            blocks_hbm.at[pl.ds(number * part, part)], blocks.at[pl.ds(number * part, part)], block_sem.at[number]
-        )
-        for number in range(CHUNKS)
-    ]
-    for copy in tile_copies + block_copies:
+    for copy in tile_copies:
         copy.start()
     tiles[piece_count * piece_tiles] = jnp.zeros((NRHS, LANES), jnp.bfloat16)
-    for copy in tile_copies + block_copies:
+    for copy in tile_copies:
         copy.wait()
 
     lower = lax.broadcasted_iota(jnp.int32, (NRHS, LANES), 1) < block
@@ -131,9 +234,11 @@
         weights = jnp.concatenate([blocks[low], blocks[high]], axis=0)
         applied = lax.dot_general(gathered, weights, TRANSPOSED, preferred_element_type=jnp.float32)
         image = jnp.where(lower, applied[:NRHS], applied[NRHS:])
-        defect = (rp_ref[pair].astype(jnp.float32) - image).astype(jnp.bfloat16)
+        defects[pair] = (rp_ref[pair].astype(jnp.float32) - image).astype(jnp.bfloat16)
+
+    for pair in range(pairs):
         x = x_ref[pair] + lax.dot_general(
-            defect, sbd_ref[pair], TRANSPOSED, preferred_element_type=jnp.float32
+            defects[pair], sbd_ref[pair], TRANSPOSED, preferred_element_type=jnp.float32
         )
         out_ref[pair] = x
         if with_rounded:
@@ -154,22 +259,52 @@
     tile_shape = (pairs, NRHS, LANES)
     params = pltpu.CompilerParams(vmem_limit_bytes=VMEM_LIMIT)
 
-    perm, starts, x, rounded, right, smooth = pl.pallas_call(
+    smooth_width, right_width = smoother.shape[1], residual.shape[1]
+    smooth_rows = rows * len(smooth_copies(smooth_width))
+    right_rows = rows * len(right_copies(right_width))
+    perm, starts, rounded = pl.pallas_call(
         functools.partial(first_sweep, full),
         out_shape=(
             jax.ShapeDtypeStruct((rows,), jnp.int32),
             jax.ShapeDtypeStruct((devices,), jnp.int32),
+            jax.ShapeDtypeStruct(tile_shape, jnp.bfloat16),
+        ),
+        in_specs=[anywhere] * 3,
+        out_specs=(smem, smem, vmem),
+        scratch_shapes=[
+            pltpu.SMEM((rows,), jnp.int32),
+            pltpu.SMEM((devices,), jnp.int32),
+            pltpu.VMEM(smoother.shape, jnp.bfloat16),
+            pltpu.VMEM(residual.shape, jnp.bfloat16),
+            pltpu.VMEM((smooth_rows, LANES), jnp.float32),
+            pltpu.VMEM((right_rows, LANES), jnp.float32),
+            pltpu.VMEM((pairs * SUB // 2, 2 * LANES), jnp.float32),
+            pltpu.SemaphoreType.DMA((3,)),
+        ],
+        compiler_params=params,
+        name="first_sweep",
+    )(dest.reshape(rows), smoother, residual)
+    x, right, smooth, blocks = pl.pallas_call(
+        prepare,
+        out_shape=(
             jax.ShapeDtypeStruct(tile_shape, jnp.float32),
             jax.ShapeDtypeStruct(tile_shape, jnp.bfloat16),
-            jax.ShapeDtypeStruct(tile_shape, jnp.bfloat16),
             jax.ShapeDtypeStruct((pairs, 2 * block, 2 * block), jnp.bfloat16),
+            jax.ShapeDtypeStruct(coarse_blocks.shape, jnp.bfloat16),
         ),
-        in_specs=[smem, vmem, vmem],
-        out_specs=(smem, smem, vmem, vmem, vmem, vmem),
-        scratch_shapes=[pltpu.SMEM((devices,), jnp.int32)],
+        in_specs=[smem] + [anywhere] * 3,
+        out_specs=(vmem,) * 4,
+        scratch_shapes=[
+            pltpu.VMEM(smoother.shape, jnp.bfloat16),
+            pltpu.VMEM(residual.shape, jnp.bfloat16),
+            pltpu.VMEM((smooth_rows, LANES), jnp.float32),
+            pltpu.VMEM((right_rows, LANES), jnp.float32),
+            pltpu.VMEM((pairs * LANES, LANES), jnp.float32),
+            pltpu.SemaphoreType.DMA((3,)),
+        ],
         compiler_params=params,
-        name="first_sweep",
-    )(dest.reshape(rows), smoother.reshape(rows, block, block), residual.reshape(rows, NRHS, block))
+        name="prepare",
+    )(perm, smoother, residual, coarse_blocks)
 
     row_bits = [1 << bit for bit in range(members.bit_length() - 2, 0, -1)]
     slots = devices * CAP
@@ -210,32 +345,32 @@
         return pl.pallas_call(
             functools.partial(later_sweep, len(pieces), not last),
             out_shape=tuple(outs),
-            in_specs=[smem, smem] + [anywhere] * (len(pieces) + 1) + [vmem] * 3,
+            in_specs=[smem, smem] + [anywhere] * len(pieces) + [vmem] * 4,
             out_specs=tuple([vmem] * len(outs)),
             scratch_shapes=[
                 pltpu.VMEM((devices * pairs + 1, NRHS, LANES), jnp.bfloat16),
-                pltpu.VMEM((rows, block, width), jnp.bfloat16),
+                pltpu.VMEM(tile_shape, jnp.bfloat16),
                 pltpu.SemaphoreType.DMA((len(pieces),)),
-                pltpu.SemaphoreType.DMA((CHUNKS,)),
             ],
             compiler_params=params,
             name="later_sweep",
-        )(perm, index, *pieces, coarse_blocks, smooth, right, x)
+        )(perm, index, *pieces, blocks, smooth, right, x)
 
     x, rounded = sweep(x, rounded, False)
     (x,) = sweep(x, rounded, True)
 
     if not full:
-        flat = x.reshape(pairs, NRHS, 2, block).transpose(0, 2, 1, 3).reshape(rows, NRHS * block)
+        flat = x.reshape(pairs, 2, NRHS // 2, 2, block).transpose(0, 3, 2, 1, 4).reshape(rows, NRHS * block)
         following = jnp.concatenate([starts[1:], jnp.full((1,), rows, jnp.int32)])
         wanted = starts[:, None] + jnp.arange(CAP, dtype=jnp.int32)[None, :]
         live = wanted < following[:, None]
         flat = jnp.where(
             live.reshape(slots, 1), jnp.take(flat, wanted.reshape(slots), axis=0, mode="clip"), 0.0
         )
-        x = flat.reshape(devices, CAP, NRHS, block).transpose(0, 2, 1, 3).reshape(devices, NRHS, CAP * block)
+        x = flat.reshape(devices, CAP, NRHS // 2, 2, block).transpose(0, 3, 2, 1, 4)
+        x = x.reshape(devices, NRHS, CAP * block)
     got = lax.all_to_all(x, ("grp", "row"), split_axis=0, concat_axis=0, tiled=True)
-    got = got.reshape(devices, NRHS, CAP, block).transpose(0, 2, 1, 3)
+    got = got.reshape(devices, 2, NRHS // 2, CAP, block).transpose(0, 3, 2, 1, 4)
     return got.reshape(slots, NRHS * block)
 
 

time: 95.1 us -> 86.3 us (0.907)
  Pallas kernels: 21 us -> 9.65 us
  local copies, waits for them, and re-layouts: 4.91 us -> 8.11 us
    pallas_call x2, Pallas kernels: 18.1 us -> 5.43 us  [sweep(): pl.pallas_call(functools.partial(later_sweep, len(pieces), not last), out...]
    unnamed x6 -> x16, local copies, waits for them, and re-layouts: 0.69 us -> 6.63 us
    reshape x3 -> x1, local copies, waits for them, and re-layouts: 3.22 us -> 0.19 us  [local(): got.reshape(devices, 2, NRHS // 2, CAP, block).transpose(0, 3, 2, 1, 4)]
    pallas_call x0 -> x1, Pallas kernels: none -> 2.11 us  [local(): pl.pallas_call(prepare, out_shape=(jax.ShapeDtypeStruct(tile_shape, jnp.f...]
  transfers between devices with their start and end apart: 18 -> 18, of which waited for: 14 -> 11; matrix products, arithmetic and copies ran while one was open for 1% -> 1% of each run, Pallas kernels for 0% -> 2%
where the time goes in v2:
time: 86.3 us; the launch traced here: 85.9 us
  waiting for transfers between devices  35 us (41%)
  starting transfers between devices  17.7 us (21%)
  blocking collectives  14.5 us (17%)
  Pallas kernels  9.65 us (11%)
  local copies, waits for them, and re-layouts  8.11 us (9%)
    ppermute x18, waiting for transfers between devices, exchange(): lax.ppermute(value, axis, [(place, place ^ distance) for place in range(s...  35 us
    ppermute x18, starting transfers between devices, exchange(): lax.ppermute(value, axis, [(place, place ^ distance) for place in range(s...  17.7 us
    all_to_all x1, blocking collectives, local(): lax.all_to_all(x, ('grp', 'row'), split_axis=0, concat_axis=0, tiled=True)  14.5 us
    unnamed x16, local copies, waits for them, and re-layouts  6.63 us
    pallas_call x2, Pallas kernels, sweep(): pl.pallas_call(functools.partial(later_sweep, len(pieces), not last), out...  5.43 us
    pallas_call x1, Pallas kernels, local(): pl.pallas_call(functools.partial(first_sweep, full), out_shape=(jax.Shape...  2.12 us
    pallas_call x1, Pallas kernels, local(): pl.pallas_call(prepare, out_shape=(jax.ShapeDtypeStruct(tile_shape, jnp.f...  2.11 us
  transfers between devices with their start and end apart: 18, of which 11 were waited for; matrix products, arithmetic and copies ran while one was open for 1% of the time, Pallas kernels for 2%

profile of v2, /device:TPU:0, one launch (start us, length us, event | category | flops | bytes accessed | tf_op | source)
XLA Modules:
  0.0 85.9 jit_solution(2731984844101101640)
XLA Ops:
  0.0 1.0 %copy-done.1 = bf16[64,4096]{1,0:T(8,128)(2,1)S(1)} copy-done((bf16[64,4096]{1,0:T(8,128)(2,1)S(1)}, bf16[64,4096]{1,0:T(8,128)(2,1)}, u32[]{:S(2)}) %copy-start.1) | copy-done | bytes 524312
  1.0 0.8 copy-done.3
  1.9 0.7 copy-done.5
  2.5 2.1 %first_sweep.1 = (s32[64]{0:T(128)S(1)}, s32[32]{0:T(128)}, bf16[32,8,128]{2,1,0:T(8,128)(2,1)S(1)}) custom-call(s32[64]{0:T(128)S(1)} %bitcast.4, bf16[64,4096]{1,0:T(8,128)(2,1)S(1)} %copy-done.1, bf16[64,512]{1,0:T(8,128)(2,1)S(1)} %copy-done.3), custom_call_target="tpu_custom_call" | custom-call | tf_op jit(solution)/shard_map/first_sweep/pallas_call | solution.py:265
  4.7 4.1 %collective-permute-start = (bf16[32,8,128]{2,1,0:T(8,128)(2,1)S(1)}, bf16[32,8,128]{2,1,0:T(8,128)(2,1)S(1)}, u32[]{:S(2)}, u32[]{:S(2)}) collective-permute-start(bf16[32,8,128]{2,1,0:T(8,128)(2,1)S(1)} %get-tuple-element.14), channel_id=1, source_target_pairs={{0,4},{1,5},{2,6},{3,7},{4,0},{5,1},{6,2},{7,3},{8,12},{9,13},{10,... | collective-permute-start | bytes 196616 | tf_op jit(solution)/shard_map/ppermute | solution.py:332
  8.8 3.6 %collective-permute-done = bf16[32,8,128]{2,1,0:T(8,128)(2,1)S(1)} collective-permute-done((bf16[32,8,128]{2,1,0:T(8,128)(2,1)S(1)}, bf16[32,8,128]{2,1,0:T(8,128)(2,1)S(1)}, u32[]{:S(2)}, u32[]{:S(2)}) %collective-permute-start) | collective-permute-done | bytes 65568 | tf_op jit(solution)/shard_map/ppermute | solution.py:332
  12.4 0.6 collective-permute-start.1
  13.1 4.4 %collective-permute-done.1 = bf16[64,8,128]{2,1,0:T(8,128)(2,1)S(1)} collective-permute-done((bf16[64,8,128]{2,1,0:T(8,128)(2,1)S(1)}, bf16[64,8,128]{2,1,0:T(8,128)(2,1)S(1)}, u32[]{:S(2)}, u32[]{:S(2)}) %collective-permute-start.1) | collective-permute-done | bytes 131104 | tf_op jit(solution)/shard_map/ppermute | solution.py:332
  17.5 2.7 %collective-permute-start.4 = (bf16[128,8,128]{2,1,0:T(8,128)(2,1)S(1)}, bf16[128,8,128]{2,1,0:T(8,128)(2,1)S(1)}, u32[]{:S(2)}, u32[]{:S(2)}) collective-permute-start(bf16[128,8,128]{2,1,0:T(8,128)(2,1)S(1)} %constant_dynamic-update-slice_fusion.refs_2_), channel_id=1, source_target_pairs={{0,24},{8,16},{16,8},{24,0},{1,25},{9,17},{17,9},{25,1},{2,26},{10... | collective-permute-start | bytes 786440 | tf_op jit(solution)/shard_map/ppermute | solution.py:332
  20.2 0.5 collective-permute-start.3
  21.0 5.7 %collective-permute-done.4.refs_5_ = bf16[128,8,128]{2,1,0:T(8,128)(2,1)S(1)} collective-permute-done((bf16[128,8,128]{2,1,0:T(8,128)(2,1)S(1)}, bf16[128,8,128]{2,1,0:T(8,128)(2,1)S(1)}, u32[]{:S(2)}, u32[]{:S(2)}) %collective-permute-start.4) | collective-permute-done | bytes 262176 | tf_op jit(solution)/shard_map/ppermute | solution.py:332
  26.8 2.7 %collective-permute-done.3.refs_4_ = bf16[128,8,128]{2,1,0:T(8,128)(2,1)S(1)} collective-permute-done((bf16[128,8,128]{2,1,0:T(8,128)(2,1)S(1)}, bf16[128,8,128]{2,1,0:T(8,128)(2,1)S(1)}, u32[]{:S(2)}, u32[]{:S(2)}) %collective-permute-start.3) | collective-permute-done | bytes 262176 | tf_op jit(solution)/shard_map/ppermute | solution.py:332
  30.0 0.7 fusion.10
  31.0 2.2 %copy-done = bf16[64,64,512]{2,1,0:T(8,128)(2,1)S(1)} copy-done((bf16[64,64,512]{2,1,0:T(8,128)(2,1)S(1)}, bf16[64,64,512]{2,1,0:T(8,128)(2,1)}, u32[]{:S(2)}) %copy-start) | copy-done | bytes 4194328
  33.1 1.0 %copy-done.2 = bf16[64,4096]{1,0:T(8,128)(2,1)S(1)} copy-done((bf16[64,4096]{1,0:T(8,128)(2,1)S(1)}, bf16[64,4096]{1,0:T(8,128)(2,1)}, u32[]{:S(2)}) %copy-start.2) | copy-done | bytes 524312
  34.2 0.8 copy-done.4
  35.0 2.1 %prepare.1 = (f32[32,8,128]{2,1,0:T(8,128)S(1)}, bf16[32,8,128]{2,1,0:T(8,128)(2,1)S(1)}, bf16[32,128,128]{2,1,0:T(8,128)(2,1)S(1)}, bf16[64,64,512]{2,1,0:T(8,128)(2,1)S(1)}) custom-call(s32[64]{0:T(128)S(1)} %get-tuple-element.13.perm_ref.refs_0_, bf16[64,4096]{1,0:T(8,128)(2,1)S(1)} %copy-done.2, bf16[64,512]{1,0:T(8,128)(2,1)S(1)} %copy-done.4, ...), custom_call_target="tpu_custom_call" | custom-call | tf_op jit(solution)/shard_map/prepare/pallas_call | solution.py:287
  37.2 2.7 %later_sweep.2 = (f32[32,8,128]{2,1,0:T(8,128)S(1)}, bf16[32,8,128]{2,1,0:T(8,128)(2,1)S(1)}) custom-call(s32[64]{0:T(128)S(1)} %get-tuple-element.13.perm_ref.refs_0_, s32[512]{0:T(512)S(1)} %reshape.13.refs_1_, bf16[128,8,128]{2,1,0:T(8,128)(2,1)S(1)} %constant_dynamic-update-slice_fusion.refs_2_, bf16[128,8,128]{2,1,0:T(8,128)(2,1)S(1)} %collective-permute-done.2.refs_3_, ...), custom_call_target="tpu_custom_call" | custom-call | tf_op jit(solution)/shard_map/later_sweep/pallas_call | solution.py:345
  39.9 4.3 %collective-permute-start.9 = (bf16[32,8,128]{2,1,0:T(8,128)(2,1)S(1)}, bf16[32,8,128]{2,1,0:T(8,128)(2,1)S(1)}, u32[]{:S(2)}, u32[]{:S(2)}) collective-permute-start(bf16[32,8,128]{2,1,0:T(8,128)(2,1)S(1)} %get-tuple-element.19), channel_id=1, source_target_pairs={{0,4},{1,5},{2,6},{3,7},{4,0},{5,1},{6,2},{7,3},{8,12},{9,13},{10,... | collective-permute-start | bytes 196616 | tf_op jit(solution)/shard_map/ppermute | solution.py:332
  44.2 3.8 %collective-permute-done.9 = bf16[32,8,128]{2,1,0:T(8,128)(2,1)S(1)} collective-permute-done((bf16[32,8,128]{2,1,0:T(8,128)(2,1)S(1)}, bf16[32,8,128]{2,1,0:T(8,128)(2,1)S(1)}, u32[]{:S(2)}, u32[]{:S(2)}) %collective-permute-start.9) | collective-permute-done | bytes 65568 | tf_op jit(solution)/shard_map/ppermute | solution.py:332
  47.9 0.7 collective-permute-start.10
  48.7 4.3 %collective-permute-done.10 = bf16[64,8,128]{2,1,0:T(8,128)(2,1)S(1)} collective-permute-done((bf16[64,8,128]{2,1,0:T(8,128)(2,1)S(1)}, bf16[64,8,128]{2,1,0:T(8,128)(2,1)S(1)}, u32[]{:S(2)}, u32[]{:S(2)}) %collective-permute-start.10) | collective-permute-done | bytes 131104 | tf_op jit(solution)/shard_map/ppermute | solution.py:332
  53.0 1.7 %collective-permute-start.13 = (bf16[128,8,128]{2,1,0:T(8,128)(2,1)S(1)}, bf16[128,8,128]{2,1,0:T(8,128)(2,1)S(1)}, u32[]{:S(2)}, u32[]{:S(2)}) collective-permute-start(bf16[128,8,128]{2,1,0:T(8,128)(2,1)S(1)} %constant_dynamic-update-slice_fusion.3.refs_2_), channel_id=1, source_target_pairs={{0,24},{8,16},{16,8},{24,0},{1,25},{9,17},{17,9},{25,1},{2,26},{10... | collective-permute-start | bytes 786440 | tf_op jit(solution)/shard_map/ppermute | solution.py:332
  54.7 1.3 %collective-permute-start.12 = (bf16[128,8,128]{2,1,0:T(8,128)(2,1)S(1)}, bf16[128,8,128]{2,1,0:T(8,128)(2,1)S(1)}, u32[]{:S(2)}, u32[]{:S(2)}) collective-permute-start(bf16[128,8,128]{2,1,0:T(8,128)(2,1)S(1)} %constant_dynamic-update-slice_fusion.3.refs_2_), channel_id=1, source_target_pairs={{0,16},{8,24},{16,0},{24,8},{1,17},{9,25},{17,1},{25,9},{2,18},{10... | collective-permute-start | bytes 786440 | tf_op jit(solution)/shard_map/ppermute | solution.py:332
  56.0 0.6 collective-permute-start.11
  56.6 6.2 %collective-permute-done.13.refs_5_ = bf16[128,8,128]{2,1,0:T(8,128)(2,1)S(1)} collective-permute-done((bf16[128,8,128]{2,1,0:T(8,128)(2,1)S(1)}, bf16[128,8,128]{2,1,0:T(8,128)(2,1)S(1)}, u32[]{:S(2)}, u32[]{:S(2)}) %collective-permute-start.13) | collective-permute-done | bytes 262176 | tf_op jit(solution)/shard_map/ppermute | solution.py:332
  62.8 2.7 %collective-permute-done.12.refs_4_ = bf16[128,8,128]{2,1,0:T(8,128)(2,1)S(1)} collective-permute-done((bf16[128,8,128]{2,1,0:T(8,128)(2,1)S(1)}, bf16[128,8,128]{2,1,0:T(8,128)(2,1)S(1)}, u32[]{:S(2)}, u32[]{:S(2)}) %collective-permute-start.12) | collective-permute-done | bytes 262176 | tf_op jit(solution)/shard_map/ppermute | solution.py:332
  65.5 0.5 collective-permute-start.15
  66.0 1.0 %collective-permute-done.16.refs_8_ = bf16[128,8,128]{2,1,0:T(8,128)(2,1)S(1)} collective-permute-done((bf16[128,8,128]{2,1,0:T(8,128)(2,1)S(1)}, bf16[128,8,128]{2,1,0:T(8,128)(2,1)S(1)}, u32[]{:S(2)}, u32[]{:S(2)}) %collective-permute-start.16) | collective-permute-done | bytes 262176 | tf_op jit(solution)/shard_map/ppermute | solution.py:332
  67.4 2.7 %later_sweep.3 = f32[32,8,128]{2,1,0:T(8,128)S(1)} custom-call(s32[64]{0:T(128)S(1)} %get-tuple-element.13.perm_ref.refs_0_, s32[512]{0:T(512)S(1)} %reshape.13.refs_1_, bf16[128,8,128]{2,1,0:T(8,128)(2,1)S(1)} %constant_dynamic-update-slice_fusion.3.refs_2_, bf16[128,8,128]{2,1,0:T(8,128)(2,1)S(1)} %collective-permute-done.11.refs_3_, ...), custom_call_target="tpu_custom_call" | custom-call | tf_op jit(solution)/shard_map/later_sweep/pallas_call | solution.py:345
  70.1 14.5 %all_to_all.5 = f32[32,8,128]{2,1,0:T(8,128)S(1)} all-to-all(f32[32,8,128]{2,1,0:T(8,128)S(1)} %later_sweep.3), channel_id=1, replica_groups=mesh['grp'=4,'row'=8] {'grp','row'}, dimensions={0} | all-to-all | bytes 262144 | tf_op jit(solution)/shard_map/all_to_all | solution.py:372
  85.0 0.9 %reshape.15 = f32[64,512]{1,0:T(8,128)} reshape(f32[32,2,4,2,64]{4,3,2,1,0:T(2,128)S(1)} %copy.9) | data formatting | bytes 262144 | tf_op jit(solution)/shard_map/reshape | solution.py:374
  (36 shorter events, 1.9 us)
Async XLA Ops:
  0.0 1.0 %copy-start.1 = (bf16[64,4096]{1,0:T(8,128)(2,1)S(1)}, bf16[64,4096]{1,0:T(8,128)(2,1)}, u32[]{:S(2)}) copy-start(bf16[64,4096]{1,0:T(8,128)(2,1)} %smooth_hbm.3) | copy-start | bytes 1572868
  1.0 0.8 copy-start.3
  1.9 0.7 copy-start.5
  4.7 7.8 %collective-permute-start = (bf16[32,8,128]{2,1,0:T(8,128)(2,1)S(1)}, bf16[32,8,128]{2,1,0:T(8,128)(2,1)S(1)}, u32[]{:S(2)}, u32[]{:S(2)}) collective-permute-start(bf16[32,8,128]{2,1,0:T(8,128)(2,1)S(1)} %get-tuple-element.14), channel_id=1, source_target_pairs={{0,4},{1,5},{2,6},{3,7},{4,0},{5,1},{6,2},{7,3},{8,12},{9,13},{10,... | collective-permute-start | bytes 196616 | tf_op jit(solution)/shard_map/ppermute | solution.py:332
  12.4 5.0 %collective-permute-start.1 = (bf16[64,8,128]{2,1,0:T(8,128)(2,1)S(1)}, bf16[64,8,128]{2,1,0:T(8,128)(2,1)S(1)}, u32[]{:S(2)}, u32[]{:S(2)}) collective-permute-start(bf16[64,8,128]{2,1,0:T(8,128)(2,1)S(1)} %pad_maximum_fusion), channel_id=1, source_target_pairs={{0,2},{1,3},{2,0},{3,1},{4,6},{5,7},{6,4},{7,5},{8,10},{9,11},{10,... | collective-permute-start | bytes 393224 | tf_op jit(solution)/shard_map/ppermute | solution.py:332
  17.5 9.3 %collective-permute-start.4 = (bf16[128,8,128]{2,1,0:T(8,128)(2,1)S(1)}, bf16[128,8,128]{2,1,0:T(8,128)(2,1)S(1)}, u32[]{:S(2)}, u32[]{:S(2)}) collective-permute-start(bf16[128,8,128]{2,1,0:T(8,128)(2,1)S(1)} %constant_dynamic-update-slice_fusion.refs_2_), channel_id=1, source_target_pairs={{0,24},{8,16},{16,8},{24,0},{1,25},{9,17},{17,9},{25,1},{2,26},{10... | collective-permute-start | bytes 786440 | tf_op jit(solution)/shard_map/ppermute | solution.py:332
  20.2 9.3 %collective-permute-start.3 = (bf16[128,8,128]{2,1,0:T(8,128)(2,1)S(1)}, bf16[128,8,128]{2,1,0:T(8,128)(2,1)S(1)}, u32[]{:S(2)}, u32[]{:S(2)}) collective-permute-start(bf16[128,8,128]{2,1,0:T(8,128)(2,1)S(1)} %constant_dynamic-update-slice_fusion.refs_2_), channel_id=1, source_target_pairs={{0,16},{8,24},{16,0},{24,8},{1,17},{9,25},{17,1},{25,9},{2,18},{10... | collective-permute-start | bytes 786440 | tf_op jit(solution)/shard_map/ppermute | solution.py:332
  20.7 8.9 %collective-permute-start.2 = (bf16[128,8,128]{2,1,0:T(8,128)(2,1)S(1)}, bf16[128,8,128]{2,1,0:T(8,128)(2,1)S(1)}, u32[]{:S(2)}, u32[]{:S(2)}) collective-permute-start(bf16[128,8,128]{2,1,0:T(8,128)(2,1)S(1)} %constant_dynamic-update-slice_fusion.refs_2_), channel_id=1, source_target_pairs={{0,8},{8,0},{16,24},{24,16},{1,9},{9,1},{17,25},{25,17},{2,10},{10... | collective-permute-start | bytes 786440 | tf_op jit(solution)/shard_map/ppermute | solution.py:332
  21.0 16.1 %collective-permute-start.5 = (bf16[128,8,128]{2,1,0:T(8,128)(2,1)S(1)}, bf16[128,8,128]{2,1,0:T(8,128)(2,1)S(1)}, u32[]{:S(2)}, u32[]{:S(2)}) collective-permute-start(bf16[128,8,128]{2,1,0:T(8,128)(2,1)S(1)} %constant_dynamic-update-slice_fusion.refs_2_), channel_id=1, source_target_pairs={{0,1},{1,0},{2,3},{3,2},{4,5},{5,4},{6,7},{7,6},{8,9},{9,8},{10,11... | collective-permute-start | bytes 786440 | tf_op jit(solution)/shard_map/ppermute | solution.py:332
  26.8 10.4 %collective-permute-start.8 = (bf16[128,8,128]{2,1,0:T(8,128)(2,1)S(1)}, bf16[128,8,128]{2,1,0:T(8,128)(2,1)S(1)}, u32[]{:S(2)}, u32[]{:S(2)}) collective-permute-start(bf16[128,8,128]{2,1,0:T(8,128)(2,1)S(1)} %collective-permute-done.4.refs_5_), channel_id=1, source_target_pairs={{0,1},{1,0},{2,3},{3,2},{4,5},{5,4},{6,7},{7,6},{8,9},{9,8},{10,11... | collective-permute-start | bytes 786440 | tf_op jit(solution)/shard_map/ppermute | solution.py:332
  29.5 7.7 %collective-permute-start.7 = (bf16[128,8,128]{2,1,0:T(8,128)(2,1)S(1)}, bf16[128,8,128]{2,1,0:T(8,128)(2,1)S(1)}, u32[]{:S(2)}, u32[]{:S(2)}) collective-permute-start(bf16[128,8,128]{2,1,0:T(8,128)(2,1)S(1)} %collective-permute-done.3.refs_4_), channel_id=1, source_target_pairs={{0,1},{1,0},{2,3},{3,2},{4,5},{5,4},{6,7},{7,6},{8,9},{9,8},{10,11... | collective-permute-start | bytes 786440 | tf_op jit(solution)/shard_map/ppermute | solution.py:332
  29.6 7.5 %collective-permute-start.6 = (bf16[128,8,128]{2,1,0:T(8,128)(2,1)S(1)}, bf16[128,8,128]{2,1,0:T(8,128)(2,1)S(1)}, u32[]{:S(2)}, u32[]{:S(2)}) collective-permute-start(bf16[128,8,128]{2,1,0:T(8,128)(2,1)S(1)} %collective-permute-done.2.refs_3_), channel_id=1, source_target_pairs={{0,1},{1,0},{2,3},{3,2},{4,5},{5,4},{6,7},{7,6},{8,9},{9,8},{10,11... | collective-permute-start | bytes 786440 | tf_op jit(solution)/shard_map/ppermute | solution.py:332
  30.9 2.2 %copy-start = (bf16[64,64,512]{2,1,0:T(8,128)(2,1)S(1)}, bf16[64,64,512]{2,1,0:T(8,128)(2,1)}, u32[]{:S(2)}) copy-start(bf16[64,64,512]{2,1,0:T(8,128)(2,1)} %blocks_hbm.1) | copy-start | bytes 12582916
  33.1 1.0 %copy-start.2 = (bf16[64,4096]{1,0:T(8,128)(2,1)S(1)}, bf16[64,4096]{1,0:T(8,128)(2,1)}, u32[]{:S(2)}) copy-start(bf16[64,4096]{1,0:T(8,128)(2,1)} %smooth_hbm.3) | copy-start | bytes 1572868
  34.2 0.8 copy-start.4
  39.9 8.0 %collective-permute-start.9 = (bf16[32,8,128]{2,1,0:T(8,128)(2,1)S(1)}, bf16[32,8,128]{2,1,0:T(8,128)(2,1)S(1)}, u32[]{:S(2)}, u32[]{:S(2)}) collective-permute-start(bf16[32,8,128]{2,1,0:T(8,128)(2,1)S(1)} %get-tuple-element.19), channel_id=1, source_target_pairs={{0,4},{1,5},{2,6},{3,7},{4,0},{5,1},{6,2},{7,3},{8,12},{9,13},{10,... | collective-permute-start | bytes 196616 | tf_op jit(solution)/shard_map/ppermute | solution.py:332
  47.9 5.0 %collective-permute-start.10 = (bf16[64,8,128]{2,1,0:T(8,128)(2,1)S(1)}, bf16[64,8,128]{2,1,0:T(8,128)(2,1)S(1)}, u32[]{:S(2)}, u32[]{:S(2)}) collective-permute-start(bf16[64,8,128]{2,1,0:T(8,128)(2,1)S(1)} %pad_maximum_fusion.1), channel_id=1, source_target_pairs={{0,2},{1,3},{2,0},{3,1},{4,6},{5,7},{6,4},{7,5},{8,10},{9,11},{10,... | collective-permute-start | bytes 393224 | tf_op jit(solution)/shard_map/ppermute | solution.py:332
  53.0 9.8 %collective-permute-start.13 = (bf16[128,8,128]{2,1,0:T(8,128)(2,1)S(1)}, bf16[128,8,128]{2,1,0:T(8,128)(2,1)S(1)}, u32[]{:S(2)}, u32[]{:S(2)}) collective-permute-start(bf16[128,8,128]{2,1,0:T(8,128)(2,1)S(1)} %constant_dynamic-update-slice_fusion.3.refs_2_), channel_id=1, source_target_pairs={{0,24},{8,16},{16,8},{24,0},{1,25},{9,17},{17,9},{25,1},{2,26},{10... | collective-permute-start | bytes 786440 | tf_op jit(solution)/shard_map/ppermute | solution.py:332
  54.7 10.8 %collective-permute-start.12 = (bf16[128,8,128]{2,1,0:T(8,128)(2,1)S(1)}, bf16[128,8,128]{2,1,0:T(8,128)(2,1)S(1)}, u32[]{:S(2)}, u32[]{:S(2)}) collective-permute-start(bf16[128,8,128]{2,1,0:T(8,128)(2,1)S(1)} %constant_dynamic-update-slice_fusion.3.refs_2_), channel_id=1, source_target_pairs={{0,16},{8,24},{16,0},{24,8},{1,17},{9,25},{17,1},{25,9},{2,18},{10... | collective-permute-start | bytes 786440 | tf_op jit(solution)/shard_map/ppermute | solution.py:332
  56.0 9.5 %collective-permute-start.11 = (bf16[128,8,128]{2,1,0:T(8,128)(2,1)S(1)}, bf16[128,8,128]{2,1,0:T(8,128)(2,1)S(1)}, u32[]{:S(2)}, u32[]{:S(2)}) collective-permute-start(bf16[128,8,128]{2,1,0:T(8,128)(2,1)S(1)} %constant_dynamic-update-slice_fusion.3.refs_2_), channel_id=1, source_target_pairs={{0,8},{8,0},{16,24},{24,16},{1,9},{9,1},{17,25},{25,17},{2,10},{10... | collective-permute-start | bytes 786440 | tf_op jit(solution)/shard_map/ppermute | solution.py:332
  56.5 9.5 %collective-permute-start.14 = (bf16[128,8,128]{2,1,0:T(8,128)(2,1)S(1)}, bf16[128,8,128]{2,1,0:T(8,128)(2,1)S(1)}, u32[]{:S(2)}, u32[]{:S(2)}) collective-permute-start(bf16[128,8,128]{2,1,0:T(8,128)(2,1)S(1)} %constant_dynamic-update-slice_fusion.3.refs_2_), channel_id=1, source_target_pairs={{0,1},{1,0},{2,3},{3,2},{4,5},{5,4},{6,7},{7,6},{8,9},{9,8},{10,11... | collective-permute-start | bytes 786440 | tf_op jit(solution)/shard_map/ppermute | solution.py:332
  62.8 3.2 %collective-permute-start.17 = (bf16[128,8,128]{2,1,0:T(8,128)(2,1)S(1)}, bf16[128,8,128]{2,1,0:T(8,128)(2,1)S(1)}, u32[]{:S(2)}, u32[]{:S(2)}) collective-permute-start(bf16[128,8,128]{2,1,0:T(8,128)(2,1)S(1)} %collective-permute-done.13.refs_5_), channel_id=1, source_target_pairs={{0,1},{1,0},{2,3},{3,2},{4,5},{5,4},{6,7},{7,6},{8,9},{9,8},{10,11... | collective-permute-start | bytes 786440 | tf_op jit(solution)/shard_map/ppermute | solution.py:332
  65.5 1.5 %collective-permute-start.16 = (bf16[128,8,128]{2,1,0:T(8,128)(2,1)S(1)}, bf16[128,8,128]{2,1,0:T(8,128)(2,1)S(1)}, u32[]{:S(2)}, u32[]{:S(2)}) collective-permute-start(bf16[128,8,128]{2,1,0:T(8,128)(2,1)S(1)} %collective-permute-done.12.refs_4_), channel_id=1, source_target_pairs={{0,1},{1,0},{2,3},{3,2},{4,5},{5,4},{6,7},{7,6},{8,9},{9,8},{10,11... | collective-permute-start | bytes 786440 | tf_op jit(solution)/shard_map/ppermute | solution.py:332
  65.5 1.9 %collective-permute-start.15 = (bf16[128,8,128]{2,1,0:T(8,128)(2,1)S(1)}, bf16[128,8,128]{2,1,0:T(8,128)(2,1)S(1)}, u32[]{:S(2)}, u32[]{:S(2)}) collective-permute-start(bf16[128,8,128]{2,1,0:T(8,128)(2,1)S(1)} %collective-permute-done.11.refs_3_), channel_id=1, source_target_pairs={{0,1},{1,0},{2,3},{3,2},{4,5},{5,4},{6,7},{7,6},{8,9},{9,8},{10,11... | collective-permute-start | bytes 786440 | tf_op jit(solution)/shard_map/ppermute | solution.py:332

commit v3 on v2

--- a/solution.py
+++ b/solution.py
@@ -141,15 +141,44 @@
             ]
 
 
+def find_tiles(groups, members, pairs, cols, mask, dest, own_row, own_group):
+    slots = groups * members * CAP
+    rank = cols % CAP
+    source = (cols % slots) // CAP
+    position = ((dest // members) * members + cols // slots) * CAP + rank
+    return place_tiles(groups, members, pairs, source, position, mask, own_row, own_group)
+
+
+def place_tiles(groups, members, pairs, source, position, mask, own_row, own_group):
+    relative_row = (source % members) ^ own_row
+    relative_group = (source // members) ^ own_group
+    piece = (relative_row % 2) * groups + relative_group
+    within = jnp.zeros_like(piece)
+    for order, bit in enumerate(row_bits(members)):
+        within = within + ((relative_row // bit) % 2) * (1 << order)
+    tile = (piece * (members // 2) + within) * pairs + position // 2
+    swap = (position + lax.broadcasted_iota(jnp.int32, position.shape, 0)) % 2
+    return jnp.where(mask != 0, tile * 2 + swap, 2 * groups * members * pairs)
+
+
+def in_hbm(value):
+    return pltpu.with_memory_space_constraint(value, pltpu.HBM)
+
+
+def row_bits(members):
+    return [1 << bit for bit in range(members.bit_length() - 2, 0, -1)]
+
+
 def prepare(
-    perm_ref, smooth_hbm, right_hbm, blocks_hbm, x_ref, rp_ref, sbd_ref, blocks_ref,
-    smooth_ref, right_ref, smooth_spread, right_spread, widened, sems,
+    full, groups, members, perm_ref, rounded_ref, cols_hbm, mask_hbm, dest_hbm, smooth_hbm, right_hbm, blocks_hbm,
+    own_ref, index_ref, x_ref, rp_ref, sbd_ref, blocks_ref,
+    cols_ref, mask_ref, dest_ref, smooth_ref, right_ref, smooth_spread, right_spread, widened, sems,
 ):
-    copies = [
-        pltpu.make_async_copy(right_hbm, right_ref, sems.at[0]),
-        pltpu.make_async_copy(smooth_hbm, smooth_ref, sems.at[1]),
-        pltpu.make_async_copy(blocks_hbm, blocks_ref, sems.at[2]),
+    moves = [
+        (cols_hbm, cols_ref), (mask_hbm, mask_ref), (dest_hbm, dest_ref),
+        (right_hbm, right_ref), (smooth_hbm, smooth_ref), (blocks_hbm, blocks_ref),
     ]
+    copies = [pltpu.make_async_copy(*move, sems.at[number]) for number, move in enumerate(moves)]
     for copy in copies:
         copy.start()
     rows, smooth_width = smooth_ref.shape
@@ -158,10 +187,20 @@
     pairs = rows // 2
     lower = lax.broadcasted_iota(jnp.int32, (SUB, LANES), 1) < block
     low_half = lax.broadcasted_iota(jnp.int32, (half, LANES), 1) < block
-    copies[0].wait()
+    own_ref[...] = rounded_ref[...]
+    for copy in copies[:3]:
+        copy.wait()
+    if full:
+        index_ref[...] = find_tiles(
+            groups, members, pairs, cols_ref[...], mask_ref[...], dest_ref[...],
+            lax.axis_index("row"), lax.axis_index("grp"),
+        )
+    else:
+        index_ref[...] = cols_ref[...]
+    copies[3].wait()
     copied = right_copies(right_ref.shape[1])
     spread_rows(right_ref, right_spread, copied)
-    copies[1].wait()
+    copies[4].wait()
     spread_rows(smooth_ref, smooth_spread, smooth_copies(smooth_width))
     for pair in range(pairs):
         low, high = perm_ref[2 * pair], perm_ref[2 * pair + 1]
@@ -184,7 +223,7 @@
         x_ref[pair] = lax.dot_general(
             rp_ref[pair], sbd_ref[pair], TRANSPOSED, preferred_element_type=jnp.float32
         )
-    copies[2].wait()
+    copies[5].wait()
 
 
 def later_sweep(piece_count, with_rounded, *refs):
@@ -213,7 +252,7 @@
     lower = lax.broadcasted_iota(jnp.int32, (NRHS, LANES), 1) < block
 
     def fetch(row, band):
-        entry = index_ref[row * bands + band]
+        entry = index_ref[band, row]
         tile = tiles[lax.shift_right_logical(entry, 1)].astype(jnp.float32)
         return pltpu.roll(tile, (entry & 1) * block, 1)
 
@@ -255,6 +294,7 @@
     full = rows == devices * CAP
     smem = pl.BlockSpec(memory_space=pltpu.SMEM)
     vmem = pl.BlockSpec(memory_space=pltpu.VMEM)
+    hbm = pl.BlockSpec(memory_space=pltpu.HBM)
     anywhere = pl.BlockSpec(memory_space=pl.ANY)
     tile_shape = (pairs, NRHS, LANES)
     params = pltpu.CompilerParams(vmem_limit_bytes=VMEM_LIMIT)
@@ -269,7 +309,7 @@
             jax.ShapeDtypeStruct((devices,), jnp.int32),
             jax.ShapeDtypeStruct(tile_shape, jnp.bfloat16),
         ),
-        in_specs=[anywhere] * 3,
+        in_specs=[hbm] * 3,
         out_specs=(smem, smem, vmem),
         scratch_shapes=[
             pltpu.SMEM((rows,), jnp.int32),
@@ -283,62 +323,59 @@
         ],
         compiler_params=params,
         name="first_sweep",
-    )(dest.reshape(rows), smoother, residual)
-    x, right, smooth, blocks = pl.pallas_call(
-        prepare,
+    )(in_hbm(dest.reshape(rows)), in_hbm(smoother), in_hbm(residual))
+    cols, mask = band_cols.T, band_mask.T
+    if not full:
+        slots = devices * CAP
+        table = lax.all_gather(starts, ("grp", "row"), axis=0, tiled=True)
+        source = (cols % slots) // CAP
+        owner = (dest.T // members) * members + cols // slots
+        position = jnp.take(table, source * devices + owner, mode="clip") + cols % CAP
+        cols = place_tiles(
+            groups, members, pairs, source, position, mask, lax.axis_index("row"), lax.axis_index("grp")
+        )
+    own, index, x, right, smooth, blocks = pl.pallas_call(
+        functools.partial(prepare, full, groups, members),
         out_shape=(
+            jax.ShapeDtypeStruct(tile_shape, jnp.bfloat16),
+            jax.ShapeDtypeStruct((bands, rows), jnp.int32),
             jax.ShapeDtypeStruct(tile_shape, jnp.float32),
             jax.ShapeDtypeStruct(tile_shape, jnp.bfloat16),
             jax.ShapeDtypeStruct((pairs, 2 * block, 2 * block), jnp.bfloat16),
             jax.ShapeDtypeStruct(coarse_blocks.shape, jnp.bfloat16),
         ),
-        in_specs=[smem] + [anywhere] * 3,
-        out_specs=(vmem,) * 4,
+        in_specs=[smem, vmem] + [hbm] * 6,
+        out_specs=(vmem,) * 6,
         scratch_shapes=[
+            pltpu.VMEM((bands, rows), jnp.int32),
+            pltpu.VMEM((bands, rows), jnp.int32),
+            pltpu.VMEM((1, rows), jnp.int32),
             pltpu.VMEM(smoother.shape, jnp.bfloat16),
             pltpu.VMEM(residual.shape, jnp.bfloat16),
             pltpu.VMEM((smooth_rows, LANES), jnp.float32),
             pltpu.VMEM((right_rows, LANES), jnp.float32),
             pltpu.VMEM((pairs * LANES, LANES), jnp.float32),
-            pltpu.SemaphoreType.DMA((3,)),
+            pltpu.SemaphoreType.DMA((6,)),
         ],
         compiler_params=params,
+        cost_estimate=pl.CostEstimate(flops=1 << 26, bytes_accessed=10 << 20, transcendentals=0),
         name="prepare",
-    )(perm, smoother, residual, coarse_blocks)
-
-    row_bits = [1 << bit for bit in range(members.bit_length() - 2, 0, -1)]
-    slots = devices * CAP
-    member = band_cols // slots
-    source = (band_cols % slots) // CAP
-    rank = band_cols % CAP
-    owner = (dest // members) * members + member
-    if full:
-        position = owner * CAP + rank
-    else:
-        table = lax.all_gather(starts, ("grp", "row"), axis=0, tiled=True)
-        position = jnp.take(table, source * devices + owner, mode="clip") + rank
-    relative_row = (source % members) ^ lax.axis_index("row")
-    relative_group = (source // members) ^ lax.axis_index("grp")
-    piece = (relative_row & 1) * groups + relative_group
-    within = jnp.zeros_like(piece)
-    for order, bit in enumerate(row_bits):
-        within = within + ((relative_row // bit) & 1) * (1 << order)
-    tile = (piece * (members // 2) + within) * pairs + position // 2
-    swap = (position ^ jnp.arange(bands, dtype=jnp.int32)[None, :]) & 1
-    dead = devices * pairs
-    index = jnp.where(band_mask != 0, tile * 2 + swap, dead * 2).reshape(rows * bands)
+    )(
+        perm, rounded, in_hbm(cols), in_hbm(mask), in_hbm(dest.T),
+        in_hbm(smoother), in_hbm(residual), in_hbm(coarse_blocks),
+    )
 
     def exchange(value, axis, size, distance):
         return lax.ppermute(value, axis, [(place, place ^ distance) for place in range(size)])
 
-    def everywhere(value):
-        for bit in row_bits:
-            value = jnp.concatenate([value, exchange(value, "row", members, bit)], axis=0)
+    def everywhere(value, own):
+        for bit in row_bits(members):
+            value = own = jnp.concatenate([own, exchange(value, "row", members, bit)], axis=0)
         near = [value] + [exchange(value, "grp", groups, distance) for distance in range(1, groups)]
         return near + [exchange(part, "row", members, 1) for part in near]
 
-    def sweep(x, rounded, last):
-        pieces = everywhere(rounded)
+    def sweep(x, rounded, own, last):
+        pieces = everywhere(rounded, own)
         outs = [jax.ShapeDtypeStruct(tile_shape, jnp.float32)]
         if not last:
             outs.append(jax.ShapeDtypeStruct(tile_shape, jnp.bfloat16))
@@ -356,12 +393,13 @@
             name="later_sweep",
         )(perm, index, *pieces, blocks, smooth, right, x)
 
-    x, rounded = sweep(x, rounded, False)
-    (x,) = sweep(x, rounded, True)
+    x, rounded = sweep(x, rounded, own, False)
+    (x,) = sweep(x, rounded, rounded, True)
 
     if not full:
         flat = x.reshape(pairs, 2, NRHS // 2, 2, block).transpose(0, 3, 2, 1, 4).reshape(rows, NRHS * block)
         following = jnp.concatenate([starts[1:], jnp.full((1,), rows, jnp.int32)])
+        slots = devices * CAP
         wanted = starts[:, None] + jnp.arange(CAP, dtype=jnp.int32)[None, :]
         live = wanted < following[:, None]
         flat = jnp.where(
@@ -371,7 +409,7 @@
         x = x.reshape(devices, NRHS, CAP * block)
     got = lax.all_to_all(x, ("grp", "row"), split_axis=0, concat_axis=0, tiled=True)
     got = got.reshape(devices, 2, NRHS // 2, CAP, block).transpose(0, 3, 2, 1, 4)
-    return got.reshape(slots, NRHS * block)
+    return got.reshape(devices * CAP, NRHS * block)
 
 
 def solution(mesh):

time: 86.3 us -> 78.7 us (0.912)
  local copies, waits for them, and re-layouts: 8.11 us -> 1.33 us
  Pallas kernels: 9.65 us -> 11.1 us
  waiting for transfers between devices: 35 us -> 33.7 us
    unnamed x16 -> x4, local copies, waits for them, and re-layouts: 6.63 us -> 0.04 us
    ppermute x18, waiting for transfers between devices: 35 us -> 33.7 us  [exchange(): lax.ppermute(value, axis, [(place, place ^ distance) for place in range(s...]
    pallas_call x1, Pallas kernels: 2.11 us -> 3.02 us  [local(): pl.pallas_call(functools.partial(prepare, full, groups, members), out_sha...]
  transfers between devices with their start and end apart: 18 -> 18, of which waited for: 11 -> 14; matrix products, arithmetic and copies ran while one was open for 1% -> 0% of each run, Pallas kernels for 2% -> 4%
where the time goes in v3:
time: 78.7 us; the launch traced here: 78.5 us
  waiting for transfers between devices  33.7 us (43%)
  starting transfers between devices  17.5 us (22%)
  blocking collectives  14.8 us (19%)
  Pallas kernels  11.1 us (14%)
  local copies, waits for them, and re-layouts  1.33 us (2%)
    ppermute x18, waiting for transfers between devices, exchange(): lax.ppermute(value, axis, [(place, place ^ distance) for place in range(s...  33.7 us
    ppermute x18, starting transfers between devices, exchange(): lax.ppermute(value, axis, [(place, place ^ distance) for place in range(s...  17.5 us
    all_to_all x1, blocking collectives, local(): lax.all_to_all(x, ('grp', 'row'), split_axis=0, concat_axis=0, tiled=True)  14.8 us
    pallas_call x2, Pallas kernels, sweep(): pl.pallas_call(functools.partial(later_sweep, len(pieces), not last), out...  5.88 us
    pallas_call x1, Pallas kernels, local(): pl.pallas_call(functools.partial(prepare, full, groups, members), out_sha...  3.02 us
    pallas_call x1, Pallas kernels, local(): pl.pallas_call(functools.partial(first_sweep, full), out_shape=(jax.Shape...  2.24 us
  transfers between devices with their start and end apart: 18, of which 14 were waited for; matrix products, arithmetic and copies ran while one was open for 0% of the time, Pallas kernels for 4%

profile of v3, /device:TPU:0, one launch (start us, length us, event | category | flops | bytes accessed | tf_op | source)
XLA Modules:
  0.0 78.5 jit_solution(10315596563348740033)
XLA Ops:
  0.0 2.2 %first_sweep.1 = (s32[64]{0:T(128)S(1)}, s32[32]{0:T(128)}, bf16[32,8,128]{2,1,0:T(8,128)(2,1)S(1)}) custom-call(s32[64]{0:T(128)} %bitcast.8, bf16[64,4096]{1,0:T(8,128)(2,1)} %smooth_hbm.3, bf16[64,512]{1,0:T(8,128)(2,1)} %right_hbm.3), custom_call_target="tpu_custom_call" | custom-call | tf_op jit(solution)/shard_map/first_sweep/pallas_call | solution.py:305
  2.2 4.1 %collective-permute-start = (bf16[32,8,128]{2,1,0:T(8,128)(2,1)S(1)}, bf16[32,8,128]{2,1,0:T(8,128)(2,1)S(1)}, u32[]{:S(2)}, u32[]{:S(2)}) collective-permute-start(bf16[32,8,128]{2,1,0:T(8,128)(2,1)S(1)} %get-tuple-element.16.rounded_ref), channel_id=1, source_target_pairs={{0,4},{1,5},{2,6},{3,7},{4,0},{5,1},{6,2},{7,3},{8,12},{9,13},{10,... | collective-permute-start | bytes 196616 | tf_op jit(solution)/shard_map/ppermute | solution.py:369
  6.3 3.0 %prepare.1 = (bf16[32,8,128]{2,1,0:T(8,128)(2,1)S(1)}, s32[8,64]{1,0:T(8,128)S(1)}, f32[32,8,128]{2,1,0:T(8,128)S(1)}, bf16[32,8,128]{2,1,0:T(8,128)(2,1)S(1)}, ...) custom-call(s32[64]{0:T(128)S(1)} %get-tuple-element.15.perm_ref.refs_0_, ...), custom_call_target="tpu_custom_call" | custom-call | flops 67108864 | bytes 10485760 | tf_op jit(solution)/shard_map/prepare/pallas_call | solution.py:337
  9.4 0.6 collective-permute-done
  10.0 1.0 %collective-permute-start.1 = (bf16[64,8,128]{2,1,0:T(8,128)(2,1)S(1)}, bf16[64,8,128]{2,1,0:T(8,128)(2,1)S(1)}, u32[]{:S(2)}, u32[]{:S(2)}) collective-permute-start(bf16[64,8,128]{2,1,0:T(8,128)(2,1)S(1)} %pad_maximum_fusion), channel_id=1, source_target_pairs={{0,2},{1,3},{2,0},{3,1},{4,6},{5,7},{6,4},{7,5},{8,10},{9,11},{10,... | collective-permute-start | bytes 393224 | tf_op jit(solution)/shard_map/ppermute | solution.py:369
  11.1 4.0 %collective-permute-done.1 = bf16[64,8,128]{2,1,0:T(8,128)(2,1)S(1)} collective-permute-done((bf16[64,8,128]{2,1,0:T(8,128)(2,1)S(1)}, bf16[64,8,128]{2,1,0:T(8,128)(2,1)S(1)}, u32[]{:S(2)}, u32[]{:S(2)}) %collective-permute-start.1) | collective-permute-done | bytes 131104 | tf_op jit(solution)/shard_map/ppermute | solution.py:369
  15.1 2.7 %collective-permute-start.4 = (bf16[128,8,128]{2,1,0:T(8,128)(2,1)S(1)}, bf16[128,8,128]{2,1,0:T(8,128)(2,1)S(1)}, u32[]{:S(2)}, u32[]{:S(2)}) collective-permute-start(bf16[128,8,128]{2,1,0:T(8,128)(2,1)S(1)} %constant_dynamic-update-slice_fusion.refs_2_), channel_id=1, source_target_pairs={{0,24},{8,16},{16,8},{24,0},{1,25},{9,17},{17,9},{25,1},{2,26},{10... | collective-permute-start | bytes 786440 | tf_op jit(solution)/shard_map/ppermute | solution.py:369
  17.8 0.5 collective-permute-start.3
  18.3 0.3 collective-permute-start.2
  18.6 6.3 %collective-permute-done.4.refs_5_ = bf16[128,8,128]{2,1,0:T(8,128)(2,1)S(1)} collective-permute-done((bf16[128,8,128]{2,1,0:T(8,128)(2,1)S(1)}, bf16[128,8,128]{2,1,0:T(8,128)(2,1)S(1)}, u32[]{:S(2)}, u32[]{:S(2)}) %collective-permute-start.4) | collective-permute-done | bytes 262176 | tf_op jit(solution)/shard_map/ppermute | solution.py:369
  24.9 2.8 %collective-permute-done.3.refs_4_ = bf16[128,8,128]{2,1,0:T(8,128)(2,1)S(1)} collective-permute-done((bf16[128,8,128]{2,1,0:T(8,128)(2,1)S(1)}, bf16[128,8,128]{2,1,0:T(8,128)(2,1)S(1)}, u32[]{:S(2)}, u32[]{:S(2)}) %collective-permute-start.3) | collective-permute-done | bytes 262176 | tf_op jit(solution)/shard_map/ppermute | solution.py:369
  27.8 0.4 collective-permute-start.6
  28.2 1.0 %collective-permute-done.7.refs_8_ = bf16[128,8,128]{2,1,0:T(8,128)(2,1)S(1)} collective-permute-done((bf16[128,8,128]{2,1,0:T(8,128)(2,1)S(1)}, bf16[128,8,128]{2,1,0:T(8,128)(2,1)S(1)}, u32[]{:S(2)}, u32[]{:S(2)}) %collective-permute-start.7) | collective-permute-done | bytes 262176 | tf_op jit(solution)/shard_map/ppermute | solution.py:369
  29.2 0.4 collective-permute-done.6.refs_7_
  29.6 2.9 %later_sweep.2 = (f32[32,8,128]{2,1,0:T(8,128)S(1)}, bf16[32,8,128]{2,1,0:T(8,128)(2,1)S(1)}) custom-call(s32[64]{0:T(128)S(1)} %get-tuple-element.15.perm_ref.refs_0_, s32[8,64]{1,0:T(8,128)S(1)} %get-tuple-element.17.refs_1_, bf16[128,8,128]{2,1,0:T(8,128)(2,1)S(1)} %constant_dynamic-update-slice_fusion.refs_2_, ...), custom_call_target="tpu_custom_call" | custom-call | tf_op jit(solution)/shard_map/later_sweep/pallas_call | solution.py:382
  32.5 3.7 %collective-permute-start.9 = (bf16[32,8,128]{2,1,0:T(8,128)(2,1)S(1)}, bf16[32,8,128]{2,1,0:T(8,128)(2,1)S(1)}, u32[]{:S(2)}, u32[]{:S(2)}) collective-permute-start(bf16[32,8,128]{2,1,0:T(8,128)(2,1)S(1)} %get-tuple-element.23), channel_id=1, source_target_pairs={{0,4},{1,5},{2,6},{3,7},{4,0},{5,1},{6,2},{7,3},{8,12},{9,13},{10,... | collective-permute-start | bytes 196616 | tf_op jit(solution)/shard_map/ppermute | solution.py:369
  36.2 3.8 %collective-permute-done.9 = bf16[32,8,128]{2,1,0:T(8,128)(2,1)S(1)} collective-permute-done((bf16[32,8,128]{2,1,0:T(8,128)(2,1)S(1)}, bf16[32,8,128]{2,1,0:T(8,128)(2,1)S(1)}, u32[]{:S(2)}, u32[]{:S(2)}) %collective-permute-start.9) | collective-permute-done | bytes 65568 | tf_op jit(solution)/shard_map/ppermute | solution.py:369
  40.0 0.7 collective-permute-start.10
  40.8 4.3 %collective-permute-done.10 = bf16[64,8,128]{2,1,0:T(8,128)(2,1)S(1)} collective-permute-done((bf16[64,8,128]{2,1,0:T(8,128)(2,1)S(1)}, bf16[64,8,128]{2,1,0:T(8,128)(2,1)S(1)}, u32[]{:S(2)}, u32[]{:S(2)}) %collective-permute-start.10) | collective-permute-done | bytes 131104 | tf_op jit(solution)/shard_map/ppermute | solution.py:369
  45.1 1.8 %collective-permute-start.13 = (bf16[128,8,128]{2,1,0:T(8,128)(2,1)S(1)}, bf16[128,8,128]{2,1,0:T(8,128)(2,1)S(1)}, u32[]{:S(2)}, u32[]{:S(2)}) collective-permute-start(bf16[128,8,128]{2,1,0:T(8,128)(2,1)S(1)} %constant_dynamic-update-slice_fusion.3.refs_2_), channel_id=1, source_target_pairs={{0,24},{8,16},{16,8},{24,0},{1,25},{9,17},{17,9},{25,1},{2,26},{10... | collective-permute-start | bytes 786440 | tf_op jit(solution)/shard_map/ppermute | solution.py:369
  46.9 1.2 %collective-permute-start.12 = (bf16[128,8,128]{2,1,0:T(8,128)(2,1)S(1)}, bf16[128,8,128]{2,1,0:T(8,128)(2,1)S(1)}, u32[]{:S(2)}, u32[]{:S(2)}) collective-permute-start(bf16[128,8,128]{2,1,0:T(8,128)(2,1)S(1)} %constant_dynamic-update-slice_fusion.3.refs_2_), channel_id=1, source_target_pairs={{0,16},{8,24},{16,0},{24,8},{1,17},{9,25},{17,1},{25,9},{2,18},{10... | collective-permute-start | bytes 786440 | tf_op jit(solution)/shard_map/ppermute | solution.py:369
  48.1 0.5 collective-permute-start.11
  48.6 6.3 %collective-permute-done.13.refs_5_ = bf16[128,8,128]{2,1,0:T(8,128)(2,1)S(1)} collective-permute-done((bf16[128,8,128]{2,1,0:T(8,128)(2,1)S(1)}, bf16[128,8,128]{2,1,0:T(8,128)(2,1)S(1)}, u32[]{:S(2)}, u32[]{:S(2)}) %collective-permute-start.13) | collective-permute-done | bytes 262176 | tf_op jit(solution)/shard_map/ppermute | solution.py:369
  54.9 2.7 %collective-permute-done.12.refs_4_ = bf16[128,8,128]{2,1,0:T(8,128)(2,1)S(1)} collective-permute-done((bf16[128,8,128]{2,1,0:T(8,128)(2,1)S(1)}, bf16[128,8,128]{2,1,0:T(8,128)(2,1)S(1)}, u32[]{:S(2)}, u32[]{:S(2)}) %collective-permute-start.12) | collective-permute-done | bytes 262176 | tf_op jit(solution)/shard_map/ppermute | solution.py:369
  57.7 0.4 collective-permute-start.15
  58.1 1.0 %collective-permute-done.16.refs_8_ = bf16[128,8,128]{2,1,0:T(8,128)(2,1)S(1)} collective-permute-done((bf16[128,8,128]{2,1,0:T(8,128)(2,1)S(1)}, bf16[128,8,128]{2,1,0:T(8,128)(2,1)S(1)}, u32[]{:S(2)}, u32[]{:S(2)}) %collective-permute-start.16) | collective-permute-done | bytes 262176 | tf_op jit(solution)/shard_map/ppermute | solution.py:369
  59.2 0.4 collective-permute-done.15.refs_7_
  59.5 2.9 %later_sweep.3 = f32[32,8,128]{2,1,0:T(8,128)S(1)} custom-call(s32[64]{0:T(128)S(1)} %get-tuple-element.15.perm_ref.refs_0_, s32[8,64]{1,0:T(8,128)S(1)} %get-tuple-element.17.refs_1_, bf16[128,8,128]{2,1,0:T(8,128)(2,1)S(1)} %constant_dynamic-update-slice_fusion.3.refs_2_, bf16[128,8,128]{2,1,0:T(8,128)(2,1)S(1)} %collective-permute-done.11.refs_3_, ...), custom_call_target="tpu_custom_call" | custom-call | tf_op jit(solution)/shard_map/later_sweep/pallas_call | solution.py:382
  62.5 14.8 %all_to_all.5 = f32[32,8,128]{2,1,0:T(8,128)S(1)} all-to-all(f32[32,8,128]{2,1,0:T(8,128)S(1)} %later_sweep.3), channel_id=1, replica_groups=mesh['grp'=4,'row'=8] {'grp','row'}, dimensions={0} | all-to-all | bytes 262144 | tf_op jit(solution)/shard_map/all_to_all | solution.py:410
  77.3 0.2 reshape.10
  77.5 0.1 copy.7
  77.6 0.9 %reshape.11 = f32[64,512]{1,0:T(8,128)} reshape(f32[32,2,4,2,64]{4,3,2,1,0:T(2,128)S(1)} %copy.7) | data formatting | bytes 262144 | tf_op jit(solution)/shard_map/reshape | solution.py:412
  (20 shorter events, 0.3 us)
Async XLA Ops:
  2.2 7.8 %collective-permute-start = (bf16[32,8,128]{2,1,0:T(8,128)(2,1)S(1)}, bf16[32,8,128]{2,1,0:T(8,128)(2,1)S(1)}, u32[]{:S(2)}, u32[]{:S(2)}) collective-permute-start(bf16[32,8,128]{2,1,0:T(8,128)(2,1)S(1)} %get-tuple-element.16.rounded_ref), channel_id=1, source_target_pairs={{0,4},{1,5},{2,6},{3,7},{4,0},{5,1},{6,2},{7,3},{8,12},{9,13},{10,... | collective-permute-start | bytes 196616 | tf_op jit(solution)/shard_map/ppermute | solution.py:369
  10.0 5.0 %collective-permute-start.1 = (bf16[64,8,128]{2,1,0:T(8,128)(2,1)S(1)}, bf16[64,8,128]{2,1,0:T(8,128)(2,1)S(1)}, u32[]{:S(2)}, u32[]{:S(2)}) collective-permute-start(bf16[64,8,128]{2,1,0:T(8,128)(2,1)S(1)} %pad_maximum_fusion), channel_id=1, source_target_pairs={{0,2},{1,3},{2,0},{3,1},{4,6},{5,7},{6,4},{7,5},{8,10},{9,11},{10,... | collective-permute-start | bytes 393224 | tf_op jit(solution)/shard_map/ppermute | solution.py:369
  15.1 9.8 %collective-permute-start.4 = (bf16[128,8,128]{2,1,0:T(8,128)(2,1)S(1)}, bf16[128,8,128]{2,1,0:T(8,128)(2,1)S(1)}, u32[]{:S(2)}, u32[]{:S(2)}) collective-permute-start(bf16[128,8,128]{2,1,0:T(8,128)(2,1)S(1)} %constant_dynamic-update-slice_fusion.refs_2_), channel_id=1, source_target_pairs={{0,24},{8,16},{16,8},{24,0},{1,25},{9,17},{17,9},{25,1},{2,26},{10... | collective-permute-start | bytes 786440 | tf_op jit(solution)/shard_map/ppermute | solution.py:369
  17.8 9.9 %collective-permute-start.3 = (bf16[128,8,128]{2,1,0:T(8,128)(2,1)S(1)}, bf16[128,8,128]{2,1,0:T(8,128)(2,1)S(1)}, u32[]{:S(2)}, u32[]{:S(2)}) collective-permute-start(bf16[128,8,128]{2,1,0:T(8,128)(2,1)S(1)} %constant_dynamic-update-slice_fusion.refs_2_), channel_id=1, source_target_pairs={{0,16},{8,24},{16,0},{24,8},{1,17},{9,25},{17,1},{25,9},{2,18},{10... | collective-permute-start | bytes 786440 | tf_op jit(solution)/shard_map/ppermute | solution.py:369
  18.3 9.5 %collective-permute-start.2 = (bf16[128,8,128]{2,1,0:T(8,128)(2,1)S(1)}, bf16[128,8,128]{2,1,0:T(8,128)(2,1)S(1)}, u32[]{:S(2)}, u32[]{:S(2)}) collective-permute-start(bf16[128,8,128]{2,1,0:T(8,128)(2,1)S(1)} %constant_dynamic-update-slice_fusion.refs_2_), channel_id=1, source_target_pairs={{0,8},{8,0},{16,24},{24,16},{1,9},{9,1},{17,25},{25,17},{2,10},{10... | collective-permute-start | bytes 786440 | tf_op jit(solution)/shard_map/ppermute | solution.py:369
  18.6 9.6 %collective-permute-start.5 = (bf16[128,8,128]{2,1,0:T(8,128)(2,1)S(1)}, bf16[128,8,128]{2,1,0:T(8,128)(2,1)S(1)}, u32[]{:S(2)}, u32[]{:S(2)}) collective-permute-start(bf16[128,8,128]{2,1,0:T(8,128)(2,1)S(1)} %constant_dynamic-update-slice_fusion.refs_2_), channel_id=1, source_target_pairs={{0,1},{1,0},{2,3},{3,2},{4,5},{5,4},{6,7},{7,6},{8,9},{9,8},{10,11... | collective-permute-start | bytes 786440 | tf_op jit(solution)/shard_map/ppermute | solution.py:369
  24.9 3.3 %collective-permute-start.8 = (bf16[128,8,128]{2,1,0:T(8,128)(2,1)S(1)}, bf16[128,8,128]{2,1,0:T(8,128)(2,1)S(1)}, u32[]{:S(2)}, u32[]{:S(2)}) collective-permute-start(bf16[128,8,128]{2,1,0:T(8,128)(2,1)S(1)} %collective-permute-done.4.refs_5_), channel_id=1, source_target_pairs={{0,1},{1,0},{2,3},{3,2},{4,5},{5,4},{6,7},{7,6},{8,9},{9,8},{10,11... | collective-permute-start | bytes 786440 | tf_op jit(solution)/shard_map/ppermute | solution.py:369
  27.7 1.5 %collective-permute-start.7 = (bf16[128,8,128]{2,1,0:T(8,128)(2,1)S(1)}, bf16[128,8,128]{2,1,0:T(8,128)(2,1)S(1)}, u32[]{:S(2)}, u32[]{:S(2)}) collective-permute-start(bf16[128,8,128]{2,1,0:T(8,128)(2,1)S(1)} %collective-permute-done.3.refs_4_), channel_id=1, source_target_pairs={{0,1},{1,0},{2,3},{3,2},{4,5},{5,4},{6,7},{7,6},{8,9},{9,8},{10,11... | collective-permute-start | bytes 786440 | tf_op jit(solution)/shard_map/ppermute | solution.py:369
  27.8 1.8 %collective-permute-start.6 = (bf16[128,8,128]{2,1,0:T(8,128)(2,1)S(1)}, bf16[128,8,128]{2,1,0:T(8,128)(2,1)S(1)}, u32[]{:S(2)}, u32[]{:S(2)}) collective-permute-start(bf16[128,8,128]{2,1,0:T(8,128)(2,1)S(1)} %collective-permute-done.2.refs_3_), channel_id=1, source_target_pairs={{0,1},{1,0},{2,3},{3,2},{4,5},{5,4},{6,7},{7,6},{8,9},{9,8},{10,11... | collective-permute-start | bytes 786440 | tf_op jit(solution)/shard_map/ppermute | solution.py:369
  32.5 7.5 %collective-permute-start.9 = (bf16[32,8,128]{2,1,0:T(8,128)(2,1)S(1)}, bf16[32,8,128]{2,1,0:T(8,128)(2,1)S(1)}, u32[]{:S(2)}, u32[]{:S(2)}) collective-permute-start(bf16[32,8,128]{2,1,0:T(8,128)(2,1)S(1)} %get-tuple-element.23), channel_id=1, source_target_pairs={{0,4},{1,5},{2,6},{3,7},{4,0},{5,1},{6,2},{7,3},{8,12},{9,13},{10,... | collective-permute-start | bytes 196616 | tf_op jit(solution)/shard_map/ppermute | solution.py:369
  40.0 5.0 %collective-permute-start.10 = (bf16[64,8,128]{2,1,0:T(8,128)(2,1)S(1)}, bf16[64,8,128]{2,1,0:T(8,128)(2,1)S(1)}, u32[]{:S(2)}, u32[]{:S(2)}) collective-permute-start(bf16[64,8,128]{2,1,0:T(8,128)(2,1)S(1)} %pad_maximum_fusion.1), channel_id=1, source_target_pairs={{0,2},{1,3},{2,0},{3,1},{4,6},{5,7},{6,4},{7,5},{8,10},{9,11},{10,... | collective-permute-start | bytes 393224 | tf_op jit(solution)/shard_map/ppermute | solution.py:369
  45.1 9.8 %collective-permute-start.13 = (bf16[128,8,128]{2,1,0:T(8,128)(2,1)S(1)}, bf16[128,8,128]{2,1,0:T(8,128)(2,1)S(1)}, u32[]{:S(2)}, u32[]{:S(2)}) collective-permute-start(bf16[128,8,128]{2,1,0:T(8,128)(2,1)S(1)} %constant_dynamic-update-slice_fusion.3.refs_2_), channel_id=1, source_target_pairs={{0,24},{8,16},{16,8},{24,0},{1,25},{9,17},{17,9},{25,1},{2,26},{10... | collective-permute-start | bytes 786440 | tf_op jit(solution)/shard_map/ppermute | solution.py:369
  46.9 10.7 %collective-permute-start.12 = (bf16[128,8,128]{2,1,0:T(8,128)(2,1)S(1)}, bf16[128,8,128]{2,1,0:T(8,128)(2,1)S(1)}, u32[]{:S(2)}, u32[]{:S(2)}) collective-permute-start(bf16[128,8,128]{2,1,0:T(8,128)(2,1)S(1)} %constant_dynamic-update-slice_fusion.3.refs_2_), channel_id=1, source_target_pairs={{0,16},{8,24},{16,0},{24,8},{1,17},{9,25},{17,1},{25,9},{2,18},{10... | collective-permute-start | bytes 786440 | tf_op jit(solution)/shard_map/ppermute | solution.py:369
  48.1 9.7 %collective-permute-start.11 = (bf16[128,8,128]{2,1,0:T(8,128)(2,1)S(1)}, bf16[128,8,128]{2,1,0:T(8,128)(2,1)S(1)}, u32[]{:S(2)}, u32[]{:S(2)}) collective-permute-start(bf16[128,8,128]{2,1,0:T(8,128)(2,1)S(1)} %constant_dynamic-update-slice_fusion.3.refs_2_), channel_id=1, source_target_pairs={{0,8},{8,0},{16,24},{24,16},{1,9},{9,1},{17,25},{25,17},{2,10},{10... | collective-permute-start | bytes 786440 | tf_op jit(solution)/shard_map/ppermute | solution.py:369
  48.6 9.5 %collective-permute-start.14 = (bf16[128,8,128]{2,1,0:T(8,128)(2,1)S(1)}, bf16[128,8,128]{2,1,0:T(8,128)(2,1)S(1)}, u32[]{:S(2)}, u32[]{:S(2)}) collective-permute-start(bf16[128,8,128]{2,1,0:T(8,128)(2,1)S(1)} %constant_dynamic-update-slice_fusion.3.refs_2_), channel_id=1, source_target_pairs={{0,1},{1,0},{2,3},{3,2},{4,5},{5,4},{6,7},{7,6},{8,9},{9,8},{10,11... | collective-permute-start | bytes 786440 | tf_op jit(solution)/shard_map/ppermute | solution.py:369
  54.9 3.2 %collective-permute-start.17 = (bf16[128,8,128]{2,1,0:T(8,128)(2,1)S(1)}, bf16[128,8,128]{2,1,0:T(8,128)(2,1)S(1)}, u32[]{:S(2)}, u32[]{:S(2)}) collective-permute-start(bf16[128,8,128]{2,1,0:T(8,128)(2,1)S(1)} %collective-permute-done.13.refs_5_), channel_id=1, source_target_pairs={{0,1},{1,0},{2,3},{3,2},{4,5},{5,4},{6,7},{7,6},{8,9},{9,8},{10,11... | collective-permute-start | bytes 786440 | tf_op jit(solution)/shard_map/ppermute | solution.py:369
  57.6 1.5 %collective-permute-start.16 = (bf16[128,8,128]{2,1,0:T(8,128)(2,1)S(1)}, bf16[128,8,128]{2,1,0:T(8,128)(2,1)S(1)}, u32[]{:S(2)}, u32[]{:S(2)}) collective-permute-start(bf16[128,8,128]{2,1,0:T(8,128)(2,1)S(1)} %collective-permute-done.12.refs_4_), channel_id=1, source_target_pairs={{0,1},{1,0},{2,3},{3,2},{4,5},{5,4},{6,7},{7,6},{8,9},{9,8},{10,11... | collective-permute-start | bytes 786440 | tf_op jit(solution)/shard_map/ppermute | solution.py:369
  57.7 1.8 %collective-permute-start.15 = (bf16[128,8,128]{2,1,0:T(8,128)(2,1)S(1)}, bf16[128,8,128]{2,1,0:T(8,128)(2,1)S(1)}, u32[]{:S(2)}, u32[]{:S(2)}) collective-permute-start(bf16[128,8,128]{2,1,0:T(8,128)(2,1)S(1)} %collective-permute-done.11.refs_3_), channel_id=1, source_target_pairs={{0,1},{1,0},{2,3},{3,2},{4,5},{5,4},{6,7},{7,6},{8,9},{9,8},{10,11... | collective-permute-start | bytes 786440 | tf_op jit(solution)/shard_map/ppermute | solution.py:369

commit v4 on v3

--- a/solution.py
+++ b/solution.py
@@ -154,19 +154,21 @@
     relative_group = (source // members) ^ own_group
     piece = (relative_row % 2) * groups + relative_group
     within = jnp.zeros_like(piece)
-    for order, bit in enumerate(row_bits(members)):
-        within = within + ((relative_row // bit) % 2) * (1 << order)
+    for parity in range(2):
+        for order, bit in enumerate(row_bits(members, parity)):
+            within = within + jnp.where(source % 2 == parity, ((relative_row // bit) % 2) * (1 << order), 0)
     tile = (piece * (members // 2) + within) * pairs + position // 2
     swap = (position + lax.broadcasted_iota(jnp.int32, position.shape, 0)) % 2
     return jnp.where(mask != 0, tile * 2 + swap, 2 * groups * members * pairs)
 
 
+def row_bits(members, parity):
+    bits = [1 << bit for bit in range(members.bit_length() - 2, 0, -1)]
+    return bits[::-1] if parity else bits
+
+
 def in_hbm(value):
     return pltpu.with_memory_space_constraint(value, pltpu.HBM)
-
-
-def row_bits(members):
-    return [1 << bit for bit in range(members.bit_length() - 2, 0, -1)]
 
 
 def prepare(
@@ -233,23 +235,21 @@
     refs = refs[6 + piece_count :]
     out_ref = refs[0]
     rounded_ref = refs[1] if with_rounded else None
-    tiles, defects, tile_sem = refs[2 if with_rounded else 1 :]
+    tiles, defects = refs[2 if with_rounded else 1 :]
     pairs = x_ref.shape[0]
     _, block, width = blocks.shape
     bands = width // block
-    piece_tiles = pieces[0].shape[0]
-
-    tile_copies = [
-        pltpu.make_async_copy(piece, tiles.at[pl.ds(number * piece_tiles, piece_tiles)], tile_sem.at[number])
-        for number, piece in enumerate(pieces)
-    ]
-    for copy in tile_copies:
-        copy.start()
-    tiles[piece_count * piece_tiles] = jnp.zeros((NRHS, LANES), jnp.bfloat16)
-    for copy in tile_copies:
-        copy.wait()
+
+    start = 0
+    for piece in pieces:
+        size = piece.shape[0]
+        tiles[pl.ds(start, size)] = piece[...]
+        start += size
+    tiles[start] = jnp.zeros((NRHS, LANES), jnp.bfloat16)
 
     lower = lax.broadcasted_iota(jnp.int32, (NRHS, LANES), 1) < block
+
+    first_half = lax.broadcasted_iota(jnp.int32, (NRHS, LANES), 0) < NRHS // 2
 
     def fetch(row, band):
         entry = index_ref[band, row]
@@ -279,9 +279,19 @@
         x = x_ref[pair] + lax.dot_general(
             defects[pair], sbd_ref[pair], TRANSPOSED, preferred_element_type=jnp.float32
         )
-        out_ref[pair] = x
         if with_rounded:
+            out_ref[pair] = x
             rounded_ref[pair] = x.astype(jnp.bfloat16)
+        else:
+            crossed = pltpu.roll(pltpu.roll(x, block, 1), NRHS // 2, 0)
+            out_ref[pair] = jnp.where(lower == first_half, x, crossed)
+
+
+def lay_out(got_ref, out_ref):
+    rows, width = out_ref.shape
+    tiles = width // LANES
+    for tile in range(tiles):
+        out_ref[:, tile * LANES : (tile + 1) * LANES] = got_ref[pl.ds(tile, rows, stride=tiles), :]
 
 
 def local(coarse_blocks, smoother, residual, dest, band_cols, band_mask):
@@ -295,7 +305,6 @@
     smem = pl.BlockSpec(memory_space=pltpu.SMEM)
     vmem = pl.BlockSpec(memory_space=pltpu.VMEM)
     hbm = pl.BlockSpec(memory_space=pltpu.HBM)
-    anywhere = pl.BlockSpec(memory_space=pl.ANY)
     tile_shape = (pairs, NRHS, LANES)
     params = pltpu.CompilerParams(vmem_limit_bytes=VMEM_LIMIT)
 
@@ -365,14 +374,17 @@
         in_hbm(smoother), in_hbm(residual), in_hbm(coarse_blocks),
     )
 
-    def exchange(value, axis, size, distance):
-        return lax.ppermute(value, axis, [(place, place ^ distance) for place in range(size)])
+    def exchange_row(value, distances):
+        return lax.ppermute(value, "row", [(place, place ^ distances[place % 2]) for place in range(members)])
 
     def everywhere(value, own):
-        for bit in row_bits(members):
-            value = own = jnp.concatenate([own, exchange(value, "row", members, bit)], axis=0)
-        near = [value] + [exchange(value, "grp", groups, distance) for distance in range(1, groups)]
-        return near + [exchange(part, "row", members, 1) for part in near]
+        for distances in zip(row_bits(members, 0), row_bits(members, 1)):
+            value = own = jnp.concatenate([own, exchange_row(value, distances)], axis=0)
+        near = [own] + [
+            lax.ppermute(own, "grp", [(place, place ^ distance) for place in range(groups)])
+            for distance in range(1, groups)
+        ]
+        return near + [exchange_row(part, (1, 1)) for part in near]
 
     def sweep(x, rounded, own, last):
         pieces = everywhere(rounded, own)
@@ -382,12 +394,11 @@
         return pl.pallas_call(
             functools.partial(later_sweep, len(pieces), not last),
             out_shape=tuple(outs),
-            in_specs=[smem, smem] + [anywhere] * len(pieces) + [vmem] * 4,
+            in_specs=[smem, smem] + [vmem] * (len(pieces) + 4),
             out_specs=tuple([vmem] * len(outs)),
             scratch_shapes=[
                 pltpu.VMEM((devices * pairs + 1, NRHS, LANES), jnp.bfloat16),
                 pltpu.VMEM(tile_shape, jnp.bfloat16),
-                pltpu.SemaphoreType.DMA((len(pieces),)),
             ],
             compiler_params=params,
             name="later_sweep",
@@ -397,7 +408,7 @@
     (x,) = sweep(x, rounded, rounded, True)
 
     if not full:
-        flat = x.reshape(pairs, 2, NRHS // 2, 2, block).transpose(0, 3, 2, 1, 4).reshape(rows, NRHS * block)
+        flat = x.reshape(rows, NRHS * block)
         following = jnp.concatenate([starts[1:], jnp.full((1,), rows, jnp.int32)])
         slots = devices * CAP
         wanted = starts[:, None] + jnp.arange(CAP, dtype=jnp.int32)[None, :]
@@ -405,11 +416,16 @@
         flat = jnp.where(
             live.reshape(slots, 1), jnp.take(flat, wanted.reshape(slots), axis=0, mode="clip"), 0.0
         )
-        x = flat.reshape(devices, CAP, NRHS // 2, 2, block).transpose(0, 3, 2, 1, 4)
-        x = x.reshape(devices, NRHS, CAP * block)
+        x = flat.reshape(devices, NRHS, LANES)
     got = lax.all_to_all(x, ("grp", "row"), split_axis=0, concat_axis=0, tiled=True)
-    got = got.reshape(devices, 2, NRHS // 2, CAP, block).transpose(0, 3, 2, 1, 4)
-    return got.reshape(devices * CAP, NRHS * block)
+    return pl.pallas_call(
+        lay_out,
+        out_shape=jax.ShapeDtypeStruct((devices * CAP, NRHS * block), jnp.float32),
+        in_specs=[vmem],
+        out_specs=vmem,
+        compiler_params=params,
+        name="lay_out",
+    )(got.reshape(devices * NRHS, LANES))
 
 
 def solution(mesh):

time: 78.7 us -> 75.5 us (0.959)
  blocking collectives: 14.8 us -> 12.1 us
  waiting for transfers between devices: 33.7 us -> 36.4 us
  starting transfers between devices: 17.5 us -> 15.1 us
  local copies, waits for them, and re-layouts: 1.33 us -> 0.07 us
    ppermute x18, waiting for transfers between devices: 33.7 us -> 36.4 us  [the longest x6 19.7 us: everywhere(): lax.ppermute(own, 'grp', [(place, place ^ distance) for place in range(gr...]
    all_to_all x1, blocking collectives: 14.8 us -> 12.1 us  [local(): lax.all_to_all(x, ('grp', 'row'), split_axis=0, concat_axis=0, tiled=True)]
    ppermute x18, starting transfers between devices: 17.5 us -> 15.1 us  [the longest x12 8.01 us: exchange_row(): lax.ppermute(value, 'row', [(place, place ^ distances[place % 2]) for pla...]
    reshape x2 -> x0, local copies, waits for them, and re-layouts: 1.12 us -> none  [the longest x1 0.94 us: local(): return got.reshape(devices * CAP, NRHS * block)]
  transfers between devices with their start and end apart: 18 -> 18, of which waited for: 14 -> 13; matrix products, arithmetic and copies ran while one was open for 0% -> 0% of each run, Pallas kernels for 4% -> 4%
where the time goes in v4:
time: 75.5 us; the launch traced here: 75.3 us
  waiting for transfers between devices  36.4 us (48%)
  starting transfers between devices  15.1 us (20%)
  blocking collectives  12.1 us (16%)
  Pallas kernels  11.5 us (15%)
    ppermute x6, waiting for transfers between devices, everywhere(): lax.ppermute(own, 'grp', [(place, place ^ distance) for place in range(gr...  19.7 us
    ppermute x12, waiting for transfers between devices, exchange_row(): lax.ppermute(value, 'row', [(place, place ^ distances[place % 2]) for pla...  16.7 us
    all_to_all x1, blocking collectives, local(): lax.all_to_all(x, ('grp', 'row'), split_axis=0, concat_axis=0, tiled=True)  12.1 us
    ppermute x12, starting transfers between devices, exchange_row(): lax.ppermute(value, 'row', [(place, place ^ distances[place % 2]) for pla...  8.01 us
    ppermute x6, starting transfers between devices, everywhere(): lax.ppermute(own, 'grp', [(place, place ^ distance) for place in range(gr...  7.11 us
    pallas_call x2, Pallas kernels, sweep(): pl.pallas_call(functools.partial(later_sweep, len(pieces), not last), out...  5.55 us
    pallas_call x1, Pallas kernels, local(): pl.pallas_call(functools.partial(prepare, full, groups, members), out_sha...  3.02 us
    pallas_call x1, Pallas kernels, local(): pl.pallas_call(functools.partial(first_sweep, full), out_shape=(jax.Shape...  2.24 us
  transfers between devices with their start and end apart: 18, of which 13 were waited for; matrix products, arithmetic and copies ran while one was open for 0% of the time, Pallas kernels for 4%

profile of v4, /device:TPU:0, one launch (start us, length us, event | category | flops | bytes accessed | tf_op | source)
XLA Modules:
  0.0 75.3 jit_solution(3186180228363753064)
XLA Ops:
  0.0 2.2 %first_sweep.1 = (s32[64]{0:T(128)S(1)}, s32[32]{0:T(128)}, bf16[32,8,128]{2,1,0:T(8,128)(2,1)S(1)}) custom-call(s32[64]{0:T(128)} %bitcast.8, bf16[64,4096]{1,0:T(8,128)(2,1)} %smooth_hbm.3, bf16[64,512]{1,0:T(8,128)(2,1)} %right_hbm.3), custom_call_target="tpu_custom_call" | custom-call | tf_op jit(solution)/shard_map/first_sweep/pallas_call | solution.py:314
  2.2 4.1 %collective-permute-start = (bf16[32,8,128]{2,1,0:T(8,128)(2,1)S(1)}, bf16[32,8,128]{2,1,0:T(8,128)(2,1)S(1)}, u32[]{:S(2)}, u32[]{:S(2)}) collective-permute-start(bf16[32,8,128]{2,1,0:T(8,128)(2,1)S(1)} %get-tuple-element.16.rounded_ref), channel_id=1, source_target_pairs={{0,4},{1,3},{2,6},{3,1},{4,0},{5,7},{6,2},{7,5},{8,12},{9,11},{10,... | collective-permute-start | bytes 196616 | tf_op jit(solution)/shard_map/ppermute | solution.py:378
  6.3 3.0 %prepare.1 = (bf16[32,8,128]{2,1,0:T(8,128)(2,1)S(1)}, s32[8,64]{1,0:T(8,128)S(1)}, f32[32,8,128]{2,1,0:T(8,128)S(1)}, bf16[32,8,128]{2,1,0:T(8,128)(2,1)S(1)}, ...) custom-call(s32[64]{0:T(128)S(1)} %get-tuple-element.15.perm_ref.refs_0_, ...), custom_call_target="tpu_custom_call" | custom-call | flops 67108864 | bytes 10485760 | tf_op jit(solution)/shard_map/prepare/pallas_call | solution.py:346
  9.4 1.6 %collective-permute-start.1 = (bf16[64,8,128]{2,1,0:T(8,128)(2,1)S(1)}, bf16[64,8,128]{2,1,0:T(8,128)(2,1)S(1)}, u32[]{:S(2)}, u32[]{:S(2)}) collective-permute-start(bf16[64,8,128]{2,1,0:T(8,128)(2,1)S(1)} %pad_maximum_fusion), channel_id=1, source_target_pairs={{0,2},{1,5},{2,0},{3,7},{4,6},{5,1},{6,4},{7,3},{8,10},{9,13},{10,... | collective-permute-start | bytes 393224 | tf_op jit(solution)/shard_map/ppermute | solution.py:378
  11.1 4.5 %collective-permute-done.1 = bf16[64,8,128]{2,1,0:T(8,128)(2,1)S(1)} collective-permute-done((bf16[64,8,128]{2,1,0:T(8,128)(2,1)S(1)}, bf16[64,8,128]{2,1,0:T(8,128)(2,1)S(1)}, u32[]{:S(2)}, u32[]{:S(2)}) %collective-permute-start.1) | collective-permute-done | bytes 131104 | tf_op jit(solution)/shard_map/ppermute | solution.py:378
  15.6 2.6 %collective-permute-start.4 = (bf16[128,8,128]{2,1,0:T(8,128)(2,1)S(1)}, bf16[128,8,128]{2,1,0:T(8,128)(2,1)S(1)}, u32[]{:S(2)}, u32[]{:S(2)}) collective-permute-start(bf16[128,8,128]{2,1,0:T(8,128)(2,1)S(1)} %constant_dynamic-update-slice_fusion.refs_2_), channel_id=1, source_target_pairs={{0,24},{8,16},{16,8},{24,0},{1,25},{9,17},{17,9},{25,1},{2,26},{10... | collective-permute-start | bytes 786440 | tf_op jit(solution)/shard_map/ppermute | solution.py:384
  18.1 0.5 collective-permute-start.3
  18.7 0.5 collective-permute-start.2
  19.1 6.7 %collective-permute-done.4.refs_5_ = bf16[128,8,128]{2,1,0:T(8,128)(2,1)S(1)} collective-permute-done((bf16[128,8,128]{2,1,0:T(8,128)(2,1)S(1)}, bf16[128,8,128]{2,1,0:T(8,128)(2,1)S(1)}, u32[]{:S(2)}, u32[]{:S(2)}) %collective-permute-start.4) | collective-permute-done | bytes 262176 | tf_op jit(solution)/shard_map/ppermute | solution.py:384
  25.8 3.1 %collective-permute-done.3.refs_4_ = bf16[128,8,128]{2,1,0:T(8,128)(2,1)S(1)} collective-permute-done((bf16[128,8,128]{2,1,0:T(8,128)(2,1)S(1)}, bf16[128,8,128]{2,1,0:T(8,128)(2,1)S(1)}, u32[]{:S(2)}, u32[]{:S(2)}) %collective-permute-start.3) | collective-permute-done | bytes 262176 | tf_op jit(solution)/shard_map/ppermute | solution.py:384
  28.9 0.1 collective-permute-done.2.refs_3_
  29.1 0.4 collective-permute-start.6
  29.4 1.0 %collective-permute-done.7.refs_8_ = bf16[128,8,128]{2,1,0:T(8,128)(2,1)S(1)} collective-permute-done((bf16[128,8,128]{2,1,0:T(8,128)(2,1)S(1)}, bf16[128,8,128]{2,1,0:T(8,128)(2,1)S(1)}, u32[]{:S(2)}, u32[]{:S(2)}) %collective-permute-start.7) | collective-permute-done | bytes 262176 | tf_op jit(solution)/shard_map/ppermute | solution.py:378
  30.4 0.4 collective-permute-done.6.refs_7_
  30.8 2.7 %later_sweep.2 = (f32[32,8,128]{2,1,0:T(8,128)S(1)}, bf16[32,8,128]{2,1,0:T(8,128)(2,1)S(1)}) custom-call(s32[64]{0:T(128)S(1)} %get-tuple-element.15.perm_ref.refs_0_, s32[8,64]{1,0:T(8,128)S(1)} %get-tuple-element.17.refs_1_, bf16[128,8,128]{2,1,0:T(8,128)(2,1)S(1)} %constant_dynamic-update-slice_fusion.refs_2_, ...), custom_call_target="tpu_custom_call" | custom-call | tf_op jit(solution)/shard_map/later_sweep/pallas_call | solution.py:394
  33.6 1.4 %collective-permute-start.9 = (bf16[32,8,128]{2,1,0:T(8,128)(2,1)S(1)}, bf16[32,8,128]{2,1,0:T(8,128)(2,1)S(1)}, u32[]{:S(2)}, u32[]{:S(2)}) collective-permute-start(bf16[32,8,128]{2,1,0:T(8,128)(2,1)S(1)} %get-tuple-element.23), channel_id=1, source_target_pairs={{0,4},{1,3},{2,6},{3,1},{4,0},{5,7},{6,2},{7,5},{8,12},{9,11},{10,... | collective-permute-start | bytes 196616 | tf_op jit(solution)/shard_map/ppermute | solution.py:378
  35.0 4.3 %collective-permute-done.9 = bf16[32,8,128]{2,1,0:T(8,128)(2,1)S(1)} collective-permute-done((bf16[32,8,128]{2,1,0:T(8,128)(2,1)S(1)}, bf16[32,8,128]{2,1,0:T(8,128)(2,1)S(1)}, u32[]{:S(2)}, u32[]{:S(2)}) %collective-permute-start.9) | collective-permute-done | bytes 65568 | tf_op jit(solution)/shard_map/ppermute | solution.py:378
  39.3 0.1 collective-permute-start.10
  39.4 5.2 %collective-permute-done.10 = bf16[64,8,128]{2,1,0:T(8,128)(2,1)S(1)} collective-permute-done((bf16[64,8,128]{2,1,0:T(8,128)(2,1)S(1)}, bf16[64,8,128]{2,1,0:T(8,128)(2,1)S(1)}, u32[]{:S(2)}, u32[]{:S(2)}) %collective-permute-start.10) | collective-permute-done | bytes 131104 | tf_op jit(solution)/shard_map/ppermute | solution.py:378
  44.6 1.8 %collective-permute-start.13 = (bf16[128,8,128]{2,1,0:T(8,128)(2,1)S(1)}, bf16[128,8,128]{2,1,0:T(8,128)(2,1)S(1)}, u32[]{:S(2)}, u32[]{:S(2)}) collective-permute-start(bf16[128,8,128]{2,1,0:T(8,128)(2,1)S(1)} %constant_dynamic-update-slice_fusion.3.refs_2_), channel_id=1, source_target_pairs={{0,24},{8,16},{16,8},{24,0},{1,25},{9,17},{17,9},{25,1},{2,26},{10... | collective-permute-start | bytes 786440 | tf_op jit(solution)/shard_map/ppermute | solution.py:384
  46.4 1.2 %collective-permute-start.12 = (bf16[128,8,128]{2,1,0:T(8,128)(2,1)S(1)}, bf16[128,8,128]{2,1,0:T(8,128)(2,1)S(1)}, u32[]{:S(2)}, u32[]{:S(2)}) collective-permute-start(bf16[128,8,128]{2,1,0:T(8,128)(2,1)S(1)} %constant_dynamic-update-slice_fusion.3.refs_2_), channel_id=1, source_target_pairs={{0,16},{8,24},{16,0},{24,8},{1,17},{9,25},{17,1},{25,9},{2,18},{10... | collective-permute-start | bytes 786440 | tf_op jit(solution)/shard_map/ppermute | solution.py:384
  47.6 0.5 collective-permute-start.11
  48.1 0.0 collective-permute-start.14
  48.1 6.6 %collective-permute-done.13.refs_5_ = bf16[128,8,128]{2,1,0:T(8,128)(2,1)S(1)} collective-permute-done((bf16[128,8,128]{2,1,0:T(8,128)(2,1)S(1)}, bf16[128,8,128]{2,1,0:T(8,128)(2,1)S(1)}, u32[]{:S(2)}, u32[]{:S(2)}) %collective-permute-start.13) | collective-permute-done | bytes 262176 | tf_op jit(solution)/shard_map/ppermute | solution.py:384
  54.8 3.0 %collective-permute-done.12.refs_4_ = bf16[128,8,128]{2,1,0:T(8,128)(2,1)S(1)} collective-permute-done((bf16[128,8,128]{2,1,0:T(8,128)(2,1)S(1)}, bf16[128,8,128]{2,1,0:T(8,128)(2,1)S(1)}, u32[]{:S(2)}, u32[]{:S(2)}) %collective-permute-start.12) | collective-permute-done | bytes 262176 | tf_op jit(solution)/shard_map/ppermute | solution.py:384
  57.8 0.1 collective-permute-done.11.refs_3_
  57.9 0.4 collective-permute-start.15
  58.3 1.0 %collective-permute-done.16.refs_8_ = bf16[128,8,128]{2,1,0:T(8,128)(2,1)S(1)} collective-permute-done((bf16[128,8,128]{2,1,0:T(8,128)(2,1)S(1)}, bf16[128,8,128]{2,1,0:T(8,128)(2,1)S(1)}, u32[]{:S(2)}, u32[]{:S(2)}) %collective-permute-start.16) | collective-permute-done | bytes 262176 | tf_op jit(solution)/shard_map/ppermute | solution.py:378
  59.3 0.4 collective-permute-done.15.refs_7_
  59.7 2.8 %later_sweep.3 = f32[32,8,128]{2,1,0:T(8,128)S(1)} custom-call(s32[64]{0:T(128)S(1)} %get-tuple-element.15.perm_ref.refs_0_, s32[8,64]{1,0:T(8,128)S(1)} %get-tuple-element.17.refs_1_, bf16[128,8,128]{2,1,0:T(8,128)(2,1)S(1)} %constant_dynamic-update-slice_fusion.3.refs_2_, bf16[128,8,128]{2,1,0:T(8,128)(2,1)S(1)} %collective-permute-done.11.refs_3_, ...), custom_call_target="tpu_custom_call" | custom-call | tf_op jit(solution)/shard_map/later_sweep/pallas_call | solution.py:394
  62.5 12.1 %all_to_all.5 = f32[32,8,128]{2,1,0:T(8,128)S(1)} all-to-all(f32[32,8,128]{2,1,0:T(8,128)S(1)} %later_sweep.3), channel_id=1, replica_groups=mesh['grp'=4,'row'=8] {'grp','row'}, dimensions={0} | all-to-all | bytes 262144 | tf_op jit(solution)/shard_map/all_to_all | solution.py:420
  74.6 0.7 lay_out.1
  (18 shorter events, 0.1 us)
Async XLA Ops:
  2.2 7.1 %collective-permute-start = (bf16[32,8,128]{2,1,0:T(8,128)(2,1)S(1)}, bf16[32,8,128]{2,1,0:T(8,128)(2,1)S(1)}, u32[]{:S(2)}, u32[]{:S(2)}) collective-permute-start(bf16[32,8,128]{2,1,0:T(8,128)(2,1)S(1)} %get-tuple-element.16.rounded_ref), channel_id=1, source_target_pairs={{0,4},{1,3},{2,6},{3,1},{4,0},{5,7},{6,2},{7,5},{8,12},{9,11},{10,... | collective-permute-start | bytes 196616 | tf_op jit(solution)/shard_map/ppermute | solution.py:378
  9.4 6.1 %collective-permute-start.1 = (bf16[64,8,128]{2,1,0:T(8,128)(2,1)S(1)}, bf16[64,8,128]{2,1,0:T(8,128)(2,1)S(1)}, u32[]{:S(2)}, u32[]{:S(2)}) collective-permute-start(bf16[64,8,128]{2,1,0:T(8,128)(2,1)S(1)} %pad_maximum_fusion), channel_id=1, source_target_pairs={{0,2},{1,5},{2,0},{3,7},{4,6},{5,1},{6,4},{7,3},{8,10},{9,13},{10,... | collective-permute-start | bytes 393224 | tf_op jit(solution)/shard_map/ppermute | solution.py:378
  15.6 10.2 %collective-permute-start.4 = (bf16[128,8,128]{2,1,0:T(8,128)(2,1)S(1)}, bf16[128,8,128]{2,1,0:T(8,128)(2,1)S(1)}, u32[]{:S(2)}, u32[]{:S(2)}) collective-permute-start(bf16[128,8,128]{2,1,0:T(8,128)(2,1)S(1)} %constant_dynamic-update-slice_fusion.refs_2_), channel_id=1, source_target_pairs={{0,24},{8,16},{16,8},{24,0},{1,25},{9,17},{17,9},{25,1},{2,26},{10... | collective-permute-start | bytes 786440 | tf_op jit(solution)/shard_map/ppermute | solution.py:384
  18.1 10.8 %collective-permute-start.3 = (bf16[128,8,128]{2,1,0:T(8,128)(2,1)S(1)}, bf16[128,8,128]{2,1,0:T(8,128)(2,1)S(1)}, u32[]{:S(2)}, u32[]{:S(2)}) collective-permute-start(bf16[128,8,128]{2,1,0:T(8,128)(2,1)S(1)} %constant_dynamic-update-slice_fusion.refs_2_), channel_id=1, source_target_pairs={{0,16},{8,24},{16,0},{24,8},{1,17},{9,25},{17,1},{25,9},{2,18},{10... | collective-permute-start | bytes 786440 | tf_op jit(solution)/shard_map/ppermute | solution.py:384
  18.7 10.4 %collective-permute-start.2 = (bf16[128,8,128]{2,1,0:T(8,128)(2,1)S(1)}, bf16[128,8,128]{2,1,0:T(8,128)(2,1)S(1)}, u32[]{:S(2)}, u32[]{:S(2)}) collective-permute-start(bf16[128,8,128]{2,1,0:T(8,128)(2,1)S(1)} %constant_dynamic-update-slice_fusion.refs_2_), channel_id=1, source_target_pairs={{0,8},{8,0},{16,24},{24,16},{1,9},{9,1},{17,25},{25,17},{2,10},{10... | collective-permute-start | bytes 786440 | tf_op jit(solution)/shard_map/ppermute | solution.py:384
  19.1 10.3 %collective-permute-start.5 = (bf16[128,8,128]{2,1,0:T(8,128)(2,1)S(1)}, bf16[128,8,128]{2,1,0:T(8,128)(2,1)S(1)}, u32[]{:S(2)}, u32[]{:S(2)}) collective-permute-start(bf16[128,8,128]{2,1,0:T(8,128)(2,1)S(1)} %constant_dynamic-update-slice_fusion.refs_2_), channel_id=1, source_target_pairs={{0,1},{1,0},{2,3},{3,2},{4,5},{5,4},{6,7},{7,6},{8,9},{9,8},{10,11... | collective-permute-start | bytes 786440 | tf_op jit(solution)/shard_map/ppermute | solution.py:378
  25.8 3.6 %collective-permute-start.8 = (bf16[128,8,128]{2,1,0:T(8,128)(2,1)S(1)}, bf16[128,8,128]{2,1,0:T(8,128)(2,1)S(1)}, u32[]{:S(2)}, u32[]{:S(2)}) collective-permute-start(bf16[128,8,128]{2,1,0:T(8,128)(2,1)S(1)} %collective-permute-done.4.refs_5_), channel_id=1, source_target_pairs={{0,1},{1,0},{2,3},{3,2},{4,5},{5,4},{6,7},{7,6},{8,9},{9,8},{10,11... | collective-permute-start | bytes 786440 | tf_op jit(solution)/shard_map/ppermute | solution.py:378
  28.9 1.5 %collective-permute-start.7 = (bf16[128,8,128]{2,1,0:T(8,128)(2,1)S(1)}, bf16[128,8,128]{2,1,0:T(8,128)(2,1)S(1)}, u32[]{:S(2)}, u32[]{:S(2)}) collective-permute-start(bf16[128,8,128]{2,1,0:T(8,128)(2,1)S(1)} %collective-permute-done.3.refs_4_), channel_id=1, source_target_pairs={{0,1},{1,0},{2,3},{3,2},{4,5},{5,4},{6,7},{7,6},{8,9},{9,8},{10,11... | collective-permute-start | bytes 786440 | tf_op jit(solution)/shard_map/ppermute | solution.py:378
  29.1 1.8 %collective-permute-start.6 = (bf16[128,8,128]{2,1,0:T(8,128)(2,1)S(1)}, bf16[128,8,128]{2,1,0:T(8,128)(2,1)S(1)}, u32[]{:S(2)}, u32[]{:S(2)}) collective-permute-start(bf16[128,8,128]{2,1,0:T(8,128)(2,1)S(1)} %collective-permute-done.2.refs_3_), channel_id=1, source_target_pairs={{0,1},{1,0},{2,3},{3,2},{4,5},{5,4},{6,7},{7,6},{8,9},{9,8},{10,11... | collective-permute-start | bytes 786440 | tf_op jit(solution)/shard_map/ppermute | solution.py:378
  33.6 5.7 %collective-permute-start.9 = (bf16[32,8,128]{2,1,0:T(8,128)(2,1)S(1)}, bf16[32,8,128]{2,1,0:T(8,128)(2,1)S(1)}, u32[]{:S(2)}, u32[]{:S(2)}) collective-permute-start(bf16[32,8,128]{2,1,0:T(8,128)(2,1)S(1)} %get-tuple-element.23), channel_id=1, source_target_pairs={{0,4},{1,3},{2,6},{3,1},{4,0},{5,7},{6,2},{7,5},{8,12},{9,11},{10,... | collective-permute-start | bytes 196616 | tf_op jit(solution)/shard_map/ppermute | solution.py:378
  39.3 5.3 %collective-permute-start.10 = (bf16[64,8,128]{2,1,0:T(8,128)(2,1)S(1)}, bf16[64,8,128]{2,1,0:T(8,128)(2,1)S(1)}, u32[]{:S(2)}, u32[]{:S(2)}) collective-permute-start(bf16[64,8,128]{2,1,0:T(8,128)(2,1)S(1)} %pad_maximum_fusion.1), channel_id=1, source_target_pairs={{0,2},{1,5},{2,0},{3,7},{4,6},{5,1},{6,4},{7,3},{8,10},{9,13},{10,... | collective-permute-start | bytes 393224 | tf_op jit(solution)/shard_map/ppermute | solution.py:378
  44.6 10.2 %collective-permute-start.13 = (bf16[128,8,128]{2,1,0:T(8,128)(2,1)S(1)}, bf16[128,8,128]{2,1,0:T(8,128)(2,1)S(1)}, u32[]{:S(2)}, u32[]{:S(2)}) collective-permute-start(bf16[128,8,128]{2,1,0:T(8,128)(2,1)S(1)} %constant_dynamic-update-slice_fusion.3.refs_2_), channel_id=1, source_target_pairs={{0,24},{8,16},{16,8},{24,0},{1,25},{9,17},{17,9},{25,1},{2,26},{10... | collective-permute-start | bytes 786440 | tf_op jit(solution)/shard_map/ppermute | solution.py:384
  46.4 11.4 %collective-permute-start.12 = (bf16[128,8,128]{2,1,0:T(8,128)(2,1)S(1)}, bf16[128,8,128]{2,1,0:T(8,128)(2,1)S(1)}, u32[]{:S(2)}, u32[]{:S(2)}) collective-permute-start(bf16[128,8,128]{2,1,0:T(8,128)(2,1)S(1)} %constant_dynamic-update-slice_fusion.3.refs_2_), channel_id=1, source_target_pairs={{0,16},{8,24},{16,0},{24,8},{1,17},{9,25},{17,1},{25,9},{2,18},{10... | collective-permute-start | bytes 786440 | tf_op jit(solution)/shard_map/ppermute | solution.py:384
  47.6 10.3 %collective-permute-start.11 = (bf16[128,8,128]{2,1,0:T(8,128)(2,1)S(1)}, bf16[128,8,128]{2,1,0:T(8,128)(2,1)S(1)}, u32[]{:S(2)}, u32[]{:S(2)}) collective-permute-start(bf16[128,8,128]{2,1,0:T(8,128)(2,1)S(1)} %constant_dynamic-update-slice_fusion.3.refs_2_), channel_id=1, source_target_pairs={{0,8},{8,0},{16,24},{24,16},{1,9},{9,1},{17,25},{25,17},{2,10},{10... | collective-permute-start | bytes 786440 | tf_op jit(solution)/shard_map/ppermute | solution.py:384
  48.1 10.2 %collective-permute-start.14 = (bf16[128,8,128]{2,1,0:T(8,128)(2,1)S(1)}, bf16[128,8,128]{2,1,0:T(8,128)(2,1)S(1)}, u32[]{:S(2)}, u32[]{:S(2)}) collective-permute-start(bf16[128,8,128]{2,1,0:T(8,128)(2,1)S(1)} %constant_dynamic-update-slice_fusion.3.refs_2_), channel_id=1, source_target_pairs={{0,1},{1,0},{2,3},{3,2},{4,5},{5,4},{6,7},{7,6},{8,9},{9,8},{10,11... | collective-permute-start | bytes 786440 | tf_op jit(solution)/shard_map/ppermute | solution.py:378
  54.8 3.5 %collective-permute-start.17 = (bf16[128,8,128]{2,1,0:T(8,128)(2,1)S(1)}, bf16[128,8,128]{2,1,0:T(8,128)(2,1)S(1)}, u32[]{:S(2)}, u32[]{:S(2)}) collective-permute-start(bf16[128,8,128]{2,1,0:T(8,128)(2,1)S(1)} %collective-permute-done.13.refs_5_), channel_id=1, source_target_pairs={{0,1},{1,0},{2,3},{3,2},{4,5},{5,4},{6,7},{7,6},{8,9},{9,8},{10,11... | collective-permute-start | bytes 786440 | tf_op jit(solution)/shard_map/ppermute | solution.py:378
  57.8 1.5 %collective-permute-start.16 = (bf16[128,8,128]{2,1,0:T(8,128)(2,1)S(1)}, bf16[128,8,128]{2,1,0:T(8,128)(2,1)S(1)}, u32[]{:S(2)}, u32[]{:S(2)}) collective-permute-start(bf16[128,8,128]{2,1,0:T(8,128)(2,1)S(1)} %collective-permute-done.12.refs_4_), channel_id=1, source_target_pairs={{0,1},{1,0},{2,3},{3,2},{4,5},{5,4},{6,7},{7,6},{8,9},{9,8},{10,11... | collective-permute-start | bytes 786440 | tf_op jit(solution)/shard_map/ppermute | solution.py:378
  57.9 1.8 %collective-permute-start.15 = (bf16[128,8,128]{2,1,0:T(8,128)(2,1)S(1)}, bf16[128,8,128]{2,1,0:T(8,128)(2,1)S(1)}, u32[]{:S(2)}, u32[]{:S(2)}) collective-permute-start(bf16[128,8,128]{2,1,0:T(8,128)(2,1)S(1)} %collective-permute-done.11.refs_3_), channel_id=1, source_target_pairs={{0,1},{1,0},{2,3},{3,2},{4,5},{5,4},{6,7},{7,6},{8,9},{9,8},{10,11... | collective-permute-start | bytes 786440 | tf_op jit(solution)/shard_map/ppermute | solution.py:378

commit v5 on v4

--- a/solution.py
+++ b/solution.py
@@ -141,30 +141,34 @@
             ]
 
 
-def find_tiles(groups, members, pairs, cols, mask, dest, own_row, own_group):
-    slots = groups * members * CAP
+def levels(devices):
+    distances = [1 << bit for bit in range(1, devices.bit_length() - 1)]
+    half = len(distances) // 2
+    return distances[:half][::-1], distances[half:]
+
+
+def find_tiles(devices, members, pairs, cols, mask, dest, own):
+    slots = devices * CAP
     rank = cols % CAP
     source = (cols % slots) // CAP
     position = ((dest // members) * members + cols // slots) * CAP + rank
-    return place_tiles(groups, members, pairs, source, position, mask, own_row, own_group)
-
-
-def place_tiles(groups, members, pairs, source, position, mask, own_row, own_group):
-    relative_row = (source % members) ^ own_row
-    relative_group = (source // members) ^ own_group
-    piece = (relative_row % 2) * groups + relative_group
-    within = jnp.zeros_like(piece)
-    for parity in range(2):
-        for order, bit in enumerate(row_bits(members, parity)):
-            within = within + jnp.where(source % 2 == parity, ((relative_row // bit) % 2) * (1 << order), 0)
-    tile = (piece * (members // 2) + within) * pairs + position // 2
+    return place_tiles(devices, pairs, source, position, mask, own)
+
+
+def place_tiles(devices, pairs, source, position, mask, own):
+    relative = source ^ own
+
+    def collect(distances):
+        return sum(((relative // distance) % 2) * (1 << order) for order, distance in enumerate(distances))
+
+    near, far = levels(devices)
+    count = 1 << len(near)
+    even = source % 2 == 0
+    piece = jnp.where(even, collect(far), collect(near))
+    within = jnp.where(even, collect(near), collect(far))
+    tile = (((relative % 2) * count + piece) * count + within) * pairs + position // 2
     swap = (position + lax.broadcasted_iota(jnp.int32, position.shape, 0)) % 2
-    return jnp.where(mask != 0, tile * 2 + swap, 2 * groups * members * pairs)
-
-
-def row_bits(members, parity):
-    bits = [1 << bit for bit in range(members.bit_length() - 2, 0, -1)]
-    return bits[::-1] if parity else bits
+    return jnp.where(mask != 0, tile * 2 + swap, 2 * devices * pairs)
 
 
 def in_hbm(value):
@@ -172,7 +176,7 @@
 
 
 def prepare(
-    full, groups, members, perm_ref, rounded_ref, cols_hbm, mask_hbm, dest_hbm, smooth_hbm, right_hbm, blocks_hbm,
+    full, devices, members, perm_ref, rounded_ref, cols_hbm, mask_hbm, dest_hbm, smooth_hbm, right_hbm, blocks_hbm,
     own_ref, index_ref, x_ref, rp_ref, sbd_ref, blocks_ref,
     cols_ref, mask_ref, dest_ref, smooth_ref, right_ref, smooth_spread, right_spread, widened, sems,
 ):
@@ -194,8 +198,8 @@
         copy.wait()
     if full:
         index_ref[...] = find_tiles(
-            groups, members, pairs, cols_ref[...], mask_ref[...], dest_ref[...],
-            lax.axis_index("row"), lax.axis_index("grp"),
+            devices, members, pairs, cols_ref[...], mask_ref[...], dest_ref[...],
+            lax.axis_index("grp") * members + lax.axis_index("row"),
         )
     else:
         index_ref[...] = cols_ref[...]
@@ -340,11 +344,9 @@
         source = (cols % slots) // CAP
         owner = (dest.T // members) * members + cols // slots
         position = jnp.take(table, source * devices + owner, mode="clip") + cols % CAP
-        cols = place_tiles(
-            groups, members, pairs, source, position, mask, lax.axis_index("row"), lax.axis_index("grp")
-        )
+        cols = place_tiles(devices, pairs, source, position, mask, lax.axis_index(("grp", "row")))
     own, index, x, right, smooth, blocks = pl.pallas_call(
-        functools.partial(prepare, full, groups, members),
+        functools.partial(prepare, full, devices, members),
         out_shape=(
             jax.ShapeDtypeStruct(tile_shape, jnp.bfloat16),
             jax.ShapeDtypeStruct((bands, rows), jnp.int32),
@@ -374,17 +376,23 @@
         in_hbm(smoother), in_hbm(residual), in_hbm(coarse_blocks),
     )
 
-    def exchange_row(value, distances):
-        return lax.ppermute(value, "row", [(place, place ^ distances[place % 2]) for place in range(members)])
+    def exchange(value, distances):
+        pairs_of = [(place, place ^ distances[place % 2]) for place in range(devices)]
+        return lax.ppermute(value, ("grp", "row"), pairs_of)
+
+    def direct(value, steps):
+        held = [value]
+        for place in range(1, 1 << len(steps)):
+            even = sum(step[0] for order, step in enumerate(steps) if place >> order & 1)
+            odd = sum(step[1] for order, step in enumerate(steps) if place >> order & 1)
+            held.append(exchange(value, (even, odd)))
+        return held
 
     def everywhere(value, own):
-        for distances in zip(row_bits(members, 0), row_bits(members, 1)):
-            value = own = jnp.concatenate([own, exchange_row(value, distances)], axis=0)
-        near = [own] + [
-            lax.ppermute(own, "grp", [(place, place ^ distance) for place in range(groups)])
-            for distance in range(1, groups)
-        ]
-        return near + [exchange_row(part, (1, 1)) for part in near]
+        even, odd = levels(devices)
+        block = jnp.concatenate([own] + direct(value, list(zip(even, odd)))[1:], axis=0)
+        near = direct(block, list(zip(odd, even)))
+        return near + [exchange(part, (1, 1)) for part in near]
 
     def sweep(x, rounded, own, last):
         pieces = everywhere(rounded, own)

time: 75.5 us -> 64.7 us (0.86)
  waiting for transfers between devices: 36.4 us -> 20.1 us
  starting transfers between devices: 15.1 us -> 21.8 us
  blocking collectives: 12.1 us -> 10.9 us
    ppermute x18 -> x20, waiting for transfers between devices: 36.4 us -> 20.1 us  [exchange(): return lax.ppermute(value, ('grp', 'row'), pairs_of)]
    ppermute x18 -> x20, starting transfers between devices: 15.1 us -> 21.8 us  [exchange(): return lax.ppermute(value, ('grp', 'row'), pairs_of)]
    all_to_all x1, blocking collectives: 12.1 us -> 10.9 us  [local(): lax.all_to_all(x, ('grp', 'row'), split_axis=0, concat_axis=0, tiled=True)]
  transfers between devices with their start and end apart: 18 -> 20, of which waited for: 13 -> 10; matrix products, arithmetic and copies ran while one was open for 0% -> 0% of each run, Pallas kernels for 4% -> 5%
where the time goes in v5:
time: 64.7 us; the launch traced here: 64.5 us
  starting transfers between devices  21.8 us (34%)
  waiting for transfers between devices  20.1 us (31%)
  Pallas kernels  11.5 us (18%)
  blocking collectives  10.9 us (17%)
    ppermute x20, starting transfers between devices, exchange(): return lax.ppermute(value, ('grp', 'row'), pairs_of)  21.8 us
    ppermute x20, waiting for transfers between devices, exchange(): return lax.ppermute(value, ('grp', 'row'), pairs_of)  20.1 us
    all_to_all x1, blocking collectives, local(): lax.all_to_all(x, ('grp', 'row'), split_axis=0, concat_axis=0, tiled=True)  10.9 us
    pallas_call x2, Pallas kernels, sweep(): pl.pallas_call(functools.partial(later_sweep, len(pieces), not last), out...  5.55 us
    pallas_call x1, Pallas kernels, local(): pl.pallas_call(functools.partial(prepare, full, devices, members), out_sh...  3.02 us
    pallas_call x1, Pallas kernels, local(): pl.pallas_call(functools.partial(first_sweep, full), out_shape=(jax.Shape...  2.24 us
  transfers between devices with their start and end apart: 20, of which 10 were waited for; matrix products, arithmetic and copies ran while one was open for 0% of the time, Pallas kernels for 5%

profile of v5, /device:TPU:0, one launch (start us, length us, event | category | flops | bytes accessed | tf_op | source)
XLA Modules:
  0.0 64.5 jit_solution(9376698569522030950)
XLA Ops:
  0.0 2.2 %first_sweep.1 = (s32[64]{0:T(128)S(1)}, s32[32]{0:T(128)}, bf16[32,8,128]{2,1,0:T(8,128)(2,1)S(1)}) custom-call(s32[64]{0:T(128)} %bitcast.8, bf16[64,4096]{1,0:T(8,128)(2,1)} %smooth_hbm.3, bf16[64,512]{1,0:T(8,128)(2,1)} %right_hbm.3), custom_call_target="tpu_custom_call" | custom-call | tf_op jit(solution)/shard_map/first_sweep/pallas_call | solution.py:318
  2.2 5.1 %collective-permute-start.2 = (bf16[32,8,128]{2,1,0:T(8,128)(2,1)S(1)}, bf16[32,8,128]{2,1,0:T(8,128)(2,1)S(1)}, u32[]{:S(2)}, u32[]{:S(2)}) collective-permute-start(bf16[32,8,128]{2,1,0:T(8,128)(2,1)S(1)} %get-tuple-element.16.rounded_ref), channel_id=1, source_target_pairs={{0,6},{1,25},{2,4},{3,27},{4,2},{5,29},{6,0},{7,31},{8,14},{9,17},... | collective-permute-start | bytes 196616 | tf_op jit(solution)/shard_map/ppermute | solution.py:381
  7.4 0.6 collective-permute-start
  8.0 3.0 %prepare.1 = (bf16[32,8,128]{2,1,0:T(8,128)(2,1)S(1)}, s32[8,64]{1,0:T(8,128)S(1)}, f32[32,8,128]{2,1,0:T(8,128)S(1)}, bf16[32,8,128]{2,1,0:T(8,128)(2,1)S(1)}, ...) custom-call(s32[64]{0:T(128)S(1)} %get-tuple-element.15.perm_ref.refs_0_, ...), custom_call_target="tpu_custom_call" | custom-call | flops 67108864 | bytes 10485760 | tf_op jit(solution)/shard_map/prepare/pallas_call | solution.py:348
  11.1 1.5 %collective-permute-done = bf16[32,8,128]{2,1,0:T(8,128)(2,1)S(1)} collective-permute-done((bf16[32,8,128]{2,1,0:T(8,128)(2,1)S(1)}, bf16[32,8,128]{2,1,0:T(8,128)(2,1)S(1)}, u32[]{:S(2)}, u32[]{:S(2)}) %collective-permute-start) | collective-permute-done | bytes 65568 | tf_op jit(solution)/shard_map/ppermute | solution.py:381
  12.6 0.0 collective-permute-done.2
  12.6 2.5 %collective-permute-start.5 = (bf16[128,8,128]{2,1,0:T(8,128)(2,1)S(1)}, bf16[128,8,128]{2,1,0:T(8,128)(2,1)S(1)}, u32[]{:S(2)}, u32[]{:S(2)}) collective-permute-start(bf16[128,8,128]{2,1,0:T(8,128)(2,1)S(1)} %constant_dynamic-update-slice_fusion.refs_2_), channel_id=1, source_target_pairs={{0,24},{1,7},{2,26},{3,5},{4,28},{5,3},{6,30},{7,1},{8,16},{9,15},... | collective-permute-start | bytes 786440 | tf_op jit(solution)/shard_map/ppermute | solution.py:381
  15.1 0.5 collective-permute-start.4
  15.6 0.5 collective-permute-start.3
  16.2 0.0 collective-permute-start.6
  16.2 3.9 %collective-permute-done.5.refs_5_ = bf16[128,8,128]{2,1,0:T(8,128)(2,1)S(1)} collective-permute-done((bf16[128,8,128]{2,1,0:T(8,128)(2,1)S(1)}, bf16[128,8,128]{2,1,0:T(8,128)(2,1)S(1)}, u32[]{:S(2)}, u32[]{:S(2)}) %collective-permute-start.5) | collective-permute-done | bytes 262176 | tf_op jit(solution)/shard_map/ppermute | solution.py:381
  20.0 2.7 %collective-permute-done.4.refs_4_ = bf16[128,8,128]{2,1,0:T(8,128)(2,1)S(1)} collective-permute-done((bf16[128,8,128]{2,1,0:T(8,128)(2,1)S(1)}, bf16[128,8,128]{2,1,0:T(8,128)(2,1)S(1)}, u32[]{:S(2)}, u32[]{:S(2)}) %collective-permute-start.4) | collective-permute-done | bytes 262176 | tf_op jit(solution)/shard_map/ppermute | solution.py:381
  22.8 0.1 collective-permute-done.3.refs_3_
  22.8 2.0 %collective-permute-start.7 = (bf16[128,8,128]{2,1,0:T(8,128)(2,1)S(1)}, bf16[128,8,128]{2,1,0:T(8,128)(2,1)S(1)}, u32[]{:S(2)}, u32[]{:S(2)}) collective-permute-start(bf16[128,8,128]{2,1,0:T(8,128)(2,1)S(1)} %collective-permute-done.3.refs_3_), channel_id=1, source_target_pairs={{0,1},{1,0},{2,3},{3,2},{4,5},{5,4},{6,7},{7,6},{8,9},{9,8},{10,11... | collective-permute-start | bytes 786440 | tf_op jit(solution)/shard_map/ppermute | solution.py:381
  24.8 1.1 %collective-permute-done.7.refs_7_ = bf16[128,8,128]{2,1,0:T(8,128)(2,1)S(1)} collective-permute-done((bf16[128,8,128]{2,1,0:T(8,128)(2,1)S(1)}, bf16[128,8,128]{2,1,0:T(8,128)(2,1)S(1)}, u32[]{:S(2)}, u32[]{:S(2)}) %collective-permute-start.7) | collective-permute-done | bytes 262176 | tf_op jit(solution)/shard_map/ppermute | solution.py:381
  26.0 2.7 %later_sweep.2 = (f32[32,8,128]{2,1,0:T(8,128)S(1)}, bf16[32,8,128]{2,1,0:T(8,128)(2,1)S(1)}) custom-call(s32[64]{0:T(128)S(1)} %get-tuple-element.15.perm_ref.refs_0_, s32[8,64]{1,0:T(8,128)S(1)} %get-tuple-element.17.refs_1_, bf16[128,8,128]{2,1,0:T(8,128)(2,1)S(1)} %constant_dynamic-update-slice_fusion.refs_2_, ...), custom_call_target="tpu_custom_call" | custom-call | tf_op jit(solution)/shard_map/later_sweep/pallas_call | solution.py:402
  28.7 1.9 %collective-permute-start.12 = (bf16[32,8,128]{2,1,0:T(8,128)(2,1)S(1)}, bf16[32,8,128]{2,1,0:T(8,128)(2,1)S(1)}, u32[]{:S(2)}, u32[]{:S(2)}) collective-permute-start(bf16[32,8,128]{2,1,0:T(8,128)(2,1)S(1)} %get-tuple-element.23), channel_id=1, source_target_pairs={{0,6},{1,25},{2,4},{3,27},{4,2},{5,29},{6,0},{7,31},{8,14},{9,17},... | collective-permute-start | bytes 196616 | tf_op jit(solution)/shard_map/ppermute | solution.py:381
  30.6 2.6 %collective-permute-start.10 = (bf16[32,8,128]{2,1,0:T(8,128)(2,1)S(1)}, bf16[32,8,128]{2,1,0:T(8,128)(2,1)S(1)}, u32[]{:S(2)}, u32[]{:S(2)}) collective-permute-start(bf16[32,8,128]{2,1,0:T(8,128)(2,1)S(1)} %get-tuple-element.23), channel_id=1, source_target_pairs={{0,4},{1,9},{2,6},{3,11},{4,0},{5,13},{6,2},{7,15},{8,12},{9,1},{1... | collective-permute-start | bytes 196616 | tf_op jit(solution)/shard_map/ppermute | solution.py:381
  33.2 2.7 %collective-permute-done.10 = bf16[32,8,128]{2,1,0:T(8,128)(2,1)S(1)} collective-permute-done((bf16[32,8,128]{2,1,0:T(8,128)(2,1)S(1)}, bf16[32,8,128]{2,1,0:T(8,128)(2,1)S(1)}, u32[]{:S(2)}, u32[]{:S(2)}) %collective-permute-start.10) | collective-permute-done | bytes 65568 | tf_op jit(solution)/shard_map/ppermute | solution.py:381
  35.8 0.4 collective-permute-done.11
  36.2 0.0 collective-permute-done.12
  36.3 2.5 %collective-permute-start.15 = (bf16[128,8,128]{2,1,0:T(8,128)(2,1)S(1)}, bf16[128,8,128]{2,1,0:T(8,128)(2,1)S(1)}, u32[]{:S(2)}, u32[]{:S(2)}) collective-permute-start(bf16[128,8,128]{2,1,0:T(8,128)(2,1)S(1)} %constant_dynamic-update-slice_fusion.4.refs_2_), channel_id=1, source_target_pairs={{0,24},{1,7},{2,26},{3,5},{4,28},{5,3},{6,30},{7,1},{8,16},{9,15},... | collective-permute-start | bytes 786440 | tf_op jit(solution)/shard_map/ppermute | solution.py:381
  38.8 0.5 collective-permute-start.14
  39.3 0.5 collective-permute-start.13
  39.8 3.9 %collective-permute-done.15.refs_5_ = bf16[128,8,128]{2,1,0:T(8,128)(2,1)S(1)} collective-permute-done((bf16[128,8,128]{2,1,0:T(8,128)(2,1)S(1)}, bf16[128,8,128]{2,1,0:T(8,128)(2,1)S(1)}, u32[]{:S(2)}, u32[]{:S(2)}) %collective-permute-start.15) | collective-permute-done | bytes 262176 | tf_op jit(solution)/shard_map/ppermute | solution.py:381
  43.7 2.7 %collective-permute-done.14.refs_4_ = bf16[128,8,128]{2,1,0:T(8,128)(2,1)S(1)} collective-permute-done((bf16[128,8,128]{2,1,0:T(8,128)(2,1)S(1)}, bf16[128,8,128]{2,1,0:T(8,128)(2,1)S(1)}, u32[]{:S(2)}, u32[]{:S(2)}) %collective-permute-start.14) | collective-permute-done | bytes 262176 | tf_op jit(solution)/shard_map/ppermute | solution.py:381
  46.4 0.2 collective-permute-start.18
  46.6 2.3 %collective-permute-start.17 = (bf16[128,8,128]{2,1,0:T(8,128)(2,1)S(1)}, bf16[128,8,128]{2,1,0:T(8,128)(2,1)S(1)}, u32[]{:S(2)}, u32[]{:S(2)}) collective-permute-start(bf16[128,8,128]{2,1,0:T(8,128)(2,1)S(1)} %collective-permute-done.13.refs_3_), channel_id=1, source_target_pairs={{0,1},{1,0},{2,3},{3,2},{4,5},{5,4},{6,7},{7,6},{8,9},{9,8},{10,11... | collective-permute-start | bytes 786440 | tf_op jit(solution)/shard_map/ppermute | solution.py:381
  48.9 1.1 %collective-permute-done.17.refs_7_ = bf16[128,8,128]{2,1,0:T(8,128)(2,1)S(1)} collective-permute-done((bf16[128,8,128]{2,1,0:T(8,128)(2,1)S(1)}, bf16[128,8,128]{2,1,0:T(8,128)(2,1)S(1)}, u32[]{:S(2)}, u32[]{:S(2)}) %collective-permute-start.17) | collective-permute-done | bytes 262176 | tf_op jit(solution)/shard_map/ppermute | solution.py:381
  50.1 2.8 %later_sweep.3 = f32[32,8,128]{2,1,0:T(8,128)S(1)} custom-call(s32[64]{0:T(128)S(1)} %get-tuple-element.15.perm_ref.refs_0_, s32[8,64]{1,0:T(8,128)S(1)} %get-tuple-element.17.refs_1_, bf16[128,8,128]{2,1,0:T(8,128)(2,1)S(1)} %constant_dynamic-update-slice_fusion.4.refs_2_, bf16[128,8,128]{2,1,0:T(8,128)(2,1)S(1)} %collective-permute-done.13.refs_3_, ...), custom_call_target="tpu_custom_call" | custom-call | tf_op jit(solution)/shard_map/later_sweep/pallas_call | solution.py:402
  52.9 10.9 %all_to_all.5 = f32[32,8,128]{2,1,0:T(8,128)S(1)} all-to-all(f32[32,8,128]{2,1,0:T(8,128)S(1)} %later_sweep.3), channel_id=1, replica_groups=mesh['grp'=4,'row'=8] {'grp','row'}, dimensions={0} | all-to-all | bytes 262144 | tf_op jit(solution)/shard_map/all_to_all | solution.py:428
  63.8 0.7 %lay_out.1 = f32[64,512]{1,0:T(8,128)} custom-call(f32[256,128]{1,0:T(8,128)S(1)} %bitcast.5), custom_call_target="tpu_custom_call" | custom-call | tf_op jit(solution)/shard_map/lay_out/pallas_call | solution.py:429
  (22 shorter events, 0.1 us)
Async XLA Ops:
  2.2 10.3 %collective-permute-start.2 = (bf16[32,8,128]{2,1,0:T(8,128)(2,1)S(1)}, bf16[32,8,128]{2,1,0:T(8,128)(2,1)S(1)}, u32[]{:S(2)}, u32[]{:S(2)}) collective-permute-start(bf16[32,8,128]{2,1,0:T(8,128)(2,1)S(1)} %get-tuple-element.16.rounded_ref), channel_id=1, source_target_pairs={{0,6},{1,25},{2,4},{3,27},{4,2},{5,29},{6,0},{7,31},{8,14},{9,17},... | collective-permute-start | bytes 196616 | tf_op jit(solution)/shard_map/ppermute | solution.py:381
  7.4 5.2 %collective-permute-start.1 = (bf16[32,8,128]{2,1,0:T(8,128)(2,1)S(1)}, bf16[32,8,128]{2,1,0:T(8,128)(2,1)S(1)}, u32[]{:S(2)}, u32[]{:S(2)}) collective-permute-start(bf16[32,8,128]{2,1,0:T(8,128)(2,1)S(1)} %get-tuple-element.16.rounded_ref), channel_id=1, source_target_pairs={{0,2},{1,17},{2,0},{3,19},{4,6},{5,21},{6,4},{7,23},{8,10},{9,25},... | collective-permute-start | bytes 196616 | tf_op jit(solution)/shard_map/ppermute | solution.py:381
  7.4 5.2 %collective-permute-start = (bf16[32,8,128]{2,1,0:T(8,128)(2,1)S(1)}, bf16[32,8,128]{2,1,0:T(8,128)(2,1)S(1)}, u32[]{:S(2)}, u32[]{:S(2)}) collective-permute-start(bf16[32,8,128]{2,1,0:T(8,128)(2,1)S(1)} %get-tuple-element.16.rounded_ref), channel_id=1, source_target_pairs={{0,4},{1,9},{2,6},{3,11},{4,0},{5,13},{6,2},{7,15},{8,12},{9,1},{1... | collective-permute-start | bytes 196616 | tf_op jit(solution)/shard_map/ppermute | solution.py:381
  12.6 7.4 %collective-permute-start.5 = (bf16[128,8,128]{2,1,0:T(8,128)(2,1)S(1)}, bf16[128,8,128]{2,1,0:T(8,128)(2,1)S(1)}, u32[]{:S(2)}, u32[]{:S(2)}) collective-permute-start(bf16[128,8,128]{2,1,0:T(8,128)(2,1)S(1)} %constant_dynamic-update-slice_fusion.refs_2_), channel_id=1, source_target_pairs={{0,24},{1,7},{2,26},{3,5},{4,28},{5,3},{6,30},{7,1},{8,16},{9,15},... | collective-permute-start | bytes 786440 | tf_op jit(solution)/shard_map/ppermute | solution.py:381
  15.1 7.6 %collective-permute-start.4 = (bf16[128,8,128]{2,1,0:T(8,128)(2,1)S(1)}, bf16[128,8,128]{2,1,0:T(8,128)(2,1)S(1)}, u32[]{:S(2)}, u32[]{:S(2)}) collective-permute-start(bf16[128,8,128]{2,1,0:T(8,128)(2,1)S(1)} %constant_dynamic-update-slice_fusion.refs_2_), channel_id=1, source_target_pairs={{0,16},{1,3},{2,18},{3,1},{4,20},{5,7},{6,22},{7,5},{8,24},{9,11},... | collective-permute-start | bytes 786440 | tf_op jit(solution)/shard_map/ppermute | solution.py:381
  15.6 7.2 %collective-permute-start.3 = (bf16[128,8,128]{2,1,0:T(8,128)(2,1)S(1)}, bf16[128,8,128]{2,1,0:T(8,128)(2,1)S(1)}, u32[]{:S(2)}, u32[]{:S(2)}) collective-permute-start(bf16[128,8,128]{2,1,0:T(8,128)(2,1)S(1)} %constant_dynamic-update-slice_fusion.refs_2_), channel_id=1, source_target_pairs={{0,8},{1,5},{2,10},{3,7},{4,12},{5,1},{6,14},{7,3},{8,0},{9,13},{1... | collective-permute-start | bytes 786440 | tf_op jit(solution)/shard_map/ppermute | solution.py:381
  16.2 8.7 %collective-permute-start.6 = (bf16[128,8,128]{2,1,0:T(8,128)(2,1)S(1)}, bf16[128,8,128]{2,1,0:T(8,128)(2,1)S(1)}, u32[]{:S(2)}, u32[]{:S(2)}) collective-permute-start(bf16[128,8,128]{2,1,0:T(8,128)(2,1)S(1)} %constant_dynamic-update-slice_fusion.refs_2_), channel_id=1, source_target_pairs={{0,1},{1,0},{2,3},{3,2},{4,5},{5,4},{6,7},{7,6},{8,9},{9,8},{10,11... | collective-permute-start | bytes 786440 | tf_op jit(solution)/shard_map/ppermute | solution.py:381
  20.0 4.8 %collective-permute-start.9 = (bf16[128,8,128]{2,1,0:T(8,128)(2,1)S(1)}, bf16[128,8,128]{2,1,0:T(8,128)(2,1)S(1)}, u32[]{:S(2)}, u32[]{:S(2)}) collective-permute-start(bf16[128,8,128]{2,1,0:T(8,128)(2,1)S(1)} %collective-permute-done.5.refs_5_), channel_id=1, source_target_pairs={{0,1},{1,0},{2,3},{3,2},{4,5},{5,4},{6,7},{7,6},{8,9},{9,8},{10,11... | collective-permute-start | bytes 786440 | tf_op jit(solution)/shard_map/ppermute | solution.py:381
  22.7 2.1 %collective-permute-start.8 = (bf16[128,8,128]{2,1,0:T(8,128)(2,1)S(1)}, bf16[128,8,128]{2,1,0:T(8,128)(2,1)S(1)}, u32[]{:S(2)}, u32[]{:S(2)}) collective-permute-start(bf16[128,8,128]{2,1,0:T(8,128)(2,1)S(1)} %collective-permute-done.4.refs_4_), channel_id=1, source_target_pairs={{0,1},{1,0},{2,3},{3,2},{4,5},{5,4},{6,7},{7,6},{8,9},{9,8},{10,11... | collective-permute-start | bytes 786440 | tf_op jit(solution)/shard_map/ppermute | solution.py:381
  22.8 3.1 %collective-permute-start.7 = (bf16[128,8,128]{2,1,0:T(8,128)(2,1)S(1)}, bf16[128,8,128]{2,1,0:T(8,128)(2,1)S(1)}, u32[]{:S(2)}, u32[]{:S(2)}) collective-permute-start(bf16[128,8,128]{2,1,0:T(8,128)(2,1)S(1)} %collective-permute-done.3.refs_3_), channel_id=1, source_target_pairs={{0,1},{1,0},{2,3},{3,2},{4,5},{5,4},{6,7},{7,6},{8,9},{9,8},{10,11... | collective-permute-start | bytes 786440 | tf_op jit(solution)/shard_map/ppermute | solution.py:381
  28.7 7.5 %collective-permute-start.12 = (bf16[32,8,128]{2,1,0:T(8,128)(2,1)S(1)}, bf16[32,8,128]{2,1,0:T(8,128)(2,1)S(1)}, u32[]{:S(2)}, u32[]{:S(2)}) collective-permute-start(bf16[32,8,128]{2,1,0:T(8,128)(2,1)S(1)} %get-tuple-element.23), channel_id=1, source_target_pairs={{0,6},{1,25},{2,4},{3,27},{4,2},{5,29},{6,0},{7,31},{8,14},{9,17},... | collective-permute-start | bytes 196616 | tf_op jit(solution)/shard_map/ppermute | solution.py:381
  30.6 5.6 %collective-permute-start.11 = (bf16[32,8,128]{2,1,0:T(8,128)(2,1)S(1)}, bf16[32,8,128]{2,1,0:T(8,128)(2,1)S(1)}, u32[]{:S(2)}, u32[]{:S(2)}) collective-permute-start(bf16[32,8,128]{2,1,0:T(8,128)(2,1)S(1)} %get-tuple-element.23), channel_id=1, source_target_pairs={{0,2},{1,17},{2,0},{3,19},{4,6},{5,21},{6,4},{7,23},{8,10},{9,25},... | collective-permute-start | bytes 196616 | tf_op jit(solution)/shard_map/ppermute | solution.py:381
  30.6 5.2 %collective-permute-start.10 = (bf16[32,8,128]{2,1,0:T(8,128)(2,1)S(1)}, bf16[32,8,128]{2,1,0:T(8,128)(2,1)S(1)}, u32[]{:S(2)}, u32[]{:S(2)}) collective-permute-start(bf16[32,8,128]{2,1,0:T(8,128)(2,1)S(1)} %get-tuple-element.23), channel_id=1, source_target_pairs={{0,4},{1,9},{2,6},{3,11},{4,0},{5,13},{6,2},{7,15},{8,12},{9,1},{1... | collective-permute-start | bytes 196616 | tf_op jit(solution)/shard_map/ppermute | solution.py:381
  36.3 7.4 %collective-permute-start.15 = (bf16[128,8,128]{2,1,0:T(8,128)(2,1)S(1)}, bf16[128,8,128]{2,1,0:T(8,128)(2,1)S(1)}, u32[]{:S(2)}, u32[]{:S(2)}) collective-permute-start(bf16[128,8,128]{2,1,0:T(8,128)(2,1)S(1)} %constant_dynamic-update-slice_fusion.4.refs_2_), channel_id=1, source_target_pairs={{0,24},{1,7},{2,26},{3,5},{4,28},{5,3},{6,30},{7,1},{8,16},{9,15},... | collective-permute-start | bytes 786440 | tf_op jit(solution)/shard_map/ppermute | solution.py:381
  38.8 7.6 %collective-permute-start.14 = (bf16[128,8,128]{2,1,0:T(8,128)(2,1)S(1)}, bf16[128,8,128]{2,1,0:T(8,128)(2,1)S(1)}, u32[]{:S(2)}, u32[]{:S(2)}) collective-permute-start(bf16[128,8,128]{2,1,0:T(8,128)(2,1)S(1)} %constant_dynamic-update-slice_fusion.4.refs_2_), channel_id=1, source_target_pairs={{0,16},{1,3},{2,18},{3,1},{4,20},{5,7},{6,22},{7,5},{8,24},{9,11},... | collective-permute-start | bytes 786440 | tf_op jit(solution)/shard_map/ppermute | solution.py:381
  39.3 7.3 %collective-permute-start.13 = (bf16[128,8,128]{2,1,0:T(8,128)(2,1)S(1)}, bf16[128,8,128]{2,1,0:T(8,128)(2,1)S(1)}, u32[]{:S(2)}, u32[]{:S(2)}) collective-permute-start(bf16[128,8,128]{2,1,0:T(8,128)(2,1)S(1)} %constant_dynamic-update-slice_fusion.4.refs_2_), channel_id=1, source_target_pairs={{0,8},{1,5},{2,10},{3,7},{4,12},{5,1},{6,14},{7,3},{8,0},{9,13},{1... | collective-permute-start | bytes 786440 | tf_op jit(solution)/shard_map/ppermute | solution.py:381
  39.8 9.1 %collective-permute-start.16 = (bf16[128,8,128]{2,1,0:T(8,128)(2,1)S(1)}, bf16[128,8,128]{2,1,0:T(8,128)(2,1)S(1)}, u32[]{:S(2)}, u32[]{:S(2)}) collective-permute-start(bf16[128,8,128]{2,1,0:T(8,128)(2,1)S(1)} %constant_dynamic-update-slice_fusion.4.refs_2_), channel_id=1, source_target_pairs={{0,1},{1,0},{2,3},{3,2},{4,5},{5,4},{6,7},{7,6},{8,9},{9,8},{10,11... | collective-permute-start | bytes 786440 | tf_op jit(solution)/shard_map/ppermute | solution.py:381
  43.7 5.2 %collective-permute-start.19 = (bf16[128,8,128]{2,1,0:T(8,128)(2,1)S(1)}, bf16[128,8,128]{2,1,0:T(8,128)(2,1)S(1)}, u32[]{:S(2)}, u32[]{:S(2)}) collective-permute-start(bf16[128,8,128]{2,1,0:T(8,128)(2,1)S(1)} %collective-permute-done.15.refs_5_), channel_id=1, source_target_pairs={{0,1},{1,0},{2,3},{3,2},{4,5},{5,4},{6,7},{7,6},{8,9},{9,8},{10,11... | collective-permute-start | bytes 786440 | tf_op jit(solution)/shard_map/ppermute | solution.py:381
  46.4 2.5 %collective-permute-start.18 = (bf16[128,8,128]{2,1,0:T(8,128)(2,1)S(1)}, bf16[128,8,128]{2,1,0:T(8,128)(2,1)S(1)}, u32[]{:S(2)}, u32[]{:S(2)}) collective-permute-start(bf16[128,8,128]{2,1,0:T(8,128)(2,1)S(1)} %collective-permute-done.14.refs_4_), channel_id=1, source_target_pairs={{0,1},{1,0},{2,3},{3,2},{4,5},{5,4},{6,7},{7,6},{8,9},{9,8},{10,11... | collective-permute-start | bytes 786440 | tf_op jit(solution)/shard_map/ppermute | solution.py:381
  46.6 3.4 %collective-permute-start.17 = (bf16[128,8,128]{2,1,0:T(8,128)(2,1)S(1)}, bf16[128,8,128]{2,1,0:T(8,128)(2,1)S(1)}, u32[]{:S(2)}, u32[]{:S(2)}) collective-permute-start(bf16[128,8,128]{2,1,0:T(8,128)(2,1)S(1)} %collective-permute-done.13.refs_3_), channel_id=1, source_target_pairs={{0,1},{1,0},{2,3},{3,2},{4,5},{5,4},{6,7},{7,6},{8,9},{9,8},{10,11... | collective-permute-start | bytes 786440 | tf_op jit(solution)/shard_map/ppermute | solution.py:381

commit v6 on v5

--- a/solution.py
+++ b/solution.py
@@ -164,8 +164,9 @@
     near, far = levels(devices)
     count = 1 << len(near)
     even = source % 2 == 0
-    piece = jnp.where(even, collect(far), collect(near))
+    piece = count - 1 - jnp.where(even, collect(far), collect(near))
     within = jnp.where(even, collect(near), collect(far))
+    within = jnp.where(within == 0, count - 1, jnp.where(within == count - 1, 0, within))
     tile = (((relative % 2) * count + piece) * count + within) * pairs + position // 2
     swap = (position + lax.broadcasted_iota(jnp.int32, position.shape, 0)) % 2
     return jnp.where(mask != 0, tile * 2 + swap, 2 * devices * pairs)
@@ -175,38 +176,54 @@
     return pltpu.with_memory_space_constraint(value, pltpu.HBM)
 
 
-def prepare(
-    full, devices, members, perm_ref, rounded_ref, cols_hbm, mask_hbm, dest_hbm, smooth_hbm, right_hbm, blocks_hbm,
-    own_ref, index_ref, x_ref, rp_ref, sbd_ref, blocks_ref,
-    cols_ref, mask_ref, dest_ref, smooth_ref, right_ref, smooth_spread, right_spread, widened, sems,
+def locate(
+    full, devices, members, rounded_ref, cols_hbm, mask_hbm, dest_hbm, own_ref, index_ref,
+    cols_ref, mask_ref, dest_ref, lined, sems, line_sems,
 ):
-    moves = [
-        (cols_hbm, cols_ref), (mask_hbm, mask_ref), (dest_hbm, dest_ref),
-        (right_hbm, right_ref), (smooth_hbm, smooth_ref), (blocks_hbm, blocks_ref),
-    ]
+    moves = [(cols_hbm, cols_ref), (mask_hbm, mask_ref), (dest_hbm, dest_ref)]
     copies = [pltpu.make_async_copy(*move, sems.at[number]) for number, move in enumerate(moves)]
     for copy in copies:
         copy.start()
+    own_ref[...] = rounded_ref[...]
+    for copy in copies:
+        copy.wait()
+    bands, rows = cols_ref.shape
+    places = cols_ref[...]
+    if full:
+        places = find_tiles(
+            devices, members, rows // 2, places, mask_ref[...], dest_ref[...],
+            lax.axis_index("grp") * members + lax.axis_index("row"),
+        )
+    lined[:, :rows] = places
+    lines = [
+        pltpu.make_async_copy(lined.at[band], index_ref.at[pl.ds(band * LANES, LANES)], line_sems.at[band])
+        for band in range(bands)
+    ]
+    for line in lines:
+        line.start()
+    for line in lines:
+        line.wait()
+
+
+def prepare(
+    perm_ref, gathered_ref, smooth_hbm, right_hbm, blocks_hbm, own_ref, x_ref, rp_ref, sbd_ref, blocks_ref,
+    smooth_ref, right_ref, smooth_spread, right_spread, widened, sems,
+):
+    moves = [(right_hbm, right_ref), (smooth_hbm, smooth_ref), (blocks_hbm, blocks_ref)]
+    copies = [pltpu.make_async_copy(*move, sems.at[number]) for number, move in enumerate(moves)]
+    for copy in copies:
+        copy.start()
+    own_ref[...] = gathered_ref[...]
     rows, smooth_width = smooth_ref.shape
     block = LANES // 2
     half = smooth_width // LANES
     pairs = rows // 2
     lower = lax.broadcasted_iota(jnp.int32, (SUB, LANES), 1) < block
     low_half = lax.broadcasted_iota(jnp.int32, (half, LANES), 1) < block
-    own_ref[...] = rounded_ref[...]
-    for copy in copies[:3]:
-        copy.wait()
-    if full:
-        index_ref[...] = find_tiles(
-            devices, members, pairs, cols_ref[...], mask_ref[...], dest_ref[...],
-            lax.axis_index("grp") * members + lax.axis_index("row"),
-        )
-    else:
-        index_ref[...] = cols_ref[...]
-    copies[3].wait()
+    copies[0].wait()
     copied = right_copies(right_ref.shape[1])
     spread_rows(right_ref, right_spread, copied)
-    copies[4].wait()
+    copies[1].wait()
     spread_rows(smooth_ref, smooth_spread, smooth_copies(smooth_width))
     for pair in range(pairs):
         low, high = perm_ref[2 * pair], perm_ref[2 * pair + 1]
@@ -224,12 +241,12 @@
             widened[pl.ds(base + number * block, half, stride=2), :] = jnp.where(keep, first, 0.0)
             widened[pl.ds(base + number * block + 1, half, stride=2), :] = jnp.where(keep, second, 0.0)
     for pair in range(pairs):
-        sbd_ref[pair] = widened[pl.ds(pair * LANES, LANES), :].astype(jnp.bfloat16)
+        sbd_ref[pair] = widened[pl.ds(pair * LANES, LANES), :].T.astype(jnp.bfloat16)
     for pair in range(pairs):
         x_ref[pair] = lax.dot_general(
-            rp_ref[pair], sbd_ref[pair], TRANSPOSED, preferred_element_type=jnp.float32
-        )
-    copies[5].wait()
+            rp_ref[pair], sbd_ref[pair], PLAIN, preferred_element_type=jnp.float32
+        )
+    copies[2].wait()
 
 
 def later_sweep(piece_count, with_rounded, *refs):
@@ -241,7 +258,7 @@
     rounded_ref = refs[1] if with_rounded else None
     tiles, defects = refs[2 if with_rounded else 1 :]
     pairs = x_ref.shape[0]
-    _, block, width = blocks.shape
+    rows, block, width = blocks.shape
     bands = width // block
 
     start = 0
@@ -256,7 +273,7 @@
     first_half = lax.broadcasted_iota(jnp.int32, (NRHS, LANES), 0) < NRHS // 2
 
     def fetch(row, band):
-        entry = index_ref[band, row]
+        entry = index_ref[band * LANES + row]
         tile = tiles[lax.shift_right_logical(entry, 1)].astype(jnp.float32)
         return pltpu.roll(tile, (entry & 1) * block, 1)
 
@@ -265,23 +282,22 @@
             jnp.where(lower, fetch(row, 2 * half), fetch(row, 2 * half + 1)) for half in range(bands // 2)
         ]
 
-    for pair in range(pairs):
-        low, high = perm_ref[2 * pair], perm_ref[2 * pair + 1]
-        gathered = jnp.concatenate(
-            [
-                jnp.concatenate(values(low), axis=1),
-                jnp.concatenate(values(high), axis=1),
-            ],
-            axis=0,
-        ).astype(jnp.bfloat16)
-        weights = jnp.concatenate([blocks[low], blocks[high]], axis=0)
-        applied = lax.dot_general(gathered, weights, TRANSPOSED, preferred_element_type=jnp.float32)
-        image = jnp.where(lower, applied[:NRHS], applied[NRHS:])
-        defects[pair] = (rp_ref[pair].astype(jnp.float32) - image).astype(jnp.bfloat16)
+    for quad in range(rows // 4):
+        members = [perm_ref[4 * quad + member] for member in range(4)]
+        gathered = jnp.concatenate([jnp.concatenate(values(row), axis=1) for row in members], axis=0)
+        weights = jnp.concatenate([blocks[row] for row in members], axis=0)
+        applied = lax.dot_general(
+            gathered.astype(jnp.bfloat16), weights, TRANSPOSED, preferred_element_type=jnp.float32
+        )
+        for half in range(2):
+            pair = 2 * quad + half
+            own = applied[2 * NRHS * half : 2 * NRHS * (half + 1), LANES * half : LANES * (half + 1)]
+            image = jnp.where(lower, own[:NRHS], own[NRHS:])
+            defects[pair] = (rp_ref[pair].astype(jnp.float32) - image).astype(jnp.bfloat16)
 
     for pair in range(pairs):
         x = x_ref[pair] + lax.dot_general(
-            defects[pair], sbd_ref[pair], TRANSPOSED, preferred_element_type=jnp.float32
+            defects[pair], sbd_ref[pair], PLAIN, preferred_element_type=jnp.float32
         )
         if with_rounded:
             out_ref[pair] = x
@@ -345,36 +361,26 @@
         owner = (dest.T // members) * members + cols // slots
         position = jnp.take(table, source * devices + owner, mode="clip") + cols % CAP
         cols = place_tiles(devices, pairs, source, position, mask, lax.axis_index(("grp", "row")))
-    own, index, x, right, smooth, blocks = pl.pallas_call(
-        functools.partial(prepare, full, devices, members),
+    own, index = pl.pallas_call(
+        functools.partial(locate, full, devices, members),
         out_shape=(
             jax.ShapeDtypeStruct(tile_shape, jnp.bfloat16),
-            jax.ShapeDtypeStruct((bands, rows), jnp.int32),
-            jax.ShapeDtypeStruct(tile_shape, jnp.float32),
-            jax.ShapeDtypeStruct(tile_shape, jnp.bfloat16),
-            jax.ShapeDtypeStruct((pairs, 2 * block, 2 * block), jnp.bfloat16),
-            jax.ShapeDtypeStruct(coarse_blocks.shape, jnp.bfloat16),
+            jax.ShapeDtypeStruct((bands * LANES,), jnp.int32),
         ),
-        in_specs=[smem, vmem] + [hbm] * 6,
-        out_specs=(vmem,) * 6,
+        in_specs=[vmem] + [hbm] * 3,
+        out_specs=(vmem, smem),
         scratch_shapes=[
             pltpu.VMEM((bands, rows), jnp.int32),
             pltpu.VMEM((bands, rows), jnp.int32),
             pltpu.VMEM((1, rows), jnp.int32),
-            pltpu.VMEM(smoother.shape, jnp.bfloat16),
-            pltpu.VMEM(residual.shape, jnp.bfloat16),
-            pltpu.VMEM((smooth_rows, LANES), jnp.float32),
-            pltpu.VMEM((right_rows, LANES), jnp.float32),
-            pltpu.VMEM((pairs * LANES, LANES), jnp.float32),
-            pltpu.SemaphoreType.DMA((6,)),
+            pltpu.VMEM((bands, LANES), jnp.int32),
+            pltpu.SemaphoreType.DMA((3,)),
+            pltpu.SemaphoreType.DMA((bands,)),
         ],
         compiler_params=params,
-        cost_estimate=pl.CostEstimate(flops=1 << 26, bytes_accessed=10 << 20, transcendentals=0),
-        name="prepare",
-    )(
-        perm, rounded, in_hbm(cols), in_hbm(mask), in_hbm(dest.T),
-        in_hbm(smoother), in_hbm(residual), in_hbm(coarse_blocks),
-    )
+        cost_estimate=pl.CostEstimate(flops=1 << 20, bytes_accessed=2 << 20, transcendentals=0),
+        name="locate",
+    )(rounded, in_hbm(cols), in_hbm(mask), in_hbm(dest.T))
 
     def exchange(value, distances):
         pairs_of = [(place, place ^ distances[place % 2]) for place in range(devices)]
@@ -388,14 +394,44 @@
             held.append(exchange(value, (even, odd)))
         return held
 
-    def everywhere(value, own):
-        even, odd = levels(devices)
-        block = jnp.concatenate([own] + direct(value, list(zip(even, odd)))[1:], axis=0)
-        near = direct(block, list(zip(odd, even)))
-        return near + [exchange(part, (1, 1)) for part in near]
-
-    def sweep(x, rounded, own, last):
-        pieces = everywhere(rounded, own)
+    even, odd = levels(devices)
+
+    def first_level(value, own):
+        held = direct(value, list(zip(even, odd)))
+        return jnp.concatenate([held[-1]] + held[1:-1] + [own], axis=0)
+
+    def second_level(value, own):
+        near = direct(value, list(zip(odd, even)))
+        near, away = near[::-1], ([own] + near[1:])[::-1]
+        return near + [exchange(part, (1, 1)) for part in away]
+
+    gathered = first_level(rounded, own)
+    own, x, right, smooth, blocks = pl.pallas_call(
+        prepare,
+        out_shape=(
+            jax.ShapeDtypeStruct(gathered.shape, jnp.bfloat16),
+            jax.ShapeDtypeStruct(tile_shape, jnp.float32),
+            jax.ShapeDtypeStruct(tile_shape, jnp.bfloat16),
+            jax.ShapeDtypeStruct((pairs, 2 * block, 2 * block), jnp.bfloat16),
+            jax.ShapeDtypeStruct(coarse_blocks.shape, jnp.bfloat16),
+        ),
+        in_specs=[smem, vmem] + [hbm] * 3,
+        out_specs=(vmem,) * 5,
+        scratch_shapes=[
+            pltpu.VMEM(smoother.shape, jnp.bfloat16),
+            pltpu.VMEM(residual.shape, jnp.bfloat16),
+            pltpu.VMEM((smooth_rows, LANES), jnp.float32),
+            pltpu.VMEM((right_rows, LANES), jnp.float32),
+            pltpu.VMEM((pairs * LANES, LANES), jnp.float32),
+            pltpu.SemaphoreType.DMA((3,)),
+        ],
+        compiler_params=params,
+        cost_estimate=pl.CostEstimate(flops=1 << 26, bytes_accessed=10 << 20, transcendentals=0),
+        name="prepare",
+    )(perm, gathered, in_hbm(smoother), in_hbm(residual), in_hbm(coarse_blocks))
+
+    def sweep(x, value, own, last):
+        pieces = second_level(value, own)
         outs = [jax.ShapeDtypeStruct(tile_shape, jnp.float32)]
         if not last:
             outs.append(jax.ShapeDtypeStruct(tile_shape, jnp.bfloat16))
@@ -412,8 +448,9 @@
             name="later_sweep",
         )(perm, index, *pieces, blocks, smooth, right, x)
 
-    x, rounded = sweep(x, rounded, own, False)
-    (x,) = sweep(x, rounded, rounded, True)
+    x, rounded = sweep(x, gathered, own, False)
+    gathered = first_level(rounded, rounded)
+    (x,) = sweep(x, gathered, gathered, True)
 
     if not full:
         flat = x.reshape(rows, NRHS * block)

time: 64.7 us -> 63.5 us (0.981)
  starting transfers between devices: 21.8 us -> 20.3 us
  waiting for transfers between devices: 20.1 us -> 18.8 us
  Pallas kernels: 11.5 us -> 12.7 us
    pallas_call x1 -> x2, Pallas kernels: 3.02 us -> 5.05 us  [the longest x1 2.95 us: local(): pl.pallas_call(prepare, out_shape=(jax.ShapeDtypeStruct(gathered.shape, j...]
    ppermute x20, starting transfers between devices: 21.8 us -> 20.3 us  [exchange(): return lax.ppermute(value, ('grp', 'row'), pairs_of)]
    ppermute x20, waiting for transfers between devices: 20.1 us -> 18.8 us  [exchange(): return lax.ppermute(value, ('grp', 'row'), pairs_of)]
    pallas_call x2, Pallas kernels: 5.55 us -> 4.73 us  [sweep(): pl.pallas_call(functools.partial(later_sweep, len(pieces), not last), out...]
  transfers between devices with their start and end apart: 20 -> 20, of which waited for: 10 -> 11; matrix products, arithmetic and copies ran while one was open for 0% -> 0% of each run, Pallas kernels for 5% -> 8%
where the time goes in v6:
time: 63.5 us; the launch traced here: 63.3 us
  starting transfers between devices  20.3 us (32%)
  waiting for transfers between devices  18.8 us (30%)
  Pallas kernels  12.7 us (20%)
  blocking collectives  11.3 us (18%)
    ppermute x20, starting transfers between devices, exchange(): return lax.ppermute(value, ('grp', 'row'), pairs_of)  20.3 us
    ppermute x20, waiting for transfers between devices, exchange(): return lax.ppermute(value, ('grp', 'row'), pairs_of)  18.8 us
    all_to_all x1, blocking collectives, local(): lax.all_to_all(x, ('grp', 'row'), split_axis=0, concat_axis=0, tiled=True)  11.3 us
    pallas_call x2, Pallas kernels, sweep(): pl.pallas_call(functools.partial(later_sweep, len(pieces), not last), out...  4.73 us
    pallas_call x1, Pallas kernels, local(): pl.pallas_call(prepare, out_shape=(jax.ShapeDtypeStruct(gathered.shape, j...  2.95 us
    pallas_call x1, Pallas kernels, local(): pl.pallas_call(functools.partial(first_sweep, full), out_shape=(jax.Shape...  2.24 us
    pallas_call x1, Pallas kernels, local(): pl.pallas_call(functools.partial(locate, full, devices, members), out_sha...  2.09 us
  transfers between devices with their start and end apart: 20, of which 11 were waited for; matrix products, arithmetic and copies ran while one was open for 0% of the time, Pallas kernels for 8%

profile of v6, /device:TPU:0, one launch (start us, length us, event | category | flops | bytes accessed | tf_op | source)
XLA Modules:
  0.0 63.3 jit_solution(17444860228434000425)
XLA Ops:
  0.0 2.2 %first_sweep.1 = (s32[64]{0:T(128)S(1)}, s32[32]{0:T(128)}, bf16[32,8,128]{2,1,0:T(8,128)(2,1)S(1)}) custom-call(s32[64]{0:T(128)} %bitcast.8, bf16[64,4096]{1,0:T(8,128)(2,1)} %smooth_hbm.3, bf16[64,512]{1,0:T(8,128)(2,1)} %right_hbm.3), custom_call_target="tpu_custom_call" | custom-call | tf_op jit(solution)/shard_map/first_sweep/pallas_call | solution.py:334
  2.2 5.1 %collective-permute-start = (bf16[32,8,128]{2,1,0:T(8,128)(2,1)S(1)}, bf16[32,8,128]{2,1,0:T(8,128)(2,1)S(1)}, u32[]{:S(2)}, u32[]{:S(2)}) collective-permute-start(bf16[32,8,128]{2,1,0:T(8,128)(2,1)S(1)} %get-tuple-element.17.rounded_ref), channel_id=1, source_target_pairs={{0,6},{1,25},{2,4},{3,27},{4,2},{5,29},{6,0},{7,31},{8,14},{9,17},... | collective-permute-start | bytes 196616 | tf_op jit(solution)/shard_map/ppermute | solution.py:387
  7.4 0.6 %collective-permute-start.2 = (bf16[32,8,128]{2,1,0:T(8,128)(2,1)S(1)}, bf16[32,8,128]{2,1,0:T(8,128)(2,1)S(1)}, u32[]{:S(2)}, u32[]{:S(2)}) collective-permute-start(bf16[32,8,128]{2,1,0:T(8,128)(2,1)S(1)} %get-tuple-element.17.rounded_ref), channel_id=1, source_target_pairs={{0,2},{1,17},{2,0},{3,19},{4,6},{5,21},{6,4},{7,23},{8,10},{9,25},... | collective-permute-start | bytes 196616 | tf_op jit(solution)/shard_map/ppermute | solution.py:387
  8.0 2.1 %locate.1 = (bf16[32,8,128]{2,1,0:T(8,128)(2,1)S(1)}, s32[1024]{0:T(1024)S(1)}) custom-call(bf16[32,8,128]{2,1,0:T(8,128)(2,1)S(1)} %get-tuple-element.17.rounded_ref, s32[8,64]{1,0:T(8,128)} %bitcast.6, s32[8,64]{1,0:T(8,128)} %bitcast.7, s32[1,64]{1,0:T(1,128)} %bitcast.9), custom_call_target="tpu_custom_call" | custom-call | flops 1048576 | bytes 2097152 | tf_op jit(solution)/shard_map/locate/pallas_call | solution.py:364
  10.1 0.0 collective-permute-done
  10.1 2.4 %collective-permute-done.1 = bf16[32,8,128]{2,1,0:T(8,128)(2,1)S(1)} collective-permute-done((bf16[32,8,128]{2,1,0:T(8,128)(2,1)S(1)}, bf16[32,8,128]{2,1,0:T(8,128)(2,1)S(1)}, u32[]{:S(2)}, u32[]{:S(2)}) %collective-permute-start.1) | collective-permute-done | bytes 65568 | tf_op jit(solution)/shard_map/ppermute | solution.py:387
  12.6 2.9 %collective-permute-start.3 = (bf16[128,8,128]{2,1,0:T(8,128)(2,1)S(1)}, bf16[128,8,128]{2,1,0:T(8,128)(2,1)S(1)}, u32[]{:S(2)}, u32[]{:S(2)}) collective-permute-start(bf16[128,8,128]{2,1,0:T(8,128)(2,1)S(1)} %constant_dynamic-update-slice_fusion.gathered_ref.refs_5_), channel_id=1, source_target_pairs={{0,24},{1,7},{2,26},{3,5},{4,28},{5,3},{6,30},{7,1},{8,16},{9,15},... | collective-permute-start | bytes 786440 | tf_op jit(solution)/shard_map/ppermute | solution.py:387
  15.5 0.1 collective-permute-start.4
  15.6 0.5 collective-permute-start.5
  16.2 3.0 %prepare.1 = (bf16[128,8,128]{2,1,0:T(8,128)(2,1)S(1)}, f32[32,8,128]{2,1,0:T(8,128)S(1)}, bf16[32,8,128]{2,1,0:T(8,128)(2,1)S(1)}, bf16[32,128,128]{2,1,0:T(8,128)(2,1)S(1)}, bf16[64,64,512]{2,1,0:T(8,128)(2,1)S(1)}) custom-call(s32[64]{0:T(128)S(1)} %get-tuple-element.16.perm_ref.refs_0_, ...), custom_call_target="tpu_custom_call" | custom-call | flops 67108864 | bytes 10485760 | tf_op jit(solution)/shard_map/prepare/pallas_call | solution.py:409
  19.1 0.1 collective-permute-start.9
  19.2 0.8 %collective-permute-done.3.refs_2_ = bf16[128,8,128]{2,1,0:T(8,128)(2,1)S(1)} collective-permute-done((bf16[128,8,128]{2,1,0:T(8,128)(2,1)S(1)}, bf16[128,8,128]{2,1,0:T(8,128)(2,1)S(1)}, u32[]{:S(2)}, u32[]{:S(2)}) %collective-permute-start.3) | collective-permute-done | bytes 262176 | tf_op jit(solution)/shard_map/ppermute | solution.py:387
  20.0 2.7 %collective-permute-done.4.refs_3_ = bf16[128,8,128]{2,1,0:T(8,128)(2,1)S(1)} collective-permute-done((bf16[128,8,128]{2,1,0:T(8,128)(2,1)S(1)}, bf16[128,8,128]{2,1,0:T(8,128)(2,1)S(1)}, u32[]{:S(2)}, u32[]{:S(2)}) %collective-permute-start.4) | collective-permute-done | bytes 262176 | tf_op jit(solution)/shard_map/ppermute | solution.py:387
  22.7 0.5 collective-permute-done.5.refs_4_
  23.2 0.7 %collective-permute-start.8 = (bf16[128,8,128]{2,1,0:T(8,128)(2,1)S(1)}, bf16[128,8,128]{2,1,0:T(8,128)(2,1)S(1)}, u32[]{:S(2)}, u32[]{:S(2)}) collective-permute-start(bf16[128,8,128]{2,1,0:T(8,128)(2,1)S(1)} %collective-permute-done.5.refs_4_), channel_id=1, source_target_pairs={{0,1},{1,0},{2,3},{3,2},{4,5},{5,4},{6,7},{7,6},{8,9},{9,8},{10,11... | collective-permute-start | bytes 786440 | tf_op jit(solution)/shard_map/ppermute | solution.py:387
  23.9 0.3 collective-permute-done.7.refs_7_
  24.3 0.8 %collective-permute-done.8.refs_8_ = bf16[128,8,128]{2,1,0:T(8,128)(2,1)S(1)} collective-permute-done((bf16[128,8,128]{2,1,0:T(8,128)(2,1)S(1)}, bf16[128,8,128]{2,1,0:T(8,128)(2,1)S(1)}, u32[]{:S(2)}, u32[]{:S(2)}) %collective-permute-start.8) | collective-permute-done | bytes 262176 | tf_op jit(solution)/shard_map/ppermute | solution.py:387
  25.1 2.3 %later_sweep.2 = (f32[32,8,128]{2,1,0:T(8,128)S(1)}, bf16[32,8,128]{2,1,0:T(8,128)(2,1)S(1)}) custom-call(s32[64]{0:T(128)S(1)} %get-tuple-element.16.perm_ref.refs_0_, s32[1024]{0:T(1024)S(1)} %get-tuple-element.18.refs_1_, bf16[128,8,128]{2,1,0:T(8,128)(2,1)S(1)} %collective-permute-done.3.refs_2_, ...), custom_call_target="tpu_custom_call" | custom-call | tf_op jit(solution)/shard_map/later_sweep/pallas_call | solution.py:438
  27.4 2.5 %collective-permute-start.10 = (bf16[32,8,128]{2,1,0:T(8,128)(2,1)S(1)}, bf16[32,8,128]{2,1,0:T(8,128)(2,1)S(1)}, u32[]{:S(2)}, u32[]{:S(2)}) collective-permute-start(bf16[32,8,128]{2,1,0:T(8,128)(2,1)S(1)} %get-tuple-element.25), channel_id=1, source_target_pairs={{0,6},{1,25},{2,4},{3,27},{4,2},{5,29},{6,0},{7,31},{8,14},{9,17},... | collective-permute-start | bytes 196616 | tf_op jit(solution)/shard_map/ppermute | solution.py:387
  29.9 2.0 %collective-permute-start.12 = (bf16[32,8,128]{2,1,0:T(8,128)(2,1)S(1)}, bf16[32,8,128]{2,1,0:T(8,128)(2,1)S(1)}, u32[]{:S(2)}, u32[]{:S(2)}) collective-permute-start(bf16[32,8,128]{2,1,0:T(8,128)(2,1)S(1)} %get-tuple-element.25), channel_id=1, source_target_pairs={{0,2},{1,17},{2,0},{3,19},{4,6},{5,21},{6,4},{7,23},{8,10},{9,25},... | collective-permute-start | bytes 196616 | tf_op jit(solution)/shard_map/ppermute | solution.py:387
  31.9 1.7 %collective-permute-done.10 = bf16[32,8,128]{2,1,0:T(8,128)(2,1)S(1)} collective-permute-done((bf16[32,8,128]{2,1,0:T(8,128)(2,1)S(1)}, bf16[32,8,128]{2,1,0:T(8,128)(2,1)S(1)}, u32[]{:S(2)}, u32[]{:S(2)}) %collective-permute-start.10) | collective-permute-done | bytes 65568 | tf_op jit(solution)/shard_map/ppermute | solution.py:387
  33.6 1.8 %collective-permute-done.11 = bf16[32,8,128]{2,1,0:T(8,128)(2,1)S(1)} collective-permute-done((bf16[32,8,128]{2,1,0:T(8,128)(2,1)S(1)}, bf16[32,8,128]{2,1,0:T(8,128)(2,1)S(1)}, u32[]{:S(2)}, u32[]{:S(2)}) %collective-permute-start.11) | collective-permute-done | bytes 65568 | tf_op jit(solution)/shard_map/ppermute | solution.py:387
  35.4 2.0 %collective-permute-start.13 = (bf16[128,8,128]{2,1,0:T(8,128)(2,1)S(1)}, bf16[128,8,128]{2,1,0:T(8,128)(2,1)S(1)}, u32[]{:S(2)}, u32[]{:S(2)}) collective-permute-start(bf16[128,8,128]{2,1,0:T(8,128)(2,1)S(1)} %constant_dynamic-update-slice_fusion.4.refs_5_), channel_id=1, source_target_pairs={{0,24},{1,7},{2,26},{3,5},{4,28},{5,3},{6,30},{7,1},{8,16},{9,15},... | collective-permute-start | bytes 786440 | tf_op jit(solution)/shard_map/ppermute | solution.py:387
  37.4 1.1 %collective-permute-start.14 = (bf16[128,8,128]{2,1,0:T(8,128)(2,1)S(1)}, bf16[128,8,128]{2,1,0:T(8,128)(2,1)S(1)}, u32[]{:S(2)}, u32[]{:S(2)}) collective-permute-start(bf16[128,8,128]{2,1,0:T(8,128)(2,1)S(1)} %constant_dynamic-update-slice_fusion.4.refs_5_), channel_id=1, source_target_pairs={{0,16},{1,3},{2,18},{3,1},{4,20},{5,7},{6,22},{7,5},{8,24},{9,11},... | collective-permute-start | bytes 786440 | tf_op jit(solution)/shard_map/ppermute | solution.py:387
  38.4 0.5 collective-permute-start.15
  39.0 3.9 %collective-permute-done.13.refs_2_ = bf16[128,8,128]{2,1,0:T(8,128)(2,1)S(1)} collective-permute-done((bf16[128,8,128]{2,1,0:T(8,128)(2,1)S(1)}, bf16[128,8,128]{2,1,0:T(8,128)(2,1)S(1)}, u32[]{:S(2)}, u32[]{:S(2)}) %collective-permute-start.13) | collective-permute-done | bytes 262176 | tf_op jit(solution)/shard_map/ppermute | solution.py:387
  42.8 2.7 %collective-permute-done.14.refs_3_ = bf16[128,8,128]{2,1,0:T(8,128)(2,1)S(1)} collective-permute-done((bf16[128,8,128]{2,1,0:T(8,128)(2,1)S(1)}, bf16[128,8,128]{2,1,0:T(8,128)(2,1)S(1)}, u32[]{:S(2)}, u32[]{:S(2)}) %collective-permute-start.14) | collective-permute-done | bytes 262176 | tf_op jit(solution)/shard_map/ppermute | solution.py:387
  45.5 2.2 %collective-permute-start.18 = (bf16[128,8,128]{2,1,0:T(8,128)(2,1)S(1)}, bf16[128,8,128]{2,1,0:T(8,128)(2,1)S(1)}, u32[]{:S(2)}, u32[]{:S(2)}) collective-permute-start(bf16[128,8,128]{2,1,0:T(8,128)(2,1)S(1)} %collective-permute-done.15.refs_4_), channel_id=1, source_target_pairs={{0,1},{1,0},{2,3},{3,2},{4,5},{5,4},{6,7},{7,6},{8,9},{9,8},{10,11... | collective-permute-start | bytes 786440 | tf_op jit(solution)/shard_map/ppermute | solution.py:387
  47.8 1.1 %collective-permute-done.18.refs_8_ = bf16[128,8,128]{2,1,0:T(8,128)(2,1)S(1)} collective-permute-done((bf16[128,8,128]{2,1,0:T(8,128)(2,1)S(1)}, bf16[128,8,128]{2,1,0:T(8,128)(2,1)S(1)}, u32[]{:S(2)}, u32[]{:S(2)}) %collective-permute-start.18) | collective-permute-done | bytes 262176 | tf_op jit(solution)/shard_map/ppermute | solution.py:387
  48.9 2.4 %later_sweep.3 = f32[32,8,128]{2,1,0:T(8,128)S(1)} custom-call(s32[64]{0:T(128)S(1)} %get-tuple-element.16.perm_ref.refs_0_, s32[1024]{0:T(1024)S(1)} %get-tuple-element.18.refs_1_, bf16[128,8,128]{2,1,0:T(8,128)(2,1)S(1)} %collective-permute-done.13.refs_2_, bf16[128,8,128]{2,1,0:T(8,128)(2,1)S(1)} %collective-permute-done.14.refs_3_, ...), custom_call_target="tpu_custom_call" | custom-call | tf_op jit(solution)/shard_map/later_sweep/pallas_call | solution.py:438
  51.3 11.3 %all_to_all.5 = f32[32,8,128]{2,1,0:T(8,128)S(1)} all-to-all(f32[32,8,128]{2,1,0:T(8,128)S(1)} %later_sweep.3), channel_id=1, replica_groups=mesh['grp'=4,'row'=8] {'grp','row'}, dimensions={0} | all-to-all | bytes 262144 | tf_op jit(solution)/shard_map/all_to_all | solution.py:465
  62.6 0.7 %lay_out.1 = f32[64,512]{1,0:T(8,128)} custom-call(f32[256,128]{1,0:T(8,128)S(1)} %bitcast.5), custom_call_target="tpu_custom_call" | custom-call | tf_op jit(solution)/shard_map/lay_out/pallas_call | solution.py:466
  (23 shorter events, 0.1 us)
Async XLA Ops:
  2.2 7.9 %collective-permute-start = (bf16[32,8,128]{2,1,0:T(8,128)(2,1)S(1)}, bf16[32,8,128]{2,1,0:T(8,128)(2,1)S(1)}, u32[]{:S(2)}, u32[]{:S(2)}) collective-permute-start(bf16[32,8,128]{2,1,0:T(8,128)(2,1)S(1)} %get-tuple-element.17.rounded_ref), channel_id=1, source_target_pairs={{0,6},{1,25},{2,4},{3,27},{4,2},{5,29},{6,0},{7,31},{8,14},{9,17},... | collective-permute-start | bytes 196616 | tf_op jit(solution)/shard_map/ppermute | solution.py:387
  7.4 5.2 %collective-permute-start.1 = (bf16[32,8,128]{2,1,0:T(8,128)(2,1)S(1)}, bf16[32,8,128]{2,1,0:T(8,128)(2,1)S(1)}, u32[]{:S(2)}, u32[]{:S(2)}) collective-permute-start(bf16[32,8,128]{2,1,0:T(8,128)(2,1)S(1)} %get-tuple-element.17.rounded_ref), channel_id=1, source_target_pairs={{0,4},{1,9},{2,6},{3,11},{4,0},{5,13},{6,2},{7,15},{8,12},{9,1},{1... | collective-permute-start | bytes 196616 | tf_op jit(solution)/shard_map/ppermute | solution.py:387
  7.4 5.2 %collective-permute-start.2 = (bf16[32,8,128]{2,1,0:T(8,128)(2,1)S(1)}, bf16[32,8,128]{2,1,0:T(8,128)(2,1)S(1)}, u32[]{:S(2)}, u32[]{:S(2)}) collective-permute-start(bf16[32,8,128]{2,1,0:T(8,128)(2,1)S(1)} %get-tuple-element.17.rounded_ref), channel_id=1, source_target_pairs={{0,2},{1,17},{2,0},{3,19},{4,6},{5,21},{6,4},{7,23},{8,10},{9,25},... | collective-permute-start | bytes 196616 | tf_op jit(solution)/shard_map/ppermute | solution.py:387
  12.6 7.4 %collective-permute-start.3 = (bf16[128,8,128]{2,1,0:T(8,128)(2,1)S(1)}, bf16[128,8,128]{2,1,0:T(8,128)(2,1)S(1)}, u32[]{:S(2)}, u32[]{:S(2)}) collective-permute-start(bf16[128,8,128]{2,1,0:T(8,128)(2,1)S(1)} %constant_dynamic-update-slice_fusion.gathered_ref.refs_5_), channel_id=1, source_target_pairs={{0,24},{1,7},{2,26},{3,5},{4,28},{5,3},{6,30},{7,1},{8,16},{9,15},... | collective-permute-start | bytes 786440 | tf_op jit(solution)/shard_map/ppermute | solution.py:387
  15.5 7.2 %collective-permute-start.4 = (bf16[128,8,128]{2,1,0:T(8,128)(2,1)S(1)}, bf16[128,8,128]{2,1,0:T(8,128)(2,1)S(1)}, u32[]{:S(2)}, u32[]{:S(2)}) collective-permute-start(bf16[128,8,128]{2,1,0:T(8,128)(2,1)S(1)} %constant_dynamic-update-slice_fusion.gathered_ref.refs_5_), channel_id=1, source_target_pairs={{0,16},{1,3},{2,18},{3,1},{4,20},{5,7},{6,22},{7,5},{8,24},{9,11},... | collective-permute-start | bytes 786440 | tf_op jit(solution)/shard_map/ppermute | solution.py:387
  15.6 7.6 %collective-permute-start.5 = (bf16[128,8,128]{2,1,0:T(8,128)(2,1)S(1)}, bf16[128,8,128]{2,1,0:T(8,128)(2,1)S(1)}, u32[]{:S(2)}, u32[]{:S(2)}) collective-permute-start(bf16[128,8,128]{2,1,0:T(8,128)(2,1)S(1)} %constant_dynamic-update-slice_fusion.gathered_ref.refs_5_), channel_id=1, source_target_pairs={{0,8},{1,5},{2,10},{3,7},{4,12},{5,1},{6,14},{7,3},{8,0},{9,13},{1... | collective-permute-start | bytes 786440 | tf_op jit(solution)/shard_map/ppermute | solution.py:387
  19.1 4.8 %collective-permute-start.9 = (bf16[128,8,128]{2,1,0:T(8,128)(2,1)S(1)}, bf16[128,8,128]{2,1,0:T(8,128)(2,1)S(1)}, u32[]{:S(2)}, u32[]{:S(2)}) collective-permute-start(bf16[128,8,128]{2,1,0:T(8,128)(2,1)S(1)} %get-tuple-element.20), channel_id=1, source_target_pairs={{0,1},{1,0},{2,3},{3,2},{4,5},{5,4},{6,7},{7,6},{8,9},{9,8},{10,11... | collective-permute-start | bytes 786440 | tf_op jit(solution)/shard_map/ppermute | solution.py:387
  20.0 3.9 %collective-permute-start.6 = (bf16[128,8,128]{2,1,0:T(8,128)(2,1)S(1)}, bf16[128,8,128]{2,1,0:T(8,128)(2,1)S(1)}, u32[]{:S(2)}, u32[]{:S(2)}) collective-permute-start(bf16[128,8,128]{2,1,0:T(8,128)(2,1)S(1)} %collective-permute-done.3.refs_2_), channel_id=1, source_target_pairs={{0,1},{1,0},{2,3},{3,2},{4,5},{5,4},{6,7},{7,6},{8,9},{9,8},{10,11... | collective-permute-start | bytes 786440 | tf_op jit(solution)/shard_map/ppermute | solution.py:387
  22.7 1.5 %collective-permute-start.7 = (bf16[128,8,128]{2,1,0:T(8,128)(2,1)S(1)}, bf16[128,8,128]{2,1,0:T(8,128)(2,1)S(1)}, u32[]{:S(2)}, u32[]{:S(2)}) collective-permute-start(bf16[128,8,128]{2,1,0:T(8,128)(2,1)S(1)} %collective-permute-done.4.refs_3_), channel_id=1, source_target_pairs={{0,1},{1,0},{2,3},{3,2},{4,5},{5,4},{6,7},{7,6},{8,9},{9,8},{10,11... | collective-permute-start | bytes 786440 | tf_op jit(solution)/shard_map/ppermute | solution.py:387
  23.2 1.9 %collective-permute-start.8 = (bf16[128,8,128]{2,1,0:T(8,128)(2,1)S(1)}, bf16[128,8,128]{2,1,0:T(8,128)(2,1)S(1)}, u32[]{:S(2)}, u32[]{:S(2)}) collective-permute-start(bf16[128,8,128]{2,1,0:T(8,128)(2,1)S(1)} %collective-permute-done.5.refs_4_), channel_id=1, source_target_pairs={{0,1},{1,0},{2,3},{3,2},{4,5},{5,4},{6,7},{7,6},{8,9},{9,8},{10,11... | collective-permute-start | bytes 786440 | tf_op jit(solution)/shard_map/ppermute | solution.py:387
  27.4 6.1 %collective-permute-start.10 = (bf16[32,8,128]{2,1,0:T(8,128)(2,1)S(1)}, bf16[32,8,128]{2,1,0:T(8,128)(2,1)S(1)}, u32[]{:S(2)}, u32[]{:S(2)}) collective-permute-start(bf16[32,8,128]{2,1,0:T(8,128)(2,1)S(1)} %get-tuple-element.25), channel_id=1, source_target_pairs={{0,6},{1,25},{2,4},{3,27},{4,2},{5,29},{6,0},{7,31},{8,14},{9,17},... | collective-permute-start | bytes 196616 | tf_op jit(solution)/shard_map/ppermute | solution.py:387
  29.9 5.4 %collective-permute-start.11 = (bf16[32,8,128]{2,1,0:T(8,128)(2,1)S(1)}, bf16[32,8,128]{2,1,0:T(8,128)(2,1)S(1)}, u32[]{:S(2)}, u32[]{:S(2)}) collective-permute-start(bf16[32,8,128]{2,1,0:T(8,128)(2,1)S(1)} %get-tuple-element.25), channel_id=1, source_target_pairs={{0,4},{1,9},{2,6},{3,11},{4,0},{5,13},{6,2},{7,15},{8,12},{9,1},{1... | collective-permute-start | bytes 196616 | tf_op jit(solution)/shard_map/ppermute | solution.py:387
  29.9 5.4 %collective-permute-start.12 = (bf16[32,8,128]{2,1,0:T(8,128)(2,1)S(1)}, bf16[32,8,128]{2,1,0:T(8,128)(2,1)S(1)}, u32[]{:S(2)}, u32[]{:S(2)}) collective-permute-start(bf16[32,8,128]{2,1,0:T(8,128)(2,1)S(1)} %get-tuple-element.25), channel_id=1, source_target_pairs={{0,2},{1,17},{2,0},{3,19},{4,6},{5,21},{6,4},{7,23},{8,10},{9,25},... | collective-permute-start | bytes 196616 | tf_op jit(solution)/shard_map/ppermute | solution.py:387
  35.4 7.4 %collective-permute-start.13 = (bf16[128,8,128]{2,1,0:T(8,128)(2,1)S(1)}, bf16[128,8,128]{2,1,0:T(8,128)(2,1)S(1)}, u32[]{:S(2)}, u32[]{:S(2)}) collective-permute-start(bf16[128,8,128]{2,1,0:T(8,128)(2,1)S(1)} %constant_dynamic-update-slice_fusion.4.refs_5_), channel_id=1, source_target_pairs={{0,24},{1,7},{2,26},{3,5},{4,28},{5,3},{6,30},{7,1},{8,16},{9,15},... | collective-permute-start | bytes 786440 | tf_op jit(solution)/shard_map/ppermute | solution.py:387
  37.4 8.2 %collective-permute-start.14 = (bf16[128,8,128]{2,1,0:T(8,128)(2,1)S(1)}, bf16[128,8,128]{2,1,0:T(8,128)(2,1)S(1)}, u32[]{:S(2)}, u32[]{:S(2)}) collective-permute-start(bf16[128,8,128]{2,1,0:T(8,128)(2,1)S(1)} %constant_dynamic-update-slice_fusion.4.refs_5_), channel_id=1, source_target_pairs={{0,16},{1,3},{2,18},{3,1},{4,20},{5,7},{6,22},{7,5},{8,24},{9,11},... | collective-permute-start | bytes 786440 | tf_op jit(solution)/shard_map/ppermute | solution.py:387
  38.4 7.1 %collective-permute-start.15 = (bf16[128,8,128]{2,1,0:T(8,128)(2,1)S(1)}, bf16[128,8,128]{2,1,0:T(8,128)(2,1)S(1)}, u32[]{:S(2)}, u32[]{:S(2)}) collective-permute-start(bf16[128,8,128]{2,1,0:T(8,128)(2,1)S(1)} %constant_dynamic-update-slice_fusion.4.refs_5_), channel_id=1, source_target_pairs={{0,8},{1,5},{2,10},{3,7},{4,12},{5,1},{6,14},{7,3},{8,0},{9,13},{1... | collective-permute-start | bytes 786440 | tf_op jit(solution)/shard_map/ppermute | solution.py:387
  38.9 8.8 %collective-permute-start.19 = (bf16[128,8,128]{2,1,0:T(8,128)(2,1)S(1)}, bf16[128,8,128]{2,1,0:T(8,128)(2,1)S(1)}, u32[]{:S(2)}, u32[]{:S(2)}) collective-permute-start(bf16[128,8,128]{2,1,0:T(8,128)(2,1)S(1)} %constant_dynamic-update-slice_fusion.4.refs_5_), channel_id=1, source_target_pairs={{0,1},{1,0},{2,3},{3,2},{4,5},{5,4},{6,7},{7,6},{8,9},{9,8},{10,11... | collective-permute-start | bytes 786440 | tf_op jit(solution)/shard_map/ppermute | solution.py:387
  42.8 4.9 %collective-permute-start.16 = (bf16[128,8,128]{2,1,0:T(8,128)(2,1)S(1)}, bf16[128,8,128]{2,1,0:T(8,128)(2,1)S(1)}, u32[]{:S(2)}, u32[]{:S(2)}) collective-permute-start(bf16[128,8,128]{2,1,0:T(8,128)(2,1)S(1)} %collective-permute-done.13.refs_2_), channel_id=1, source_target_pairs={{0,1},{1,0},{2,3},{3,2},{4,5},{5,4},{6,7},{7,6},{8,9},{9,8},{10,11... | collective-permute-start | bytes 786440 | tf_op jit(solution)/shard_map/ppermute | solution.py:387
  45.5 2.2 %collective-permute-start.17 = (bf16[128,8,128]{2,1,0:T(8,128)(2,1)S(1)}, bf16[128,8,128]{2,1,0:T(8,128)(2,1)S(1)}, u32[]{:S(2)}, u32[]{:S(2)}) collective-permute-start(bf16[128,8,128]{2,1,0:T(8,128)(2,1)S(1)} %collective-permute-done.14.refs_3_), channel_id=1, source_target_pairs={{0,1},{1,0},{2,3},{3,2},{4,5},{5,4},{6,7},{7,6},{8,9},{9,8},{10,11... | collective-permute-start | bytes 786440 | tf_op jit(solution)/shard_map/ppermute | solution.py:387
  45.5 3.4 %collective-permute-start.18 = (bf16[128,8,128]{2,1,0:T(8,128)(2,1)S(1)}, bf16[128,8,128]{2,1,0:T(8,128)(2,1)S(1)}, u32[]{:S(2)}, u32[]{:S(2)}) collective-permute-start(bf16[128,8,128]{2,1,0:T(8,128)(2,1)S(1)} %collective-permute-done.15.refs_4_), channel_id=1, source_target_pairs={{0,1},{1,0},{2,3},{3,2},{4,5},{5,4},{6,7},{7,6},{8,9},{9,8},{10,11... | collective-permute-start | bytes 786440 | tf_op jit(solution)/shard_map/ppermute | solution.py:387

commit v7 on v6

--- a/solution.py
+++ b/solution.py
@@ -165,7 +165,7 @@
     count = 1 << len(near)
     even = source % 2 == 0
     piece = count - 1 - jnp.where(even, collect(far), collect(near))
-    within = jnp.where(even, collect(near), collect(far))
+    within = jnp.where(even, collect(near), collect(far[::-1]))
     within = jnp.where(within == 0, count - 1, jnp.where(within == count - 1, 0, within))
     tile = (((relative % 2) * count + piece) * count + within) * pairs + position // 2
     swap = (position + lax.broadcasted_iota(jnp.int32, position.shape, 0)) % 2
@@ -203,6 +203,10 @@
         line.start()
     for line in lines:
         line.wait()
+
+
+def duplicate(value_ref, out_ref):
+    out_ref[...] = value_ref[...]
 
 
 def prepare(
@@ -249,7 +253,7 @@
     copies[2].wait()
 
 
-def later_sweep(piece_count, with_rounded, *refs):
+def later_sweep(plan, piece_count, with_rounded, *refs):
     perm_ref, index_ref = refs[:2]
     pieces = refs[2 : 2 + piece_count]
     blocks, sbd_ref, rp_ref, x_ref = refs[2 + piece_count : 6 + piece_count]
@@ -261,12 +265,9 @@
     rows, block, width = blocks.shape
     bands = width // block
 
-    start = 0
-    for piece in pieces:
-        size = piece.shape[0]
-        tiles[pl.ds(start, size)] = piece[...]
-        start += size
-    tiles[start] = jnp.zeros((NRHS, LANES), jnp.bfloat16)
+    for number, start, size, place in plan:
+        tiles[pl.ds(place * pairs, size * pairs)] = pieces[number][pl.ds(start * pairs, size * pairs)]
+    tiles[tiles.shape[0] - 1] = jnp.zeros((NRHS, LANES), jnp.bfloat16)
 
     lower = lax.broadcasted_iota(jnp.int32, (NRHS, LANES), 1) < block
 
@@ -395,15 +396,42 @@
         return held
 
     even, odd = levels(devices)
+    count = 1 << len(even)
 
     def first_level(value, own):
-        held = direct(value, list(zip(even, odd)))
+        held = direct(value, list(zip(even, odd[::-1])))
         return jnp.concatenate([held[-1]] + held[1:-1] + [own], axis=0)
 
     def second_level(value, own):
         near = direct(value, list(zip(odd, even)))
         near, away = near[::-1], ([own] + near[1:])[::-1]
-        return near + [exchange(part, (1, 1)) for part in away]
+        plan = [(number, 0, count, number * count) for number in range(2 * count)]
+        return plan, near + [exchange(part, (1, 1)) for part in away]
+
+    def both_levels(value):
+        ahead = direct(value, list(zip(even, odd[::-1])))
+        copy = pl.pallas_call(
+            duplicate,
+            out_shape=jax.ShapeDtypeStruct(tile_shape, jnp.bfloat16),
+            in_specs=[vmem],
+            out_specs=vmem,
+            compiler_params=params,
+            name="duplicate",
+        )(value)
+        aside = direct(copy, list(zip(odd, even)))
+        ahead = jnp.concatenate([ahead[-1]] + ahead[1:-1], axis=0)
+        aside = jnp.concatenate([aside[-1]] + aside[1:-1] + [copy], axis=0)
+        near = [aside, ahead] + direct(ahead, list(zip(odd, even)))[:0:-1]
+        plan = []
+        for core in range(2):
+            base, number = core * count * count, core * len(near)
+            for place in range(count):
+                row = {0: 0, count - 1: count - 1}.get(place, count - 1 - place)
+                plan.append((number, place, 1, base + row * count + count - 1))
+            plan.append((number + 1, 0, count - 1, base + (count - 1) * count))
+            for row in range(count - 1):
+                plan.append((number + 2 + row, 0, count - 1, base + row * count))
+        return plan, near + [exchange(part, (1, 1)) for part in near]
 
     gathered = first_level(rounded, own)
     own, x, right, smooth, blocks = pl.pallas_call(
@@ -430,13 +458,12 @@
         name="prepare",
     )(perm, gathered, in_hbm(smoother), in_hbm(residual), in_hbm(coarse_blocks))
 
-    def sweep(x, value, own, last):
-        pieces = second_level(value, own)
+    def sweep(x, plan, pieces, last):
         outs = [jax.ShapeDtypeStruct(tile_shape, jnp.float32)]
         if not last:
             outs.append(jax.ShapeDtypeStruct(tile_shape, jnp.bfloat16))
         return pl.pallas_call(
-            functools.partial(later_sweep, len(pieces), not last),
+            functools.partial(later_sweep, plan, len(pieces), not last),
             out_shape=tuple(outs),
             in_specs=[smem, smem] + [vmem] * (len(pieces) + 4),
             out_specs=tuple([vmem] * len(outs)),
@@ -448,9 +475,8 @@
             name="later_sweep",
         )(perm, index, *pieces, blocks, smooth, right, x)
 
-    x, rounded = sweep(x, gathered, own, False)
-    gathered = first_level(rounded, rounded)
-    (x,) = sweep(x, gathered, gathered, True)
+    x, rounded = sweep(x, *second_level(gathered, own), False)
+    (x,) = sweep(x, *both_levels(rounded), True)
 
     if not full:
         flat = x.reshape(rows, NRHS * block)

time: 63.5 us -> 62.8 us (0.989)
  waiting for transfers between devices: 18.8 us -> 14.9 us
  starting transfers between devices: 20.3 us -> 23 us
    ppermute x20 -> x24, waiting for transfers between devices: 18.8 us -> 14.9 us  [exchange(): return lax.ppermute(value, ('grp', 'row'), pairs_of)]
    ppermute x20 -> x24, starting transfers between devices: 20.3 us -> 23 us  [exchange(): return lax.ppermute(value, ('grp', 'row'), pairs_of)]
    pallas_call x2 -> x3, Pallas kernels: 4.73 us -> 4.73 us  [the longest x2 4.72 us: sweep(): pl.pallas_call(functools.partial(later_sweep, plan, len(pieces), not last...]
  transfers between devices with their start and end apart: 20 -> 24, of which waited for: 11 -> 11; matrix products, arithmetic and copies ran while one was open for 0% -> 0% of each run, Pallas kernels for 8% -> 8%
where the time goes in v7:
time: 62.8 us; the launch traced here: 62.6 us
  starting transfers between devices  23 us (37%)
  waiting for transfers between devices  14.9 us (24%)
  Pallas kernels  12.7 us (20%)
  blocking collectives  11.8 us (19%)
    ppermute x24, starting transfers between devices, exchange(): return lax.ppermute(value, ('grp', 'row'), pairs_of)  23 us
    ppermute x24, waiting for transfers between devices, exchange(): return lax.ppermute(value, ('grp', 'row'), pairs_of)  14.9 us
    all_to_all x1, blocking collectives, local(): lax.all_to_all(x, ('grp', 'row'), split_axis=0, concat_axis=0, tiled=True)  11.8 us
    pallas_call x2, Pallas kernels, sweep(): pl.pallas_call(functools.partial(later_sweep, plan, len(pieces), not last...  4.72 us
    pallas_call x1, Pallas kernels, local(): pl.pallas_call(prepare, out_shape=(jax.ShapeDtypeStruct(gathered.shape, j...  2.95 us
    pallas_call x1, Pallas kernels, local(): pl.pallas_call(functools.partial(first_sweep, full), out_shape=(jax.Shape...  2.24 us
    pallas_call x1, Pallas kernels, local(): pl.pallas_call(functools.partial(locate, full, devices, members), out_sha...  2.09 us
  transfers between devices with their start and end apart: 24, of which 11 were waited for; matrix products, arithmetic and copies ran while one was open for 0% of the time, Pallas kernels for 8%

profile of v7, /device:TPU:0, one launch (start us, length us, event | category | flops | bytes accessed | tf_op | source)
XLA Modules:
  0.0 62.6 jit_solution(13222770534283517479)
XLA Ops:
  0.0 2.2 %first_sweep.1 = (s32[64]{0:T(128)S(1)}, s32[32]{0:T(128)}, bf16[32,8,128]{2,1,0:T(8,128)(2,1)S(1)}) custom-call(s32[64]{0:T(128)} %bitcast.8, bf16[64,4096]{1,0:T(8,128)(2,1)} %smooth_hbm.3, bf16[64,512]{1,0:T(8,128)(2,1)} %right_hbm.3), custom_call_target="tpu_custom_call" | custom-call | tf_op jit(solution)/shard_map/first_sweep/pallas_call | solution.py:335
  2.2 5.1 %collective-permute-start = (bf16[32,8,128]{2,1,0:T(8,128)(2,1)S(1)}, bf16[32,8,128]{2,1,0:T(8,128)(2,1)S(1)}, u32[]{:S(2)}, u32[]{:S(2)}) collective-permute-start(bf16[32,8,128]{2,1,0:T(8,128)(2,1)S(1)} %get-tuple-element.17.rounded_ref), channel_id=1, source_target_pairs={{0,6},{1,25},{2,4},{3,27},{4,2},{5,29},{6,0},{7,31},{8,14},{9,17},... | collective-permute-start | bytes 196616 | tf_op jit(solution)/shard_map/ppermute | solution.py:388
  7.4 0.6 %collective-permute-start.2 = (bf16[32,8,128]{2,1,0:T(8,128)(2,1)S(1)}, bf16[32,8,128]{2,1,0:T(8,128)(2,1)S(1)}, u32[]{:S(2)}, u32[]{:S(2)}) collective-permute-start(bf16[32,8,128]{2,1,0:T(8,128)(2,1)S(1)} %get-tuple-element.17.rounded_ref), channel_id=1, source_target_pairs={{0,2},{1,9},{2,0},{3,11},{4,6},{5,13},{6,4},{7,15},{8,10},{9,1},{1... | collective-permute-start | bytes 196616 | tf_op jit(solution)/shard_map/ppermute | solution.py:388
  8.0 2.1 %locate.1 = (bf16[32,8,128]{2,1,0:T(8,128)(2,1)S(1)}, s32[1024]{0:T(1024)S(1)}) custom-call(bf16[32,8,128]{2,1,0:T(8,128)(2,1)S(1)} %get-tuple-element.17.rounded_ref, s32[8,64]{1,0:T(8,128)} %bitcast.6, s32[8,64]{1,0:T(8,128)} %bitcast.7, s32[1,64]{1,0:T(1,128)} %bitcast.9), custom_call_target="tpu_custom_call" | custom-call | flops 1048576 | bytes 2097152 | tf_op jit(solution)/shard_map/locate/pallas_call | solution.py:365
  10.1 2.4 %collective-permute-done.1 = bf16[32,8,128]{2,1,0:T(8,128)(2,1)S(1)} collective-permute-done((bf16[32,8,128]{2,1,0:T(8,128)(2,1)S(1)}, bf16[32,8,128]{2,1,0:T(8,128)(2,1)S(1)}, u32[]{:S(2)}, u32[]{:S(2)}) %collective-permute-start.1) | collective-permute-done | bytes 65568 | tf_op jit(solution)/shard_map/ppermute | solution.py:388
  12.6 2.9 %collective-permute-start.3 = (bf16[128,8,128]{2,1,0:T(8,128)(2,1)S(1)}, bf16[128,8,128]{2,1,0:T(8,128)(2,1)S(1)}, u32[]{:S(2)}, u32[]{:S(2)}) collective-permute-start(bf16[128,8,128]{2,1,0:T(8,128)(2,1)S(1)} %constant_dynamic-update-slice_fusion.gathered_ref.refs_5_), channel_id=1, source_target_pairs={{0,24},{1,7},{2,26},{3,5},{4,28},{5,3},{6,30},{7,1},{8,16},{9,15},... | collective-permute-start | bytes 786440 | tf_op jit(solution)/shard_map/ppermute | solution.py:388
  15.5 0.5 collective-permute-start.4
  16.2 3.0 %prepare.1 = (bf16[128,8,128]{2,1,0:T(8,128)(2,1)S(1)}, f32[32,8,128]{2,1,0:T(8,128)S(1)}, bf16[32,8,128]{2,1,0:T(8,128)(2,1)S(1)}, bf16[32,128,128]{2,1,0:T(8,128)(2,1)S(1)}, bf16[64,64,512]{2,1,0:T(8,128)(2,1)S(1)}) custom-call(s32[64]{0:T(128)S(1)} %get-tuple-element.16.perm_ref.refs_0_, ...), custom_call_target="tpu_custom_call" | custom-call | flops 67108864 | bytes 10485760 | tf_op jit(solution)/shard_map/prepare/pallas_call | solution.py:437
  19.2 0.8 %collective-permute-done.3.refs_2_ = bf16[128,8,128]{2,1,0:T(8,128)(2,1)S(1)} collective-permute-done((bf16[128,8,128]{2,1,0:T(8,128)(2,1)S(1)}, bf16[128,8,128]{2,1,0:T(8,128)(2,1)S(1)}, u32[]{:S(2)}, u32[]{:S(2)}) %collective-permute-start.3) | collective-permute-done | bytes 262176 | tf_op jit(solution)/shard_map/ppermute | solution.py:388
  20.0 2.7 %collective-permute-done.4.refs_3_ = bf16[128,8,128]{2,1,0:T(8,128)(2,1)S(1)} collective-permute-done((bf16[128,8,128]{2,1,0:T(8,128)(2,1)S(1)}, bf16[128,8,128]{2,1,0:T(8,128)(2,1)S(1)}, u32[]{:S(2)}, u32[]{:S(2)}) %collective-permute-start.4) | collective-permute-done | bytes 262176 | tf_op jit(solution)/shard_map/ppermute | solution.py:388
  22.8 1.1 %collective-permute-start.8 = (bf16[128,8,128]{2,1,0:T(8,128)(2,1)S(1)}, bf16[128,8,128]{2,1,0:T(8,128)(2,1)S(1)}, u32[]{:S(2)}, u32[]{:S(2)}) collective-permute-start(bf16[128,8,128]{2,1,0:T(8,128)(2,1)S(1)} %collective-permute-done.5.refs_4_), channel_id=1, source_target_pairs={{0,1},{1,0},{2,3},{3,2},{4,5},{5,4},{6,7},{7,6},{8,9},{9,8},{10,11... | collective-permute-start | bytes 786440 | tf_op jit(solution)/shard_map/ppermute | solution.py:388
  23.9 0.4 collective-permute-done.7.refs_7_
  24.3 0.8 %collective-permute-done.8.refs_8_ = bf16[128,8,128]{2,1,0:T(8,128)(2,1)S(1)} collective-permute-done((bf16[128,8,128]{2,1,0:T(8,128)(2,1)S(1)}, bf16[128,8,128]{2,1,0:T(8,128)(2,1)S(1)}, u32[]{:S(2)}, u32[]{:S(2)}) %collective-permute-start.8) | collective-permute-done | bytes 262176 | tf_op jit(solution)/shard_map/ppermute | solution.py:388
  25.1 2.3 %later_sweep.2 = (f32[32,8,128]{2,1,0:T(8,128)S(1)}, bf16[32,8,128]{2,1,0:T(8,128)(2,1)S(1)}) custom-call(s32[64]{0:T(128)S(1)} %get-tuple-element.16.perm_ref.refs_0_, s32[1024]{0:T(1024)S(1)} %get-tuple-element.18.refs_1_, bf16[128,8,128]{2,1,0:T(8,128)(2,1)S(1)} %collective-permute-done.3.refs_2_, ...), custom_call_target="tpu_custom_call" | custom-call | tf_op jit(solution)/shard_map/later_sweep/pallas_call | solution.py:465
  27.4 2.5 %collective-permute-start.13 = (bf16[32,8,128]{2,1,0:T(8,128)(2,1)S(1)}, bf16[32,8,128]{2,1,0:T(8,128)(2,1)S(1)}, u32[]{:S(2)}, u32[]{:S(2)}) collective-permute-start(bf16[32,8,128]{2,1,0:T(8,128)(2,1)S(1)} %get-tuple-element.25.value_ref), channel_id=1, source_target_pairs={{0,6},{1,25},{2,4},{3,27},{4,2},{5,29},{6,0},{7,31},{8,14},{9,17},... | collective-permute-start | bytes 196616 | tf_op jit(solution)/shard_map/ppermute | solution.py:388
  29.9 2.0 %collective-permute-start.15 = (bf16[32,8,128]{2,1,0:T(8,128)(2,1)S(1)}, bf16[32,8,128]{2,1,0:T(8,128)(2,1)S(1)}, u32[]{:S(2)}, u32[]{:S(2)}) collective-permute-start(bf16[32,8,128]{2,1,0:T(8,128)(2,1)S(1)} %get-tuple-element.25.value_ref), channel_id=1, source_target_pairs={{0,2},{1,9},{2,0},{3,11},{4,6},{5,13},{6,4},{7,15},{8,10},{9,1},{1... | collective-permute-start | bytes 196616 | tf_op jit(solution)/shard_map/ppermute | solution.py:388
  31.9 2.2 %collective-permute-start.10 = (bf16[32,8,128]{2,1,0:T(8,128)(2,1)S(1)}, bf16[32,8,128]{2,1,0:T(8,128)(2,1)S(1)}, u32[]{:S(2)}, u32[]{:S(2)}) collective-permute-start(bf16[32,8,128]{2,1,0:T(8,128)(2,1)S(1)} %duplicate.1), channel_id=1, source_target_pairs={{0,24},{1,7},{2,26},{3,5},{4,28},{5,3},{6,30},{7,1},{8,16},{9,15},... | collective-permute-start | bytes 196616 | tf_op jit(solution)/shard_map/ppermute | solution.py:388
  34.0 0.8 %collective-permute-start.11 = (bf16[32,8,128]{2,1,0:T(8,128)(2,1)S(1)}, bf16[32,8,128]{2,1,0:T(8,128)(2,1)S(1)}, u32[]{:S(2)}, u32[]{:S(2)}) collective-permute-start(bf16[32,8,128]{2,1,0:T(8,128)(2,1)S(1)} %duplicate.1), channel_id=1, source_target_pairs={{0,8},{1,5},{2,10},{3,7},{4,12},{5,1},{6,14},{7,3},{8,0},{9,13},{1... | collective-permute-start | bytes 196616 | tf_op jit(solution)/shard_map/ppermute | solution.py:388
  34.8 0.5 collective-permute-start.12
  35.4 1.9 %collective-permute-done.14 = bf16[32,8,128]{2,1,0:T(8,128)(2,1)S(1)} collective-permute-done((bf16[32,8,128]{2,1,0:T(8,128)(2,1)S(1)}, bf16[32,8,128]{2,1,0:T(8,128)(2,1)S(1)}, u32[]{:S(2)}, u32[]{:S(2)}) %collective-permute-start.14) | collective-permute-done | bytes 65568 | tf_op jit(solution)/shard_map/ppermute | solution.py:388
  37.3 2.1 %collective-permute-start.16 = (bf16[96,8,128]{2,1,0:T(8,128)(2,1)S(1)}, bf16[96,8,128]{2,1,0:T(8,128)(2,1)S(1)}, u32[]{:S(2)}, u32[]{:S(2)}) collective-permute-start(bf16[96,8,128]{2,1,0:T(8,128)(2,1)S(1)} %constant_dynamic-update-slice_fusion.4.refs_3_), channel_id=1, source_target_pairs={{0,24},{1,7},{2,26},{3,5},{4,28},{5,3},{6,30},{7,1},{8,16},{9,15},... | collective-permute-start | bytes 589832 | tf_op jit(solution)/shard_map/ppermute | solution.py:388
  39.5 0.8 %collective-permute-start.17 = (bf16[96,8,128]{2,1,0:T(8,128)(2,1)S(1)}, bf16[96,8,128]{2,1,0:T(8,128)(2,1)S(1)}, u32[]{:S(2)}, u32[]{:S(2)}) collective-permute-start(bf16[96,8,128]{2,1,0:T(8,128)(2,1)S(1)} %constant_dynamic-update-slice_fusion.4.refs_3_), channel_id=1, source_target_pairs={{0,16},{1,3},{2,18},{3,1},{4,20},{5,7},{6,22},{7,5},{8,24},{9,11},... | collective-permute-start | bytes 589832 | tf_op jit(solution)/shard_map/ppermute | solution.py:388
  40.3 0.6 collective-permute-start.18
  41.0 0.5 collective-permute-start.20
  41.5 2.6 %collective-permute-done.16.refs_4_ = bf16[96,8,128]{2,1,0:T(8,128)(2,1)S(1)} collective-permute-done((bf16[96,8,128]{2,1,0:T(8,128)(2,1)S(1)}, bf16[96,8,128]{2,1,0:T(8,128)(2,1)S(1)}, u32[]{:S(2)}, u32[]{:S(2)}) %collective-permute-start.16) | collective-permute-done | bytes 196640 | tf_op jit(solution)/shard_map/ppermute | solution.py:388
  44.1 2.0 %collective-permute-done.17.refs_5_ = bf16[96,8,128]{2,1,0:T(8,128)(2,1)S(1)} collective-permute-done((bf16[96,8,128]{2,1,0:T(8,128)(2,1)S(1)}, bf16[96,8,128]{2,1,0:T(8,128)(2,1)S(1)}, u32[]{:S(2)}, u32[]{:S(2)}) %collective-permute-start.17) | collective-permute-done | bytes 196640 | tf_op jit(solution)/shard_map/ppermute | solution.py:388
  46.1 0.5 collective-permute-start.23
  46.6 0.9 %collective-permute-done.22.refs_10_ = bf16[96,8,128]{2,1,0:T(8,128)(2,1)S(1)} collective-permute-done((bf16[96,8,128]{2,1,0:T(8,128)(2,1)S(1)}, bf16[96,8,128]{2,1,0:T(8,128)(2,1)S(1)}, u32[]{:S(2)}, u32[]{:S(2)}) %collective-permute-start.22) | collective-permute-done | bytes 196640 | tf_op jit(solution)/shard_map/ppermute | solution.py:388
  47.5 0.3 collective-permute-done.23.refs_11_
  47.8 2.4 %later_sweep.3 = f32[32,8,128]{2,1,0:T(8,128)S(1)} custom-call(s32[64]{0:T(128)S(1)} %get-tuple-element.16.perm_ref.refs_0_, s32[1024]{0:T(1024)S(1)} %get-tuple-element.18.refs_1_, bf16[128,8,128]{2,1,0:T(8,128)(2,1)S(1)} %pad_maximum_fusion.refs_2_, bf16[96,8,128]{2,1,0:T(8,128)(2,1)S(1)} %constant_dynamic-update-slice_fusion.4.refs_3_, ...), custom_call_target="tpu_custom_call" | custom-call | tf_op jit(solution)/shard_map/later_sweep/pallas_call | solution.py:465
  50.2 11.8 %all_to_all.5 = f32[32,8,128]{2,1,0:T(8,128)S(1)} all-to-all(f32[32,8,128]{2,1,0:T(8,128)S(1)} %later_sweep.3), channel_id=1, replica_groups=mesh['grp'=4,'row'=8] {'grp','row'}, dimensions={0} | all-to-all | bytes 262144 | tf_op jit(solution)/shard_map/all_to_all | solution.py:491
  62.0 0.7 %lay_out.1 = f32[64,512]{1,0:T(8,128)} custom-call(f32[256,128]{1,0:T(8,128)S(1)} %bitcast.5), custom_call_target="tpu_custom_call" | custom-call | tf_op jit(solution)/shard_map/lay_out/pallas_call | solution.py:492
  (32 shorter events, 0.6 us)
Async XLA Ops:
  2.2 7.9 %collective-permute-start = (bf16[32,8,128]{2,1,0:T(8,128)(2,1)S(1)}, bf16[32,8,128]{2,1,0:T(8,128)(2,1)S(1)}, u32[]{:S(2)}, u32[]{:S(2)}) collective-permute-start(bf16[32,8,128]{2,1,0:T(8,128)(2,1)S(1)} %get-tuple-element.17.rounded_ref), channel_id=1, source_target_pairs={{0,6},{1,25},{2,4},{3,27},{4,2},{5,29},{6,0},{7,31},{8,14},{9,17},... | collective-permute-start | bytes 196616 | tf_op jit(solution)/shard_map/ppermute | solution.py:388
  7.4 5.2 %collective-permute-start.1 = (bf16[32,8,128]{2,1,0:T(8,128)(2,1)S(1)}, bf16[32,8,128]{2,1,0:T(8,128)(2,1)S(1)}, u32[]{:S(2)}, u32[]{:S(2)}) collective-permute-start(bf16[32,8,128]{2,1,0:T(8,128)(2,1)S(1)} %get-tuple-element.17.rounded_ref), channel_id=1, source_target_pairs={{0,4},{1,17},{2,6},{3,19},{4,0},{5,21},{6,2},{7,23},{8,12},{9,25},... | collective-permute-start | bytes 196616 | tf_op jit(solution)/shard_map/ppermute | solution.py:388
  7.4 5.2 %collective-permute-start.2 = (bf16[32,8,128]{2,1,0:T(8,128)(2,1)S(1)}, bf16[32,8,128]{2,1,0:T(8,128)(2,1)S(1)}, u32[]{:S(2)}, u32[]{:S(2)}) collective-permute-start(bf16[32,8,128]{2,1,0:T(8,128)(2,1)S(1)} %get-tuple-element.17.rounded_ref), channel_id=1, source_target_pairs={{0,2},{1,9},{2,0},{3,11},{4,6},{5,13},{6,4},{7,15},{8,10},{9,1},{1... | collective-permute-start | bytes 196616 | tf_op jit(solution)/shard_map/ppermute | solution.py:388
  12.6 7.4 %collective-permute-start.3 = (bf16[128,8,128]{2,1,0:T(8,128)(2,1)S(1)}, bf16[128,8,128]{2,1,0:T(8,128)(2,1)S(1)}, u32[]{:S(2)}, u32[]{:S(2)}) collective-permute-start(bf16[128,8,128]{2,1,0:T(8,128)(2,1)S(1)} %constant_dynamic-update-slice_fusion.gathered_ref.refs_5_), channel_id=1, source_target_pairs={{0,24},{1,7},{2,26},{3,5},{4,28},{5,3},{6,30},{7,1},{8,16},{9,15},... | collective-permute-start | bytes 786440 | tf_op jit(solution)/shard_map/ppermute | solution.py:388
  15.5 7.2 %collective-permute-start.4 = (bf16[128,8,128]{2,1,0:T(8,128)(2,1)S(1)}, bf16[128,8,128]{2,1,0:T(8,128)(2,1)S(1)}, u32[]{:S(2)}, u32[]{:S(2)}) collective-permute-start(bf16[128,8,128]{2,1,0:T(8,128)(2,1)S(1)} %constant_dynamic-update-slice_fusion.gathered_ref.refs_5_), channel_id=1, source_target_pairs={{0,16},{1,3},{2,18},{3,1},{4,20},{5,7},{6,22},{7,5},{8,24},{9,11},... | collective-permute-start | bytes 786440 | tf_op jit(solution)/shard_map/ppermute | solution.py:388
  16.0 6.8 %collective-permute-start.5 = (bf16[128,8,128]{2,1,0:T(8,128)(2,1)S(1)}, bf16[128,8,128]{2,1,0:T(8,128)(2,1)S(1)}, u32[]{:S(2)}, u32[]{:S(2)}) collective-permute-start(bf16[128,8,128]{2,1,0:T(8,128)(2,1)S(1)} %constant_dynamic-update-slice_fusion.gathered_ref.refs_5_), channel_id=1, source_target_pairs={{0,8},{1,5},{2,10},{3,7},{4,12},{5,1},{6,14},{7,3},{8,0},{9,13},{1... | collective-permute-start | bytes 786440 | tf_op jit(solution)/shard_map/ppermute | solution.py:388
  19.1 4.8 %collective-permute-start.9 = (bf16[128,8,128]{2,1,0:T(8,128)(2,1)S(1)}, bf16[128,8,128]{2,1,0:T(8,128)(2,1)S(1)}, u32[]{:S(2)}, u32[]{:S(2)}) collective-permute-start(bf16[128,8,128]{2,1,0:T(8,128)(2,1)S(1)} %get-tuple-element.20), channel_id=1, source_target_pairs={{0,1},{1,0},{2,3},{3,2},{4,5},{5,4},{6,7},{7,6},{8,9},{9,8},{10,11... | collective-permute-start | bytes 786440 | tf_op jit(solution)/shard_map/ppermute | solution.py:388
  20.0 3.9 %collective-permute-start.6 = (bf16[128,8,128]{2,1,0:T(8,128)(2,1)S(1)}, bf16[128,8,128]{2,1,0:T(8,128)(2,1)S(1)}, u32[]{:S(2)}, u32[]{:S(2)}) collective-permute-start(bf16[128,8,128]{2,1,0:T(8,128)(2,1)S(1)} %collective-permute-done.3.refs_2_), channel_id=1, source_target_pairs={{0,1},{1,0},{2,3},{3,2},{4,5},{5,4},{6,7},{7,6},{8,9},{9,8},{10,11... | collective-permute-start | bytes 786440 | tf_op jit(solution)/shard_map/ppermute | solution.py:388
  22.7 1.5 %collective-permute-start.7 = (bf16[128,8,128]{2,1,0:T(8,128)(2,1)S(1)}, bf16[128,8,128]{2,1,0:T(8,128)(2,1)S(1)}, u32[]{:S(2)}, u32[]{:S(2)}) collective-permute-start(bf16[128,8,128]{2,1,0:T(8,128)(2,1)S(1)} %collective-permute-done.4.refs_3_), channel_id=1, source_target_pairs={{0,1},{1,0},{2,3},{3,2},{4,5},{5,4},{6,7},{7,6},{8,9},{9,8},{10,11... | collective-permute-start | bytes 786440 | tf_op jit(solution)/shard_map/ppermute | solution.py:388
  22.8 2.2 %collective-permute-start.8 = (bf16[128,8,128]{2,1,0:T(8,128)(2,1)S(1)}, bf16[128,8,128]{2,1,0:T(8,128)(2,1)S(1)}, u32[]{:S(2)}, u32[]{:S(2)}) collective-permute-start(bf16[128,8,128]{2,1,0:T(8,128)(2,1)S(1)} %collective-permute-done.5.refs_4_), channel_id=1, source_target_pairs={{0,1},{1,0},{2,3},{3,2},{4,5},{5,4},{6,7},{7,6},{8,9},{9,8},{10,11... | collective-permute-start | bytes 786440 | tf_op jit(solution)/shard_map/ppermute | solution.py:388
  27.4 7.4 %collective-permute-start.13 = (bf16[32,8,128]{2,1,0:T(8,128)(2,1)S(1)}, bf16[32,8,128]{2,1,0:T(8,128)(2,1)S(1)}, u32[]{:S(2)}, u32[]{:S(2)}) collective-permute-start(bf16[32,8,128]{2,1,0:T(8,128)(2,1)S(1)} %get-tuple-element.25.value_ref), channel_id=1, source_target_pairs={{0,6},{1,25},{2,4},{3,27},{4,2},{5,29},{6,0},{7,31},{8,14},{9,17},... | collective-permute-start | bytes 196616 | tf_op jit(solution)/shard_map/ppermute | solution.py:388
  29.9 7.4 %collective-permute-start.14 = (bf16[32,8,128]{2,1,0:T(8,128)(2,1)S(1)}, bf16[32,8,128]{2,1,0:T(8,128)(2,1)S(1)}, u32[]{:S(2)}, u32[]{:S(2)}) collective-permute-start(bf16[32,8,128]{2,1,0:T(8,128)(2,1)S(1)} %get-tuple-element.25.value_ref), channel_id=1, source_target_pairs={{0,4},{1,17},{2,6},{3,19},{4,0},{5,21},{6,2},{7,23},{8,12},{9,25},... | collective-permute-start | bytes 196616 | tf_op jit(solution)/shard_map/ppermute | solution.py:388
  29.9 7.4 %collective-permute-start.15 = (bf16[32,8,128]{2,1,0:T(8,128)(2,1)S(1)}, bf16[32,8,128]{2,1,0:T(8,128)(2,1)S(1)}, u32[]{:S(2)}, u32[]{:S(2)}) collective-permute-start(bf16[32,8,128]{2,1,0:T(8,128)(2,1)S(1)} %get-tuple-element.25.value_ref), channel_id=1, source_target_pairs={{0,2},{1,9},{2,0},{3,11},{4,6},{5,13},{6,4},{7,15},{8,10},{9,1},{1... | collective-permute-start | bytes 196616 | tf_op jit(solution)/shard_map/ppermute | solution.py:388
  31.9 8.4 %collective-permute-start.10 = (bf16[32,8,128]{2,1,0:T(8,128)(2,1)S(1)}, bf16[32,8,128]{2,1,0:T(8,128)(2,1)S(1)}, u32[]{:S(2)}, u32[]{:S(2)}) collective-permute-start(bf16[32,8,128]{2,1,0:T(8,128)(2,1)S(1)} %duplicate.1), channel_id=1, source_target_pairs={{0,24},{1,7},{2,26},{3,5},{4,28},{5,3},{6,30},{7,1},{8,16},{9,15},... | collective-permute-start | bytes 196616 | tf_op jit(solution)/shard_map/ppermute | solution.py:388
  34.0 6.9 %collective-permute-start.11 = (bf16[32,8,128]{2,1,0:T(8,128)(2,1)S(1)}, bf16[32,8,128]{2,1,0:T(8,128)(2,1)S(1)}, u32[]{:S(2)}, u32[]{:S(2)}) collective-permute-start(bf16[32,8,128]{2,1,0:T(8,128)(2,1)S(1)} %duplicate.1), channel_id=1, source_target_pairs={{0,8},{1,5},{2,10},{3,7},{4,12},{5,1},{6,14},{7,3},{8,0},{9,13},{1... | collective-permute-start | bytes 196616 | tf_op jit(solution)/shard_map/ppermute | solution.py:388
  34.8 6.0 %collective-permute-start.12 = (bf16[32,8,128]{2,1,0:T(8,128)(2,1)S(1)}, bf16[32,8,128]{2,1,0:T(8,128)(2,1)S(1)}, u32[]{:S(2)}, u32[]{:S(2)}) collective-permute-start(bf16[32,8,128]{2,1,0:T(8,128)(2,1)S(1)} %duplicate.1), channel_id=1, source_target_pairs={{0,16},{1,3},{2,18},{3,1},{4,20},{5,7},{6,22},{7,5},{8,24},{9,11},... | collective-permute-start | bytes 196616 | tf_op jit(solution)/shard_map/ppermute | solution.py:388
  37.3 6.7 %collective-permute-start.16 = (bf16[96,8,128]{2,1,0:T(8,128)(2,1)S(1)}, bf16[96,8,128]{2,1,0:T(8,128)(2,1)S(1)}, u32[]{:S(2)}, u32[]{:S(2)}) collective-permute-start(bf16[96,8,128]{2,1,0:T(8,128)(2,1)S(1)} %constant_dynamic-update-slice_fusion.4.refs_3_), channel_id=1, source_target_pairs={{0,24},{1,7},{2,26},{3,5},{4,28},{5,3},{6,30},{7,1},{8,16},{9,15},... | collective-permute-start | bytes 589832 | tf_op jit(solution)/shard_map/ppermute | solution.py:388
  39.5 6.6 %collective-permute-start.17 = (bf16[96,8,128]{2,1,0:T(8,128)(2,1)S(1)}, bf16[96,8,128]{2,1,0:T(8,128)(2,1)S(1)}, u32[]{:S(2)}, u32[]{:S(2)}) collective-permute-start(bf16[96,8,128]{2,1,0:T(8,128)(2,1)S(1)} %constant_dynamic-update-slice_fusion.4.refs_3_), channel_id=1, source_target_pairs={{0,16},{1,3},{2,18},{3,1},{4,20},{5,7},{6,22},{7,5},{8,24},{9,11},... | collective-permute-start | bytes 589832 | tf_op jit(solution)/shard_map/ppermute | solution.py:388
  40.3 5.8 %collective-permute-start.18 = (bf16[96,8,128]{2,1,0:T(8,128)(2,1)S(1)}, bf16[96,8,128]{2,1,0:T(8,128)(2,1)S(1)}, u32[]{:S(2)}, u32[]{:S(2)}) collective-permute-start(bf16[96,8,128]{2,1,0:T(8,128)(2,1)S(1)} %constant_dynamic-update-slice_fusion.4.refs_3_), channel_id=1, source_target_pairs={{0,8},{1,5},{2,10},{3,7},{4,12},{5,1},{6,14},{7,3},{8,0},{9,13},{1... | collective-permute-start | bytes 589832 | tf_op jit(solution)/shard_map/ppermute | solution.py:388
  40.9 5.7 %collective-permute-start.19 = (bf16[128,8,128]{2,1,0:T(8,128)(2,1)S(1)}, bf16[128,8,128]{2,1,0:T(8,128)(2,1)S(1)}, u32[]{:S(2)}, u32[]{:S(2)}) collective-permute-start(bf16[128,8,128]{2,1,0:T(8,128)(2,1)S(1)} %pad_maximum_fusion.refs_2_), channel_id=1, source_target_pairs={{0,1},{1,0},{2,3},{3,2},{4,5},{5,4},{6,7},{7,6},{8,9},{9,8},{10,11... | collective-permute-start | bytes 786440 | tf_op jit(solution)/shard_map/ppermute | solution.py:388
  41.0 5.6 %collective-permute-start.20 = (bf16[96,8,128]{2,1,0:T(8,128)(2,1)S(1)}, bf16[96,8,128]{2,1,0:T(8,128)(2,1)S(1)}, u32[]{:S(2)}, u32[]{:S(2)}) collective-permute-start(bf16[96,8,128]{2,1,0:T(8,128)(2,1)S(1)} %constant_dynamic-update-slice_fusion.4.refs_3_), channel_id=1, source_target_pairs={{0,1},{1,0},{2,3},{3,2},{4,5},{5,4},{6,7},{7,6},{8,9},{9,8},{10,11... | collective-permute-start | bytes 589832 | tf_op jit(solution)/shard_map/ppermute | solution.py:388
  44.1 2.5 %collective-permute-start.21 = (bf16[96,8,128]{2,1,0:T(8,128)(2,1)S(1)}, bf16[96,8,128]{2,1,0:T(8,128)(2,1)S(1)}, u32[]{:S(2)}, u32[]{:S(2)}) collective-permute-start(bf16[96,8,128]{2,1,0:T(8,128)(2,1)S(1)} %collective-permute-done.16.refs_4_), channel_id=1, source_target_pairs={{0,1},{1,0},{2,3},{3,2},{4,5},{5,4},{6,7},{7,6},{8,9},{9,8},{10,11... | collective-permute-start | bytes 589832 | tf_op jit(solution)/shard_map/ppermute | solution.py:388
  46.1 1.4 %collective-permute-start.22 = (bf16[96,8,128]{2,1,0:T(8,128)(2,1)S(1)}, bf16[96,8,128]{2,1,0:T(8,128)(2,1)S(1)}, u32[]{:S(2)}, u32[]{:S(2)}) collective-permute-start(bf16[96,8,128]{2,1,0:T(8,128)(2,1)S(1)} %collective-permute-done.17.refs_5_), channel_id=1, source_target_pairs={{0,1},{1,0},{2,3},{3,2},{4,5},{5,4},{6,7},{7,6},{8,9},{9,8},{10,11... | collective-permute-start | bytes 589832 | tf_op jit(solution)/shard_map/ppermute | solution.py:388
  46.1 1.7 %collective-permute-start.23 = (bf16[96,8,128]{2,1,0:T(8,128)(2,1)S(1)}, bf16[96,8,128]{2,1,0:T(8,128)(2,1)S(1)}, u32[]{:S(2)}, u32[]{:S(2)}) collective-permute-start(bf16[96,8,128]{2,1,0:T(8,128)(2,1)S(1)} %collective-permute-done.18.refs_6_), channel_id=1, source_target_pairs={{0,1},{1,0},{2,3},{3,2},{4,5},{5,4},{6,7},{7,6},{8,9},{9,8},{10,11... | collective-permute-start | bytes 589832 | tf_op jit(solution)/shard_map/ppermute | solution.py:388

commit v8 on v7

--- a/solution.py
+++ b/solution.py
@@ -283,15 +283,15 @@
             jnp.where(lower, fetch(row, 2 * half), fetch(row, 2 * half + 1)) for half in range(bands // 2)
         ]
 
-    for quad in range(rows // 4):
-        members = [perm_ref[4 * quad + member] for member in range(4)]
+    for group in range(rows // 8):
+        members = [perm_ref[8 * group + member] for member in range(8)]
         gathered = jnp.concatenate([jnp.concatenate(values(row), axis=1) for row in members], axis=0)
         weights = jnp.concatenate([blocks[row] for row in members], axis=0)
         applied = lax.dot_general(
             gathered.astype(jnp.bfloat16), weights, TRANSPOSED, preferred_element_type=jnp.float32
         )
-        for half in range(2):
-            pair = 2 * quad + half
+        for half in range(4):
+            pair = 4 * group + half
             own = applied[2 * NRHS * half : 2 * NRHS * (half + 1), LANES * half : LANES * (half + 1)]
             image = jnp.where(lower, own[:NRHS], own[NRHS:])
             defects[pair] = (rp_ref[pair].astype(jnp.float32) - image).astype(jnp.bfloat16)

time: 62.8 us -> 63 us (level)
  no operation moved by 1% of the time
where the time goes in v8:
time: 63 us; the launch traced here: 62.8 us
  starting transfers between devices  23 us (37%)
  waiting for transfers between devices  14.9 us (24%)
  Pallas kernels  12.9 us (20%)
  blocking collectives  11.8 us (19%)
    ppermute x24, starting transfers between devices, exchange(): return lax.ppermute(value, ('grp', 'row'), pairs_of)  23 us
    ppermute x24, waiting for transfers between devices, exchange(): return lax.ppermute(value, ('grp', 'row'), pairs_of)  14.9 us
    all_to_all x1, blocking collectives, local(): lax.all_to_all(x, ('grp', 'row'), split_axis=0, concat_axis=0, tiled=True)  11.8 us
    pallas_call x2, Pallas kernels, sweep(): pl.pallas_call(functools.partial(later_sweep, plan, len(pieces), not last...  4.91 us
    pallas_call x1, Pallas kernels, local(): pl.pallas_call(prepare, out_shape=(jax.ShapeDtypeStruct(gathered.shape, j...  2.95 us
    pallas_call x1, Pallas kernels, local(): pl.pallas_call(functools.partial(first_sweep, full), out_shape=(jax.Shape...  2.24 us
    pallas_call x1, Pallas kernels, local(): pl.pallas_call(functools.partial(locate, full, devices, members), out_sha...  2.09 us
  transfers between devices with their start and end apart: 24, of which 11 were waited for; matrix products, arithmetic and copies ran while one was open for 0% of the time, Pallas kernels for 8%

profile of v8, /device:TPU:0, one launch (start us, length us, event | category | flops | bytes accessed | tf_op | source)
XLA Modules:
  0.0 62.8 jit_solution(12993298563874707918)
XLA Ops:
  0.0 2.2 %first_sweep.1 = (s32[64]{0:T(128)S(1)}, s32[32]{0:T(128)}, bf16[32,8,128]{2,1,0:T(8,128)(2,1)S(1)}) custom-call(s32[64]{0:T(128)} %bitcast.8, bf16[64,4096]{1,0:T(8,128)(2,1)} %smooth_hbm.3, bf16[64,512]{1,0:T(8,128)(2,1)} %right_hbm.3), custom_call_target="tpu_custom_call" | custom-call | tf_op jit(solution)/shard_map/first_sweep/pallas_call | solution.py:335
  2.2 5.1 %collective-permute-start = (bf16[32,8,128]{2,1,0:T(8,128)(2,1)S(1)}, bf16[32,8,128]{2,1,0:T(8,128)(2,1)S(1)}, u32[]{:S(2)}, u32[]{:S(2)}) collective-permute-start(bf16[32,8,128]{2,1,0:T(8,128)(2,1)S(1)} %get-tuple-element.17.rounded_ref), channel_id=1, source_target_pairs={{0,6},{1,25},{2,4},{3,27},{4,2},{5,29},{6,0},{7,31},{8,14},{9,17},... | collective-permute-start | bytes 196616 | tf_op jit(solution)/shard_map/ppermute | solution.py:388
  7.4 0.6 %collective-permute-start.2 = (bf16[32,8,128]{2,1,0:T(8,128)(2,1)S(1)}, bf16[32,8,128]{2,1,0:T(8,128)(2,1)S(1)}, u32[]{:S(2)}, u32[]{:S(2)}) collective-permute-start(bf16[32,8,128]{2,1,0:T(8,128)(2,1)S(1)} %get-tuple-element.17.rounded_ref), channel_id=1, source_target_pairs={{0,2},{1,9},{2,0},{3,11},{4,6},{5,13},{6,4},{7,15},{8,10},{9,1},{1... | collective-permute-start | bytes 196616 | tf_op jit(solution)/shard_map/ppermute | solution.py:388
  8.0 2.1 %locate.1 = (bf16[32,8,128]{2,1,0:T(8,128)(2,1)S(1)}, s32[1024]{0:T(1024)S(1)}) custom-call(bf16[32,8,128]{2,1,0:T(8,128)(2,1)S(1)} %get-tuple-element.17.rounded_ref, s32[8,64]{1,0:T(8,128)} %bitcast.6, s32[8,64]{1,0:T(8,128)} %bitcast.7, s32[1,64]{1,0:T(1,128)} %bitcast.9), custom_call_target="tpu_custom_call" | custom-call | flops 1048576 | bytes 2097152 | tf_op jit(solution)/shard_map/locate/pallas_call | solution.py:365
  10.1 2.4 %collective-permute-done.1 = bf16[32,8,128]{2,1,0:T(8,128)(2,1)S(1)} collective-permute-done((bf16[32,8,128]{2,1,0:T(8,128)(2,1)S(1)}, bf16[32,8,128]{2,1,0:T(8,128)(2,1)S(1)}, u32[]{:S(2)}, u32[]{:S(2)}) %collective-permute-start.1) | collective-permute-done | bytes 65568 | tf_op jit(solution)/shard_map/ppermute | solution.py:388
  12.6 2.9 %collective-permute-start.3 = (bf16[128,8,128]{2,1,0:T(8,128)(2,1)S(1)}, bf16[128,8,128]{2,1,0:T(8,128)(2,1)S(1)}, u32[]{:S(2)}, u32[]{:S(2)}) collective-permute-start(bf16[128,8,128]{2,1,0:T(8,128)(2,1)S(1)} %constant_dynamic-update-slice_fusion.gathered_ref.refs_5_), channel_id=1, source_target_pairs={{0,24},{1,7},{2,26},{3,5},{4,28},{5,3},{6,30},{7,1},{8,16},{9,15},... | collective-permute-start | bytes 786440 | tf_op jit(solution)/shard_map/ppermute | solution.py:388
  15.5 0.5 collective-permute-start.4
  16.2 3.0 %prepare.1 = (bf16[128,8,128]{2,1,0:T(8,128)(2,1)S(1)}, f32[32,8,128]{2,1,0:T(8,128)S(1)}, bf16[32,8,128]{2,1,0:T(8,128)(2,1)S(1)}, bf16[32,128,128]{2,1,0:T(8,128)(2,1)S(1)}, bf16[64,64,512]{2,1,0:T(8,128)(2,1)S(1)}) custom-call(s32[64]{0:T(128)S(1)} %get-tuple-element.16.perm_ref.refs_0_, ...), custom_call_target="tpu_custom_call" | custom-call | flops 67108864 | bytes 10485760 | tf_op jit(solution)/shard_map/prepare/pallas_call | solution.py:437
  19.2 0.8 %collective-permute-done.3.refs_2_ = bf16[128,8,128]{2,1,0:T(8,128)(2,1)S(1)} collective-permute-done((bf16[128,8,128]{2,1,0:T(8,128)(2,1)S(1)}, bf16[128,8,128]{2,1,0:T(8,128)(2,1)S(1)}, u32[]{:S(2)}, u32[]{:S(2)}) %collective-permute-start.3) | collective-permute-done | bytes 262176 | tf_op jit(solution)/shard_map/ppermute | solution.py:388
  20.0 2.7 %collective-permute-done.4.refs_3_ = bf16[128,8,128]{2,1,0:T(8,128)(2,1)S(1)} collective-permute-done((bf16[128,8,128]{2,1,0:T(8,128)(2,1)S(1)}, bf16[128,8,128]{2,1,0:T(8,128)(2,1)S(1)}, u32[]{:S(2)}, u32[]{:S(2)}) %collective-permute-start.4) | collective-permute-done | bytes 262176 | tf_op jit(solution)/shard_map/ppermute | solution.py:388
  22.8 1.1 %collective-permute-start.8 = (bf16[128,8,128]{2,1,0:T(8,128)(2,1)S(1)}, bf16[128,8,128]{2,1,0:T(8,128)(2,1)S(1)}, u32[]{:S(2)}, u32[]{:S(2)}) collective-permute-start(bf16[128,8,128]{2,1,0:T(8,128)(2,1)S(1)} %collective-permute-done.5.refs_4_), channel_id=1, source_target_pairs={{0,1},{1,0},{2,3},{3,2},{4,5},{5,4},{6,7},{7,6},{8,9},{9,8},{10,11... | collective-permute-start | bytes 786440 | tf_op jit(solution)/shard_map/ppermute | solution.py:388
  23.9 0.4 collective-permute-done.7.refs_7_
  24.3 0.8 %collective-permute-done.8.refs_8_ = bf16[128,8,128]{2,1,0:T(8,128)(2,1)S(1)} collective-permute-done((bf16[128,8,128]{2,1,0:T(8,128)(2,1)S(1)}, bf16[128,8,128]{2,1,0:T(8,128)(2,1)S(1)}, u32[]{:S(2)}, u32[]{:S(2)}) %collective-permute-start.8) | collective-permute-done | bytes 262176 | tf_op jit(solution)/shard_map/ppermute | solution.py:388
  25.1 2.4 %later_sweep.2 = (f32[32,8,128]{2,1,0:T(8,128)S(1)}, bf16[32,8,128]{2,1,0:T(8,128)(2,1)S(1)}) custom-call(s32[64]{0:T(128)S(1)} %get-tuple-element.16.perm_ref.refs_0_, s32[1024]{0:T(1024)S(1)} %get-tuple-element.18.refs_1_, bf16[128,8,128]{2,1,0:T(8,128)(2,1)S(1)} %collective-permute-done.3.refs_2_, ...), custom_call_target="tpu_custom_call" | custom-call | tf_op jit(solution)/shard_map/later_sweep/pallas_call | solution.py:465
  27.5 2.5 %collective-permute-start.13 = (bf16[32,8,128]{2,1,0:T(8,128)(2,1)S(1)}, bf16[32,8,128]{2,1,0:T(8,128)(2,1)S(1)}, u32[]{:S(2)}, u32[]{:S(2)}) collective-permute-start(bf16[32,8,128]{2,1,0:T(8,128)(2,1)S(1)} %get-tuple-element.25.value_ref), channel_id=1, source_target_pairs={{0,6},{1,25},{2,4},{3,27},{4,2},{5,29},{6,0},{7,31},{8,14},{9,17},... | collective-permute-start | bytes 196616 | tf_op jit(solution)/shard_map/ppermute | solution.py:388
  30.0 2.0 %collective-permute-start.15 = (bf16[32,8,128]{2,1,0:T(8,128)(2,1)S(1)}, bf16[32,8,128]{2,1,0:T(8,128)(2,1)S(1)}, u32[]{:S(2)}, u32[]{:S(2)}) collective-permute-start(bf16[32,8,128]{2,1,0:T(8,128)(2,1)S(1)} %get-tuple-element.25.value_ref), channel_id=1, source_target_pairs={{0,2},{1,9},{2,0},{3,11},{4,6},{5,13},{6,4},{7,15},{8,10},{9,1},{1... | collective-permute-start | bytes 196616 | tf_op jit(solution)/shard_map/ppermute | solution.py:388
  31.9 2.2 %collective-permute-start.10 = (bf16[32,8,128]{2,1,0:T(8,128)(2,1)S(1)}, bf16[32,8,128]{2,1,0:T(8,128)(2,1)S(1)}, u32[]{:S(2)}, u32[]{:S(2)}) collective-permute-start(bf16[32,8,128]{2,1,0:T(8,128)(2,1)S(1)} %duplicate.1), channel_id=1, source_target_pairs={{0,24},{1,7},{2,26},{3,5},{4,28},{5,3},{6,30},{7,1},{8,16},{9,15},... | collective-permute-start | bytes 196616 | tf_op jit(solution)/shard_map/ppermute | solution.py:388
  34.1 0.8 %collective-permute-start.11 = (bf16[32,8,128]{2,1,0:T(8,128)(2,1)S(1)}, bf16[32,8,128]{2,1,0:T(8,128)(2,1)S(1)}, u32[]{:S(2)}, u32[]{:S(2)}) collective-permute-start(bf16[32,8,128]{2,1,0:T(8,128)(2,1)S(1)} %duplicate.1), channel_id=1, source_target_pairs={{0,8},{1,5},{2,10},{3,7},{4,12},{5,1},{6,14},{7,3},{8,0},{9,13},{1... | collective-permute-start | bytes 196616 | tf_op jit(solution)/shard_map/ppermute | solution.py:388
  34.9 0.5 collective-permute-start.12
  35.4 1.9 %collective-permute-done.14 = bf16[32,8,128]{2,1,0:T(8,128)(2,1)S(1)} collective-permute-done((bf16[32,8,128]{2,1,0:T(8,128)(2,1)S(1)}, bf16[32,8,128]{2,1,0:T(8,128)(2,1)S(1)}, u32[]{:S(2)}, u32[]{:S(2)}) %collective-permute-start.14) | collective-permute-done | bytes 65568 | tf_op jit(solution)/shard_map/ppermute | solution.py:388
  37.4 2.1 %collective-permute-start.16 = (bf16[96,8,128]{2,1,0:T(8,128)(2,1)S(1)}, bf16[96,8,128]{2,1,0:T(8,128)(2,1)S(1)}, u32[]{:S(2)}, u32[]{:S(2)}) collective-permute-start(bf16[96,8,128]{2,1,0:T(8,128)(2,1)S(1)} %constant_dynamic-update-slice_fusion.4.refs_3_), channel_id=1, source_target_pairs={{0,24},{1,7},{2,26},{3,5},{4,28},{5,3},{6,30},{7,1},{8,16},{9,15},... | collective-permute-start | bytes 589832 | tf_op jit(solution)/shard_map/ppermute | solution.py:388
  39.5 0.8 %collective-permute-start.17 = (bf16[96,8,128]{2,1,0:T(8,128)(2,1)S(1)}, bf16[96,8,128]{2,1,0:T(8,128)(2,1)S(1)}, u32[]{:S(2)}, u32[]{:S(2)}) collective-permute-start(bf16[96,8,128]{2,1,0:T(8,128)(2,1)S(1)} %constant_dynamic-update-slice_fusion.4.refs_3_), channel_id=1, source_target_pairs={{0,16},{1,3},{2,18},{3,1},{4,20},{5,7},{6,22},{7,5},{8,24},{9,11},... | collective-permute-start | bytes 589832 | tf_op jit(solution)/shard_map/ppermute | solution.py:388
  40.4 0.6 collective-permute-start.18
  41.1 0.5 collective-permute-start.20
  41.6 2.6 %collective-permute-done.16.refs_4_ = bf16[96,8,128]{2,1,0:T(8,128)(2,1)S(1)} collective-permute-done((bf16[96,8,128]{2,1,0:T(8,128)(2,1)S(1)}, bf16[96,8,128]{2,1,0:T(8,128)(2,1)S(1)}, u32[]{:S(2)}, u32[]{:S(2)}) %collective-permute-start.16) | collective-permute-done | bytes 196640 | tf_op jit(solution)/shard_map/ppermute | solution.py:388
  44.1 2.0 %collective-permute-done.17.refs_5_ = bf16[96,8,128]{2,1,0:T(8,128)(2,1)S(1)} collective-permute-done((bf16[96,8,128]{2,1,0:T(8,128)(2,1)S(1)}, bf16[96,8,128]{2,1,0:T(8,128)(2,1)S(1)}, u32[]{:S(2)}, u32[]{:S(2)}) %collective-permute-start.17) | collective-permute-done | bytes 196640 | tf_op jit(solution)/shard_map/ppermute | solution.py:388
  46.2 0.5 collective-permute-start.23
  46.7 0.9 %collective-permute-done.22.refs_10_ = bf16[96,8,128]{2,1,0:T(8,128)(2,1)S(1)} collective-permute-done((bf16[96,8,128]{2,1,0:T(8,128)(2,1)S(1)}, bf16[96,8,128]{2,1,0:T(8,128)(2,1)S(1)}, u32[]{:S(2)}, u32[]{:S(2)}) %collective-permute-start.22) | collective-permute-done | bytes 196640 | tf_op jit(solution)/shard_map/ppermute | solution.py:388
  47.6 0.3 collective-permute-done.23.refs_11_
  47.9 2.5 %later_sweep.3 = f32[32,8,128]{2,1,0:T(8,128)S(1)} custom-call(s32[64]{0:T(128)S(1)} %get-tuple-element.16.perm_ref.refs_0_, s32[1024]{0:T(1024)S(1)} %get-tuple-element.18.refs_1_, bf16[128,8,128]{2,1,0:T(8,128)(2,1)S(1)} %pad_maximum_fusion.refs_2_, bf16[96,8,128]{2,1,0:T(8,128)(2,1)S(1)} %constant_dynamic-update-slice_fusion.4.refs_3_, ...), custom_call_target="tpu_custom_call" | custom-call | tf_op jit(solution)/shard_map/later_sweep/pallas_call | solution.py:465
  50.4 11.8 %all_to_all.5 = f32[32,8,128]{2,1,0:T(8,128)S(1)} all-to-all(f32[32,8,128]{2,1,0:T(8,128)S(1)} %later_sweep.3), channel_id=1, replica_groups=mesh['grp'=4,'row'=8] {'grp','row'}, dimensions={0} | all-to-all | bytes 262144 | tf_op jit(solution)/shard_map/all_to_all | solution.py:491
  62.1 0.7 %lay_out.1 = f32[64,512]{1,0:T(8,128)} custom-call(f32[256,128]{1,0:T(8,128)S(1)} %bitcast.5), custom_call_target="tpu_custom_call" | custom-call | tf_op jit(solution)/shard_map/lay_out/pallas_call | solution.py:492
  (32 shorter events, 0.6 us)
Async XLA Ops:
  2.2 7.9 %collective-permute-start = (bf16[32,8,128]{2,1,0:T(8,128)(2,1)S(1)}, bf16[32,8,128]{2,1,0:T(8,128)(2,1)S(1)}, u32[]{:S(2)}, u32[]{:S(2)}) collective-permute-start(bf16[32,8,128]{2,1,0:T(8,128)(2,1)S(1)} %get-tuple-element.17.rounded_ref), channel_id=1, source_target_pairs={{0,6},{1,25},{2,4},{3,27},{4,2},{5,29},{6,0},{7,31},{8,14},{9,17},... | collective-permute-start | bytes 196616 | tf_op jit(solution)/shard_map/ppermute | solution.py:388
  7.4 5.2 %collective-permute-start.1 = (bf16[32,8,128]{2,1,0:T(8,128)(2,1)S(1)}, bf16[32,8,128]{2,1,0:T(8,128)(2,1)S(1)}, u32[]{:S(2)}, u32[]{:S(2)}) collective-permute-start(bf16[32,8,128]{2,1,0:T(8,128)(2,1)S(1)} %get-tuple-element.17.rounded_ref), channel_id=1, source_target_pairs={{0,4},{1,17},{2,6},{3,19},{4,0},{5,21},{6,2},{7,23},{8,12},{9,25},... | collective-permute-start | bytes 196616 | tf_op jit(solution)/shard_map/ppermute | solution.py:388
  7.4 5.2 %collective-permute-start.2 = (bf16[32,8,128]{2,1,0:T(8,128)(2,1)S(1)}, bf16[32,8,128]{2,1,0:T(8,128)(2,1)S(1)}, u32[]{:S(2)}, u32[]{:S(2)}) collective-permute-start(bf16[32,8,128]{2,1,0:T(8,128)(2,1)S(1)} %get-tuple-element.17.rounded_ref), channel_id=1, source_target_pairs={{0,2},{1,9},{2,0},{3,11},{4,6},{5,13},{6,4},{7,15},{8,10},{9,1},{1... | collective-permute-start | bytes 196616 | tf_op jit(solution)/shard_map/ppermute | solution.py:388
  12.6 7.4 %collective-permute-start.3 = (bf16[128,8,128]{2,1,0:T(8,128)(2,1)S(1)}, bf16[128,8,128]{2,1,0:T(8,128)(2,1)S(1)}, u32[]{:S(2)}, u32[]{:S(2)}) collective-permute-start(bf16[128,8,128]{2,1,0:T(8,128)(2,1)S(1)} %constant_dynamic-update-slice_fusion.gathered_ref.refs_5_), channel_id=1, source_target_pairs={{0,24},{1,7},{2,26},{3,5},{4,28},{5,3},{6,30},{7,1},{8,16},{9,15},... | collective-permute-start | bytes 786440 | tf_op jit(solution)/shard_map/ppermute | solution.py:388
  15.5 7.2 %collective-permute-start.4 = (bf16[128,8,128]{2,1,0:T(8,128)(2,1)S(1)}, bf16[128,8,128]{2,1,0:T(8,128)(2,1)S(1)}, u32[]{:S(2)}, u32[]{:S(2)}) collective-permute-start(bf16[128,8,128]{2,1,0:T(8,128)(2,1)S(1)} %constant_dynamic-update-slice_fusion.gathered_ref.refs_5_), channel_id=1, source_target_pairs={{0,16},{1,3},{2,18},{3,1},{4,20},{5,7},{6,22},{7,5},{8,24},{9,11},... | collective-permute-start | bytes 786440 | tf_op jit(solution)/shard_map/ppermute | solution.py:388
  16.0 6.8 %collective-permute-start.5 = (bf16[128,8,128]{2,1,0:T(8,128)(2,1)S(1)}, bf16[128,8,128]{2,1,0:T(8,128)(2,1)S(1)}, u32[]{:S(2)}, u32[]{:S(2)}) collective-permute-start(bf16[128,8,128]{2,1,0:T(8,128)(2,1)S(1)} %constant_dynamic-update-slice_fusion.gathered_ref.refs_5_), channel_id=1, source_target_pairs={{0,8},{1,5},{2,10},{3,7},{4,12},{5,1},{6,14},{7,3},{8,0},{9,13},{1... | collective-permute-start | bytes 786440 | tf_op jit(solution)/shard_map/ppermute | solution.py:388
  19.1 4.8 %collective-permute-start.9 = (bf16[128,8,128]{2,1,0:T(8,128)(2,1)S(1)}, bf16[128,8,128]{2,1,0:T(8,128)(2,1)S(1)}, u32[]{:S(2)}, u32[]{:S(2)}) collective-permute-start(bf16[128,8,128]{2,1,0:T(8,128)(2,1)S(1)} %get-tuple-element.20), channel_id=1, source_target_pairs={{0,1},{1,0},{2,3},{3,2},{4,5},{5,4},{6,7},{7,6},{8,9},{9,8},{10,11... | collective-permute-start | bytes 786440 | tf_op jit(solution)/shard_map/ppermute | solution.py:388
  20.0 3.9 %collective-permute-start.6 = (bf16[128,8,128]{2,1,0:T(8,128)(2,1)S(1)}, bf16[128,8,128]{2,1,0:T(8,128)(2,1)S(1)}, u32[]{:S(2)}, u32[]{:S(2)}) collective-permute-start(bf16[128,8,128]{2,1,0:T(8,128)(2,1)S(1)} %collective-permute-done.3.refs_2_), channel_id=1, source_target_pairs={{0,1},{1,0},{2,3},{3,2},{4,5},{5,4},{6,7},{7,6},{8,9},{9,8},{10,11... | collective-permute-start | bytes 786440 | tf_op jit(solution)/shard_map/ppermute | solution.py:388
  22.7 1.5 %collective-permute-start.7 = (bf16[128,8,128]{2,1,0:T(8,128)(2,1)S(1)}, bf16[128,8,128]{2,1,0:T(8,128)(2,1)S(1)}, u32[]{:S(2)}, u32[]{:S(2)}) collective-permute-start(bf16[128,8,128]{2,1,0:T(8,128)(2,1)S(1)} %collective-permute-done.4.refs_3_), channel_id=1, source_target_pairs={{0,1},{1,0},{2,3},{3,2},{4,5},{5,4},{6,7},{7,6},{8,9},{9,8},{10,11... | collective-permute-start | bytes 786440 | tf_op jit(solution)/shard_map/ppermute | solution.py:388
  22.8 2.2 %collective-permute-start.8 = (bf16[128,8,128]{2,1,0:T(8,128)(2,1)S(1)}, bf16[128,8,128]{2,1,0:T(8,128)(2,1)S(1)}, u32[]{:S(2)}, u32[]{:S(2)}) collective-permute-start(bf16[128,8,128]{2,1,0:T(8,128)(2,1)S(1)} %collective-permute-done.5.refs_4_), channel_id=1, source_target_pairs={{0,1},{1,0},{2,3},{3,2},{4,5},{5,4},{6,7},{7,6},{8,9},{9,8},{10,11... | collective-permute-start | bytes 786440 | tf_op jit(solution)/shard_map/ppermute | solution.py:388
  27.5 7.4 %collective-permute-start.13 = (bf16[32,8,128]{2,1,0:T(8,128)(2,1)S(1)}, bf16[32,8,128]{2,1,0:T(8,128)(2,1)S(1)}, u32[]{:S(2)}, u32[]{:S(2)}) collective-permute-start(bf16[32,8,128]{2,1,0:T(8,128)(2,1)S(1)} %get-tuple-element.25.value_ref), channel_id=1, source_target_pairs={{0,6},{1,25},{2,4},{3,27},{4,2},{5,29},{6,0},{7,31},{8,14},{9,17},... | collective-permute-start | bytes 196616 | tf_op jit(solution)/shard_map/ppermute | solution.py:388
  30.0 7.4 %collective-permute-start.14 = (bf16[32,8,128]{2,1,0:T(8,128)(2,1)S(1)}, bf16[32,8,128]{2,1,0:T(8,128)(2,1)S(1)}, u32[]{:S(2)}, u32[]{:S(2)}) collective-permute-start(bf16[32,8,128]{2,1,0:T(8,128)(2,1)S(1)} %get-tuple-element.25.value_ref), channel_id=1, source_target_pairs={{0,4},{1,17},{2,6},{3,19},{4,0},{5,21},{6,2},{7,23},{8,12},{9,25},... | collective-permute-start | bytes 196616 | tf_op jit(solution)/shard_map/ppermute | solution.py:388
  30.0 7.4 %collective-permute-start.15 = (bf16[32,8,128]{2,1,0:T(8,128)(2,1)S(1)}, bf16[32,8,128]{2,1,0:T(8,128)(2,1)S(1)}, u32[]{:S(2)}, u32[]{:S(2)}) collective-permute-start(bf16[32,8,128]{2,1,0:T(8,128)(2,1)S(1)} %get-tuple-element.25.value_ref), channel_id=1, source_target_pairs={{0,2},{1,9},{2,0},{3,11},{4,6},{5,13},{6,4},{7,15},{8,10},{9,1},{1... | collective-permute-start | bytes 196616 | tf_op jit(solution)/shard_map/ppermute | solution.py:388
  31.9 8.4 %collective-permute-start.10 = (bf16[32,8,128]{2,1,0:T(8,128)(2,1)S(1)}, bf16[32,8,128]{2,1,0:T(8,128)(2,1)S(1)}, u32[]{:S(2)}, u32[]{:S(2)}) collective-permute-start(bf16[32,8,128]{2,1,0:T(8,128)(2,1)S(1)} %duplicate.1), channel_id=1, source_target_pairs={{0,24},{1,7},{2,26},{3,5},{4,28},{5,3},{6,30},{7,1},{8,16},{9,15},... | collective-permute-start | bytes 196616 | tf_op jit(solution)/shard_map/ppermute | solution.py:388
  34.1 6.9 %collective-permute-start.11 = (bf16[32,8,128]{2,1,0:T(8,128)(2,1)S(1)}, bf16[32,8,128]{2,1,0:T(8,128)(2,1)S(1)}, u32[]{:S(2)}, u32[]{:S(2)}) collective-permute-start(bf16[32,8,128]{2,1,0:T(8,128)(2,1)S(1)} %duplicate.1), channel_id=1, source_target_pairs={{0,8},{1,5},{2,10},{3,7},{4,12},{5,1},{6,14},{7,3},{8,0},{9,13},{1... | collective-permute-start | bytes 196616 | tf_op jit(solution)/shard_map/ppermute | solution.py:388
  34.9 6.0 %collective-permute-start.12 = (bf16[32,8,128]{2,1,0:T(8,128)(2,1)S(1)}, bf16[32,8,128]{2,1,0:T(8,128)(2,1)S(1)}, u32[]{:S(2)}, u32[]{:S(2)}) collective-permute-start(bf16[32,8,128]{2,1,0:T(8,128)(2,1)S(1)} %duplicate.1), channel_id=1, source_target_pairs={{0,16},{1,3},{2,18},{3,1},{4,20},{5,7},{6,22},{7,5},{8,24},{9,11},... | collective-permute-start | bytes 196616 | tf_op jit(solution)/shard_map/ppermute | solution.py:388
  37.4 6.7 %collective-permute-start.16 = (bf16[96,8,128]{2,1,0:T(8,128)(2,1)S(1)}, bf16[96,8,128]{2,1,0:T(8,128)(2,1)S(1)}, u32[]{:S(2)}, u32[]{:S(2)}) collective-permute-start(bf16[96,8,128]{2,1,0:T(8,128)(2,1)S(1)} %constant_dynamic-update-slice_fusion.4.refs_3_), channel_id=1, source_target_pairs={{0,24},{1,7},{2,26},{3,5},{4,28},{5,3},{6,30},{7,1},{8,16},{9,15},... | collective-permute-start | bytes 589832 | tf_op jit(solution)/shard_map/ppermute | solution.py:388
  39.5 6.6 %collective-permute-start.17 = (bf16[96,8,128]{2,1,0:T(8,128)(2,1)S(1)}, bf16[96,8,128]{2,1,0:T(8,128)(2,1)S(1)}, u32[]{:S(2)}, u32[]{:S(2)}) collective-permute-start(bf16[96,8,128]{2,1,0:T(8,128)(2,1)S(1)} %constant_dynamic-update-slice_fusion.4.refs_3_), channel_id=1, source_target_pairs={{0,16},{1,3},{2,18},{3,1},{4,20},{5,7},{6,22},{7,5},{8,24},{9,11},... | collective-permute-start | bytes 589832 | tf_op jit(solution)/shard_map/ppermute | solution.py:388
  40.4 5.8 %collective-permute-start.18 = (bf16[96,8,128]{2,1,0:T(8,128)(2,1)S(1)}, bf16[96,8,128]{2,1,0:T(8,128)(2,1)S(1)}, u32[]{:S(2)}, u32[]{:S(2)}) collective-permute-start(bf16[96,8,128]{2,1,0:T(8,128)(2,1)S(1)} %constant_dynamic-update-slice_fusion.4.refs_3_), channel_id=1, source_target_pairs={{0,8},{1,5},{2,10},{3,7},{4,12},{5,1},{6,14},{7,3},{8,0},{9,13},{1... | collective-permute-start | bytes 589832 | tf_op jit(solution)/shard_map/ppermute | solution.py:388
  41.0 5.7 %collective-permute-start.19 = (bf16[128,8,128]{2,1,0:T(8,128)(2,1)S(1)}, bf16[128,8,128]{2,1,0:T(8,128)(2,1)S(1)}, u32[]{:S(2)}, u32[]{:S(2)}) collective-permute-start(bf16[128,8,128]{2,1,0:T(8,128)(2,1)S(1)} %pad_maximum_fusion.refs_2_), channel_id=1, source_target_pairs={{0,1},{1,0},{2,3},{3,2},{4,5},{5,4},{6,7},{7,6},{8,9},{9,8},{10,11... | collective-permute-start | bytes 786440 | tf_op jit(solution)/shard_map/ppermute | solution.py:388
  41.1 5.6 %collective-permute-start.20 = (bf16[96,8,128]{2,1,0:T(8,128)(2,1)S(1)}, bf16[96,8,128]{2,1,0:T(8,128)(2,1)S(1)}, u32[]{:S(2)}, u32[]{:S(2)}) collective-permute-start(bf16[96,8,128]{2,1,0:T(8,128)(2,1)S(1)} %constant_dynamic-update-slice_fusion.4.refs_3_), channel_id=1, source_target_pairs={{0,1},{1,0},{2,3},{3,2},{4,5},{5,4},{6,7},{7,6},{8,9},{9,8},{10,11... | collective-permute-start | bytes 589832 | tf_op jit(solution)/shard_map/ppermute | solution.py:388
  44.1 2.5 %collective-permute-start.21 = (bf16[96,8,128]{2,1,0:T(8,128)(2,1)S(1)}, bf16[96,8,128]{2,1,0:T(8,128)(2,1)S(1)}, u32[]{:S(2)}, u32[]{:S(2)}) collective-permute-start(bf16[96,8,128]{2,1,0:T(8,128)(2,1)S(1)} %collective-permute-done.16.refs_4_), channel_id=1, source_target_pairs={{0,1},{1,0},{2,3},{3,2},{4,5},{5,4},{6,7},{7,6},{8,9},{9,8},{10,11... | collective-permute-start | bytes 589832 | tf_op jit(solution)/shard_map/ppermute | solution.py:388
  46.1 1.4 %collective-permute-start.22 = (bf16[96,8,128]{2,1,0:T(8,128)(2,1)S(1)}, bf16[96,8,128]{2,1,0:T(8,128)(2,1)S(1)}, u32[]{:S(2)}, u32[]{:S(2)}) collective-permute-start(bf16[96,8,128]{2,1,0:T(8,128)(2,1)S(1)} %collective-permute-done.17.refs_5_), channel_id=1, source_target_pairs={{0,1},{1,0},{2,3},{3,2},{4,5},{5,4},{6,7},{7,6},{8,9},{9,8},{10,11... | collective-permute-start | bytes 589832 | tf_op jit(solution)/shard_map/ppermute | solution.py:388
  46.2 1.7 %collective-permute-start.23 = (bf16[96,8,128]{2,1,0:T(8,128)(2,1)S(1)}, bf16[96,8,128]{2,1,0:T(8,128)(2,1)S(1)}, u32[]{:S(2)}, u32[]{:S(2)}) collective-permute-start(bf16[96,8,128]{2,1,0:T(8,128)(2,1)S(1)} %collective-permute-done.18.refs_6_), channel_id=1, source_target_pairs={{0,1},{1,0},{2,3},{3,2},{4,5},{5,4},{6,7},{7,6},{8,9},{9,8},{10,11... | collective-permute-start | bytes 589832 | tf_op jit(solution)/shard_map/ppermute | solution.py:388

commit v9 on v7

--- a/solution.py
+++ b/solution.py
@@ -203,10 +203,6 @@
         line.start()
     for line in lines:
         line.wait()
-
-
-def duplicate(value_ref, out_ref):
-    out_ref[...] = value_ref[...]
 
 
 def prepare(
@@ -410,17 +406,9 @@
 
     def both_levels(value):
         ahead = direct(value, list(zip(even, odd[::-1])))
-        copy = pl.pallas_call(
-            duplicate,
-            out_shape=jax.ShapeDtypeStruct(tile_shape, jnp.bfloat16),
-            in_specs=[vmem],
-            out_specs=vmem,
-            compiler_params=params,
-            name="duplicate",
-        )(value)
-        aside = direct(copy, list(zip(odd, even)))
+        aside = direct(value, list(zip(odd, even)))
         ahead = jnp.concatenate([ahead[-1]] + ahead[1:-1], axis=0)
-        aside = jnp.concatenate([aside[-1]] + aside[1:-1] + [copy], axis=0)
+        aside = jnp.concatenate([aside[-1]] + aside[1:-1] + [value], axis=0)
         near = [aside, ahead] + direct(ahead, list(zip(odd, even)))[:0:-1]
         plan = []
         for core in range(2):

time: 62.8 us -> 62.9 us (level)
  no operation moved by 1% of the time
where the time goes in v9:
time: 62.9 us; the launch traced here: 62.6 us
  starting transfers between devices  23 us (37%)
  waiting for transfers between devices  14.9 us (24%)
  Pallas kernels  12.7 us (20%)
  blocking collectives  11.8 us (19%)
    ppermute x24, starting transfers between devices, exchange(): return lax.ppermute(value, ('grp', 'row'), pairs_of)  23 us
    ppermute x24, waiting for transfers between devices, exchange(): return lax.ppermute(value, ('grp', 'row'), pairs_of)  14.9 us
    all_to_all x1, blocking collectives, local(): lax.all_to_all(x, ('grp', 'row'), split_axis=0, concat_axis=0, tiled=True)  11.8 us
    pallas_call x2, Pallas kernels, sweep(): pl.pallas_call(functools.partial(later_sweep, plan, len(pieces), not last...  4.73 us
    pallas_call x1, Pallas kernels, local(): pl.pallas_call(prepare, out_shape=(jax.ShapeDtypeStruct(gathered.shape, j...  2.95 us
    pallas_call x1, Pallas kernels, local(): pl.pallas_call(functools.partial(first_sweep, full), out_shape=(jax.Shape...  2.24 us
    pallas_call x1, Pallas kernels, local(): pl.pallas_call(functools.partial(locate, full, devices, members), out_sha...  2.09 us
  transfers between devices with their start and end apart: 24, of which 11 were waited for; matrix products, arithmetic and copies ran while one was open for 0% of the time, Pallas kernels for 8%

profile of v9, /device:TPU:0, one launch (start us, length us, event | category | flops | bytes accessed | tf_op | source)
XLA Modules:
  0.0 62.6 jit_solution(4720176823616182902)
XLA Ops:
  0.0 2.2 %first_sweep.1 = (s32[64]{0:T(128)S(1)}, s32[32]{0:T(128)}, bf16[32,8,128]{2,1,0:T(8,128)(2,1)S(1)}) custom-call(s32[64]{0:T(128)} %bitcast.8, bf16[64,4096]{1,0:T(8,128)(2,1)} %smooth_hbm.3, bf16[64,512]{1,0:T(8,128)(2,1)} %right_hbm.3), custom_call_target="tpu_custom_call" | custom-call | tf_op jit(solution)/shard_map/first_sweep/pallas_call | solution.py:331
  2.2 5.1 %collective-permute-start = (bf16[32,8,128]{2,1,0:T(8,128)(2,1)S(1)}, bf16[32,8,128]{2,1,0:T(8,128)(2,1)S(1)}, u32[]{:S(2)}, u32[]{:S(2)}) collective-permute-start(bf16[32,8,128]{2,1,0:T(8,128)(2,1)S(1)} %get-tuple-element.17.rounded_ref), channel_id=1, source_target_pairs={{0,6},{1,25},{2,4},{3,27},{4,2},{5,29},{6,0},{7,31},{8,14},{9,17},... | collective-permute-start | bytes 196616 | tf_op jit(solution)/shard_map/ppermute | solution.py:384
  7.4 0.6 %collective-permute-start.2 = (bf16[32,8,128]{2,1,0:T(8,128)(2,1)S(1)}, bf16[32,8,128]{2,1,0:T(8,128)(2,1)S(1)}, u32[]{:S(2)}, u32[]{:S(2)}) collective-permute-start(bf16[32,8,128]{2,1,0:T(8,128)(2,1)S(1)} %get-tuple-element.17.rounded_ref), channel_id=1, source_target_pairs={{0,2},{1,9},{2,0},{3,11},{4,6},{5,13},{6,4},{7,15},{8,10},{9,1},{1... | collective-permute-start | bytes 196616 | tf_op jit(solution)/shard_map/ppermute | solution.py:384
  8.0 2.1 %locate.1 = (bf16[32,8,128]{2,1,0:T(8,128)(2,1)S(1)}, s32[1024]{0:T(1024)S(1)}) custom-call(bf16[32,8,128]{2,1,0:T(8,128)(2,1)S(1)} %get-tuple-element.17.rounded_ref, s32[8,64]{1,0:T(8,128)} %bitcast.6, s32[8,64]{1,0:T(8,128)} %bitcast.7, s32[1,64]{1,0:T(1,128)} %bitcast.9), custom_call_target="tpu_custom_call" | custom-call | flops 1048576 | bytes 2097152 | tf_op jit(solution)/shard_map/locate/pallas_call | solution.py:361
  10.1 2.4 %collective-permute-done.1 = bf16[32,8,128]{2,1,0:T(8,128)(2,1)S(1)} collective-permute-done((bf16[32,8,128]{2,1,0:T(8,128)(2,1)S(1)}, bf16[32,8,128]{2,1,0:T(8,128)(2,1)S(1)}, u32[]{:S(2)}, u32[]{:S(2)}) %collective-permute-start.1) | collective-permute-done | bytes 65568 | tf_op jit(solution)/shard_map/ppermute | solution.py:384
  12.6 2.9 %collective-permute-start.3 = (bf16[128,8,128]{2,1,0:T(8,128)(2,1)S(1)}, bf16[128,8,128]{2,1,0:T(8,128)(2,1)S(1)}, u32[]{:S(2)}, u32[]{:S(2)}) collective-permute-start(bf16[128,8,128]{2,1,0:T(8,128)(2,1)S(1)} %constant_dynamic-update-slice_fusion.gathered_ref.refs_5_), channel_id=1, source_target_pairs={{0,24},{1,7},{2,26},{3,5},{4,28},{5,3},{6,30},{7,1},{8,16},{9,15},... | collective-permute-start | bytes 786440 | tf_op jit(solution)/shard_map/ppermute | solution.py:384
  15.5 0.5 collective-permute-start.4
  16.2 3.0 %prepare.1 = (bf16[128,8,128]{2,1,0:T(8,128)(2,1)S(1)}, f32[32,8,128]{2,1,0:T(8,128)S(1)}, bf16[32,8,128]{2,1,0:T(8,128)(2,1)S(1)}, bf16[32,128,128]{2,1,0:T(8,128)(2,1)S(1)}, bf16[64,64,512]{2,1,0:T(8,128)(2,1)S(1)}) custom-call(s32[64]{0:T(128)S(1)} %get-tuple-element.16.perm_ref.refs_0_, ...), custom_call_target="tpu_custom_call" | custom-call | flops 67108864 | bytes 10485760 | tf_op jit(solution)/shard_map/prepare/pallas_call | solution.py:425
  19.2 0.8 %collective-permute-done.3.refs_2_ = bf16[128,8,128]{2,1,0:T(8,128)(2,1)S(1)} collective-permute-done((bf16[128,8,128]{2,1,0:T(8,128)(2,1)S(1)}, bf16[128,8,128]{2,1,0:T(8,128)(2,1)S(1)}, u32[]{:S(2)}, u32[]{:S(2)}) %collective-permute-start.3) | collective-permute-done | bytes 262176 | tf_op jit(solution)/shard_map/ppermute | solution.py:384
  20.0 2.7 %collective-permute-done.4.refs_3_ = bf16[128,8,128]{2,1,0:T(8,128)(2,1)S(1)} collective-permute-done((bf16[128,8,128]{2,1,0:T(8,128)(2,1)S(1)}, bf16[128,8,128]{2,1,0:T(8,128)(2,1)S(1)}, u32[]{:S(2)}, u32[]{:S(2)}) %collective-permute-start.4) | collective-permute-done | bytes 262176 | tf_op jit(solution)/shard_map/ppermute | solution.py:384
  22.8 1.1 %collective-permute-start.8 = (bf16[128,8,128]{2,1,0:T(8,128)(2,1)S(1)}, bf16[128,8,128]{2,1,0:T(8,128)(2,1)S(1)}, u32[]{:S(2)}, u32[]{:S(2)}) collective-permute-start(bf16[128,8,128]{2,1,0:T(8,128)(2,1)S(1)} %collective-permute-done.5.refs_4_), channel_id=1, source_target_pairs={{0,1},{1,0},{2,3},{3,2},{4,5},{5,4},{6,7},{7,6},{8,9},{9,8},{10,11... | collective-permute-start | bytes 786440 | tf_op jit(solution)/shard_map/ppermute | solution.py:384
  23.9 0.4 collective-permute-done.7.refs_7_
  24.3 0.8 %collective-permute-done.8.refs_8_ = bf16[128,8,128]{2,1,0:T(8,128)(2,1)S(1)} collective-permute-done((bf16[128,8,128]{2,1,0:T(8,128)(2,1)S(1)}, bf16[128,8,128]{2,1,0:T(8,128)(2,1)S(1)}, u32[]{:S(2)}, u32[]{:S(2)}) %collective-permute-start.8) | collective-permute-done | bytes 262176 | tf_op jit(solution)/shard_map/ppermute | solution.py:384
  25.1 2.3 %later_sweep.2 = (f32[32,8,128]{2,1,0:T(8,128)S(1)}, bf16[32,8,128]{2,1,0:T(8,128)(2,1)S(1)}) custom-call(s32[64]{0:T(128)S(1)} %get-tuple-element.16.perm_ref.refs_0_, s32[1024]{0:T(1024)S(1)} %get-tuple-element.18.refs_1_, bf16[128,8,128]{2,1,0:T(8,128)(2,1)S(1)} %collective-permute-done.3.refs_2_, ...), custom_call_target="tpu_custom_call" | custom-call | tf_op jit(solution)/shard_map/later_sweep/pallas_call | solution.py:453
  27.4 2.5 %collective-permute-start.13 = (bf16[32,8,128]{2,1,0:T(8,128)(2,1)S(1)}, bf16[32,8,128]{2,1,0:T(8,128)(2,1)S(1)}, u32[]{:S(2)}, u32[]{:S(2)}) collective-permute-start(bf16[32,8,128]{2,1,0:T(8,128)(2,1)S(1)} %get-tuple-element.25), channel_id=1, source_target_pairs={{0,6},{1,25},{2,4},{3,27},{4,2},{5,29},{6,0},{7,31},{8,14},{9,17},... | collective-permute-start | bytes 196616 | tf_op jit(solution)/shard_map/ppermute | solution.py:384
  29.9 2.0 %collective-permute-start.15 = (bf16[32,8,128]{2,1,0:T(8,128)(2,1)S(1)}, bf16[32,8,128]{2,1,0:T(8,128)(2,1)S(1)}, u32[]{:S(2)}, u32[]{:S(2)}) collective-permute-start(bf16[32,8,128]{2,1,0:T(8,128)(2,1)S(1)} %get-tuple-element.25), channel_id=1, source_target_pairs={{0,2},{1,9},{2,0},{3,11},{4,6},{5,13},{6,4},{7,15},{8,10},{9,1},{1... | collective-permute-start | bytes 196616 | tf_op jit(solution)/shard_map/ppermute | solution.py:384
  31.9 2.2 %collective-permute-start.10 = (bf16[32,8,128]{2,1,0:T(8,128)(2,1)S(1)}, bf16[32,8,128]{2,1,0:T(8,128)(2,1)S(1)}, u32[]{:S(2)}, u32[]{:S(2)}) collective-permute-start(bf16[32,8,128]{2,1,0:T(8,128)(2,1)S(1)} %get-tuple-element.25), channel_id=1, source_target_pairs={{0,24},{1,7},{2,26},{3,5},{4,28},{5,3},{6,30},{7,1},{8,16},{9,15},... | collective-permute-start | bytes 196616 | tf_op jit(solution)/shard_map/ppermute | solution.py:384
  34.0 0.8 %collective-permute-start.11 = (bf16[32,8,128]{2,1,0:T(8,128)(2,1)S(1)}, bf16[32,8,128]{2,1,0:T(8,128)(2,1)S(1)}, u32[]{:S(2)}, u32[]{:S(2)}) collective-permute-start(bf16[32,8,128]{2,1,0:T(8,128)(2,1)S(1)} %get-tuple-element.25), channel_id=1, source_target_pairs={{0,8},{1,5},{2,10},{3,7},{4,12},{5,1},{6,14},{7,3},{8,0},{9,13},{1... | collective-permute-start | bytes 196616 | tf_op jit(solution)/shard_map/ppermute | solution.py:384
  34.8 0.5 collective-permute-start.12
  35.4 1.9 %collective-permute-done.14 = bf16[32,8,128]{2,1,0:T(8,128)(2,1)S(1)} collective-permute-done((bf16[32,8,128]{2,1,0:T(8,128)(2,1)S(1)}, bf16[32,8,128]{2,1,0:T(8,128)(2,1)S(1)}, u32[]{:S(2)}, u32[]{:S(2)}) %collective-permute-start.14) | collective-permute-done | bytes 65568 | tf_op jit(solution)/shard_map/ppermute | solution.py:384
  37.3 2.2 %collective-permute-start.16 = (bf16[96,8,128]{2,1,0:T(8,128)(2,1)S(1)}, bf16[96,8,128]{2,1,0:T(8,128)(2,1)S(1)}, u32[]{:S(2)}, u32[]{:S(2)}) collective-permute-start(bf16[96,8,128]{2,1,0:T(8,128)(2,1)S(1)} %constant_dynamic-update-slice_fusion.8.refs_3_), channel_id=1, source_target_pairs={{0,24},{1,7},{2,26},{3,5},{4,28},{5,3},{6,30},{7,1},{8,16},{9,15},... | collective-permute-start | bytes 589832 | tf_op jit(solution)/shard_map/ppermute | solution.py:384
  39.5 0.8 %collective-permute-start.17 = (bf16[96,8,128]{2,1,0:T(8,128)(2,1)S(1)}, bf16[96,8,128]{2,1,0:T(8,128)(2,1)S(1)}, u32[]{:S(2)}, u32[]{:S(2)}) collective-permute-start(bf16[96,8,128]{2,1,0:T(8,128)(2,1)S(1)} %constant_dynamic-update-slice_fusion.8.refs_3_), channel_id=1, source_target_pairs={{0,16},{1,3},{2,18},{3,1},{4,20},{5,7},{6,22},{7,5},{8,24},{9,11},... | collective-permute-start | bytes 589832 | tf_op jit(solution)/shard_map/ppermute | solution.py:384
  40.3 0.6 collective-permute-start.18
  41.0 0.5 collective-permute-start.20
  41.5 2.5 %collective-permute-done.16.refs_4_ = bf16[96,8,128]{2,1,0:T(8,128)(2,1)S(1)} collective-permute-done((bf16[96,8,128]{2,1,0:T(8,128)(2,1)S(1)}, bf16[96,8,128]{2,1,0:T(8,128)(2,1)S(1)}, u32[]{:S(2)}, u32[]{:S(2)}) %collective-permute-start.16) | collective-permute-done | bytes 196640 | tf_op jit(solution)/shard_map/ppermute | solution.py:384
  44.1 2.0 %collective-permute-done.17.refs_5_ = bf16[96,8,128]{2,1,0:T(8,128)(2,1)S(1)} collective-permute-done((bf16[96,8,128]{2,1,0:T(8,128)(2,1)S(1)}, bf16[96,8,128]{2,1,0:T(8,128)(2,1)S(1)}, u32[]{:S(2)}, u32[]{:S(2)}) %collective-permute-start.17) | collective-permute-done | bytes 196640 | tf_op jit(solution)/shard_map/ppermute | solution.py:384
  46.1 0.5 collective-permute-start.23
  46.6 0.9 %collective-permute-done.22.refs_10_ = bf16[96,8,128]{2,1,0:T(8,128)(2,1)S(1)} collective-permute-done((bf16[96,8,128]{2,1,0:T(8,128)(2,1)S(1)}, bf16[96,8,128]{2,1,0:T(8,128)(2,1)S(1)}, u32[]{:S(2)}, u32[]{:S(2)}) %collective-permute-start.22) | collective-permute-done | bytes 196640 | tf_op jit(solution)/shard_map/ppermute | solution.py:384
  47.5 0.3 collective-permute-done.23.refs_11_
  47.8 2.4 %later_sweep.3 = f32[32,8,128]{2,1,0:T(8,128)S(1)} custom-call(s32[64]{0:T(128)S(1)} %get-tuple-element.16.perm_ref.refs_0_, s32[1024]{0:T(1024)S(1)} %get-tuple-element.18.refs_1_, bf16[128,8,128]{2,1,0:T(8,128)(2,1)S(1)} %constant_dynamic-update-slice_fusion.4.refs_2_, bf16[96,8,128]{2,1,0:T(8,128)(2,1)S(1)} %constant_dynamic-update-slice_fusion.8.refs_3_, ...), custom_call_target="tpu_custom_call" | custom-call | tf_op jit(solution)/shard_map/later_sweep/pallas_call | solution.py:453
  50.2 11.8 %all_to_all.5 = f32[32,8,128]{2,1,0:T(8,128)S(1)} all-to-all(f32[32,8,128]{2,1,0:T(8,128)S(1)} %later_sweep.3), channel_id=1, replica_groups=mesh['grp'=4,'row'=8] {'grp','row'}, dimensions={0} | all-to-all | bytes 262144 | tf_op jit(solution)/shard_map/all_to_all | solution.py:479
  62.0 0.7 %lay_out.1 = f32[64,512]{1,0:T(8,128)} custom-call(f32[256,128]{1,0:T(8,128)S(1)} %bitcast.5), custom_call_target="tpu_custom_call" | custom-call | tf_op jit(solution)/shard_map/lay_out/pallas_call | solution.py:480
  (34 shorter events, 0.6 us)
Async XLA Ops:
  2.2 7.9 %collective-permute-start = (bf16[32,8,128]{2,1,0:T(8,128)(2,1)S(1)}, bf16[32,8,128]{2,1,0:T(8,128)(2,1)S(1)}, u32[]{:S(2)}, u32[]{:S(2)}) collective-permute-start(bf16[32,8,128]{2,1,0:T(8,128)(2,1)S(1)} %get-tuple-element.17.rounded_ref), channel_id=1, source_target_pairs={{0,6},{1,25},{2,4},{3,27},{4,2},{5,29},{6,0},{7,31},{8,14},{9,17},... | collective-permute-start | bytes 196616 | tf_op jit(solution)/shard_map/ppermute | solution.py:384
  7.4 5.2 %collective-permute-start.1 = (bf16[32,8,128]{2,1,0:T(8,128)(2,1)S(1)}, bf16[32,8,128]{2,1,0:T(8,128)(2,1)S(1)}, u32[]{:S(2)}, u32[]{:S(2)}) collective-permute-start(bf16[32,8,128]{2,1,0:T(8,128)(2,1)S(1)} %get-tuple-element.17.rounded_ref), channel_id=1, source_target_pairs={{0,4},{1,17},{2,6},{3,19},{4,0},{5,21},{6,2},{7,23},{8,12},{9,25},... | collective-permute-start | bytes 196616 | tf_op jit(solution)/shard_map/ppermute | solution.py:384
  7.4 5.2 %collective-permute-start.2 = (bf16[32,8,128]{2,1,0:T(8,128)(2,1)S(1)}, bf16[32,8,128]{2,1,0:T(8,128)(2,1)S(1)}, u32[]{:S(2)}, u32[]{:S(2)}) collective-permute-start(bf16[32,8,128]{2,1,0:T(8,128)(2,1)S(1)} %get-tuple-element.17.rounded_ref), channel_id=1, source_target_pairs={{0,2},{1,9},{2,0},{3,11},{4,6},{5,13},{6,4},{7,15},{8,10},{9,1},{1... | collective-permute-start | bytes 196616 | tf_op jit(solution)/shard_map/ppermute | solution.py:384
  12.6 7.4 %collective-permute-start.3 = (bf16[128,8,128]{2,1,0:T(8,128)(2,1)S(1)}, bf16[128,8,128]{2,1,0:T(8,128)(2,1)S(1)}, u32[]{:S(2)}, u32[]{:S(2)}) collective-permute-start(bf16[128,8,128]{2,1,0:T(8,128)(2,1)S(1)} %constant_dynamic-update-slice_fusion.gathered_ref.refs_5_), channel_id=1, source_target_pairs={{0,24},{1,7},{2,26},{3,5},{4,28},{5,3},{6,30},{7,1},{8,16},{9,15},... | collective-permute-start | bytes 786440 | tf_op jit(solution)/shard_map/ppermute | solution.py:384
  15.5 7.2 %collective-permute-start.4 = (bf16[128,8,128]{2,1,0:T(8,128)(2,1)S(1)}, bf16[128,8,128]{2,1,0:T(8,128)(2,1)S(1)}, u32[]{:S(2)}, u32[]{:S(2)}) collective-permute-start(bf16[128,8,128]{2,1,0:T(8,128)(2,1)S(1)} %constant_dynamic-update-slice_fusion.gathered_ref.refs_5_), channel_id=1, source_target_pairs={{0,16},{1,3},{2,18},{3,1},{4,20},{5,7},{6,22},{7,5},{8,24},{9,11},... | collective-permute-start | bytes 786440 | tf_op jit(solution)/shard_map/ppermute | solution.py:384
  16.0 6.8 %collective-permute-start.5 = (bf16[128,8,128]{2,1,0:T(8,128)(2,1)S(1)}, bf16[128,8,128]{2,1,0:T(8,128)(2,1)S(1)}, u32[]{:S(2)}, u32[]{:S(2)}) collective-permute-start(bf16[128,8,128]{2,1,0:T(8,128)(2,1)S(1)} %constant_dynamic-update-slice_fusion.gathered_ref.refs_5_), channel_id=1, source_target_pairs={{0,8},{1,5},{2,10},{3,7},{4,12},{5,1},{6,14},{7,3},{8,0},{9,13},{1... | collective-permute-start | bytes 786440 | tf_op jit(solution)/shard_map/ppermute | solution.py:384
  19.1 4.8 %collective-permute-start.9 = (bf16[128,8,128]{2,1,0:T(8,128)(2,1)S(1)}, bf16[128,8,128]{2,1,0:T(8,128)(2,1)S(1)}, u32[]{:S(2)}, u32[]{:S(2)}) collective-permute-start(bf16[128,8,128]{2,1,0:T(8,128)(2,1)S(1)} %get-tuple-element.20), channel_id=1, source_target_pairs={{0,1},{1,0},{2,3},{3,2},{4,5},{5,4},{6,7},{7,6},{8,9},{9,8},{10,11... | collective-permute-start | bytes 786440 | tf_op jit(solution)/shard_map/ppermute | solution.py:384
  20.0 3.9 %collective-permute-start.6 = (bf16[128,8,128]{2,1,0:T(8,128)(2,1)S(1)}, bf16[128,8,128]{2,1,0:T(8,128)(2,1)S(1)}, u32[]{:S(2)}, u32[]{:S(2)}) collective-permute-start(bf16[128,8,128]{2,1,0:T(8,128)(2,1)S(1)} %collective-permute-done.3.refs_2_), channel_id=1, source_target_pairs={{0,1},{1,0},{2,3},{3,2},{4,5},{5,4},{6,7},{7,6},{8,9},{9,8},{10,11... | collective-permute-start | bytes 786440 | tf_op jit(solution)/shard_map/ppermute | solution.py:384
  22.7 1.5 %collective-permute-start.7 = (bf16[128,8,128]{2,1,0:T(8,128)(2,1)S(1)}, bf16[128,8,128]{2,1,0:T(8,128)(2,1)S(1)}, u32[]{:S(2)}, u32[]{:S(2)}) collective-permute-start(bf16[128,8,128]{2,1,0:T(8,128)(2,1)S(1)} %collective-permute-done.4.refs_3_), channel_id=1, source_target_pairs={{0,1},{1,0},{2,3},{3,2},{4,5},{5,4},{6,7},{7,6},{8,9},{9,8},{10,11... | collective-permute-start | bytes 786440 | tf_op jit(solution)/shard_map/ppermute | solution.py:384
  22.8 2.2 %collective-permute-start.8 = (bf16[128,8,128]{2,1,0:T(8,128)(2,1)S(1)}, bf16[128,8,128]{2,1,0:T(8,128)(2,1)S(1)}, u32[]{:S(2)}, u32[]{:S(2)}) collective-permute-start(bf16[128,8,128]{2,1,0:T(8,128)(2,1)S(1)} %collective-permute-done.5.refs_4_), channel_id=1, source_target_pairs={{0,1},{1,0},{2,3},{3,2},{4,5},{5,4},{6,7},{7,6},{8,9},{9,8},{10,11... | collective-permute-start | bytes 786440 | tf_op jit(solution)/shard_map/ppermute | solution.py:384
  27.4 7.4 %collective-permute-start.13 = (bf16[32,8,128]{2,1,0:T(8,128)(2,1)S(1)}, bf16[32,8,128]{2,1,0:T(8,128)(2,1)S(1)}, u32[]{:S(2)}, u32[]{:S(2)}) collective-permute-start(bf16[32,8,128]{2,1,0:T(8,128)(2,1)S(1)} %get-tuple-element.25), channel_id=1, source_target_pairs={{0,6},{1,25},{2,4},{3,27},{4,2},{5,29},{6,0},{7,31},{8,14},{9,17},... | collective-permute-start | bytes 196616 | tf_op jit(solution)/shard_map/ppermute | solution.py:384
  29.9 7.4 %collective-permute-start.14 = (bf16[32,8,128]{2,1,0:T(8,128)(2,1)S(1)}, bf16[32,8,128]{2,1,0:T(8,128)(2,1)S(1)}, u32[]{:S(2)}, u32[]{:S(2)}) collective-permute-start(bf16[32,8,128]{2,1,0:T(8,128)(2,1)S(1)} %get-tuple-element.25), channel_id=1, source_target_pairs={{0,4},{1,17},{2,6},{3,19},{4,0},{5,21},{6,2},{7,23},{8,12},{9,25},... | collective-permute-start | bytes 196616 | tf_op jit(solution)/shard_map/ppermute | solution.py:384
  29.9 7.4 %collective-permute-start.15 = (bf16[32,8,128]{2,1,0:T(8,128)(2,1)S(1)}, bf16[32,8,128]{2,1,0:T(8,128)(2,1)S(1)}, u32[]{:S(2)}, u32[]{:S(2)}) collective-permute-start(bf16[32,8,128]{2,1,0:T(8,128)(2,1)S(1)} %get-tuple-element.25), channel_id=1, source_target_pairs={{0,2},{1,9},{2,0},{3,11},{4,6},{5,13},{6,4},{7,15},{8,10},{9,1},{1... | collective-permute-start | bytes 196616 | tf_op jit(solution)/shard_map/ppermute | solution.py:384
  31.9 8.4 %collective-permute-start.10 = (bf16[32,8,128]{2,1,0:T(8,128)(2,1)S(1)}, bf16[32,8,128]{2,1,0:T(8,128)(2,1)S(1)}, u32[]{:S(2)}, u32[]{:S(2)}) collective-permute-start(bf16[32,8,128]{2,1,0:T(8,128)(2,1)S(1)} %get-tuple-element.25), channel_id=1, source_target_pairs={{0,24},{1,7},{2,26},{3,5},{4,28},{5,3},{6,30},{7,1},{8,16},{9,15},... | collective-permute-start | bytes 196616 | tf_op jit(solution)/shard_map/ppermute | solution.py:384
  34.0 6.9 %collective-permute-start.11 = (bf16[32,8,128]{2,1,0:T(8,128)(2,1)S(1)}, bf16[32,8,128]{2,1,0:T(8,128)(2,1)S(1)}, u32[]{:S(2)}, u32[]{:S(2)}) collective-permute-start(bf16[32,8,128]{2,1,0:T(8,128)(2,1)S(1)} %get-tuple-element.25), channel_id=1, source_target_pairs={{0,8},{1,5},{2,10},{3,7},{4,12},{5,1},{6,14},{7,3},{8,0},{9,13},{1... | collective-permute-start | bytes 196616 | tf_op jit(solution)/shard_map/ppermute | solution.py:384
  34.8 6.1 %collective-permute-start.12 = (bf16[32,8,128]{2,1,0:T(8,128)(2,1)S(1)}, bf16[32,8,128]{2,1,0:T(8,128)(2,1)S(1)}, u32[]{:S(2)}, u32[]{:S(2)}) collective-permute-start(bf16[32,8,128]{2,1,0:T(8,128)(2,1)S(1)} %get-tuple-element.25), channel_id=1, source_target_pairs={{0,16},{1,3},{2,18},{3,1},{4,20},{5,7},{6,22},{7,5},{8,24},{9,11},... | collective-permute-start | bytes 196616 | tf_op jit(solution)/shard_map/ppermute | solution.py:384
  37.3 6.7 %collective-permute-start.16 = (bf16[96,8,128]{2,1,0:T(8,128)(2,1)S(1)}, bf16[96,8,128]{2,1,0:T(8,128)(2,1)S(1)}, u32[]{:S(2)}, u32[]{:S(2)}) collective-permute-start(bf16[96,8,128]{2,1,0:T(8,128)(2,1)S(1)} %constant_dynamic-update-slice_fusion.8.refs_3_), channel_id=1, source_target_pairs={{0,24},{1,7},{2,26},{3,5},{4,28},{5,3},{6,30},{7,1},{8,16},{9,15},... | collective-permute-start | bytes 589832 | tf_op jit(solution)/shard_map/ppermute | solution.py:384
  39.5 6.6 %collective-permute-start.17 = (bf16[96,8,128]{2,1,0:T(8,128)(2,1)S(1)}, bf16[96,8,128]{2,1,0:T(8,128)(2,1)S(1)}, u32[]{:S(2)}, u32[]{:S(2)}) collective-permute-start(bf16[96,8,128]{2,1,0:T(8,128)(2,1)S(1)} %constant_dynamic-update-slice_fusion.8.refs_3_), channel_id=1, source_target_pairs={{0,16},{1,3},{2,18},{3,1},{4,20},{5,7},{6,22},{7,5},{8,24},{9,11},... | collective-permute-start | bytes 589832 | tf_op jit(solution)/shard_map/ppermute | solution.py:384
  40.3 5.8 %collective-permute-start.18 = (bf16[96,8,128]{2,1,0:T(8,128)(2,1)S(1)}, bf16[96,8,128]{2,1,0:T(8,128)(2,1)S(1)}, u32[]{:S(2)}, u32[]{:S(2)}) collective-permute-start(bf16[96,8,128]{2,1,0:T(8,128)(2,1)S(1)} %constant_dynamic-update-slice_fusion.8.refs_3_), channel_id=1, source_target_pairs={{0,8},{1,5},{2,10},{3,7},{4,12},{5,1},{6,14},{7,3},{8,0},{9,13},{1... | collective-permute-start | bytes 589832 | tf_op jit(solution)/shard_map/ppermute | solution.py:384
  41.0 5.6 %collective-permute-start.19 = (bf16[128,8,128]{2,1,0:T(8,128)(2,1)S(1)}, bf16[128,8,128]{2,1,0:T(8,128)(2,1)S(1)}, u32[]{:S(2)}, u32[]{:S(2)}) collective-permute-start(bf16[128,8,128]{2,1,0:T(8,128)(2,1)S(1)} %constant_dynamic-update-slice_fusion.4.refs_2_), channel_id=1, source_target_pairs={{0,1},{1,0},{2,3},{3,2},{4,5},{5,4},{6,7},{7,6},{8,9},{9,8},{10,11... | collective-permute-start | bytes 786440 | tf_op jit(solution)/shard_map/ppermute | solution.py:384
  41.0 5.5 %collective-permute-start.20 = (bf16[96,8,128]{2,1,0:T(8,128)(2,1)S(1)}, bf16[96,8,128]{2,1,0:T(8,128)(2,1)S(1)}, u32[]{:S(2)}, u32[]{:S(2)}) collective-permute-start(bf16[96,8,128]{2,1,0:T(8,128)(2,1)S(1)} %constant_dynamic-update-slice_fusion.8.refs_3_), channel_id=1, source_target_pairs={{0,1},{1,0},{2,3},{3,2},{4,5},{5,4},{6,7},{7,6},{8,9},{9,8},{10,11... | collective-permute-start | bytes 589832 | tf_op jit(solution)/shard_map/ppermute | solution.py:384
  44.1 2.5 %collective-permute-start.21 = (bf16[96,8,128]{2,1,0:T(8,128)(2,1)S(1)}, bf16[96,8,128]{2,1,0:T(8,128)(2,1)S(1)}, u32[]{:S(2)}, u32[]{:S(2)}) collective-permute-start(bf16[96,8,128]{2,1,0:T(8,128)(2,1)S(1)} %collective-permute-done.16.refs_4_), channel_id=1, source_target_pairs={{0,1},{1,0},{2,3},{3,2},{4,5},{5,4},{6,7},{7,6},{8,9},{9,8},{10,11... | collective-permute-start | bytes 589832 | tf_op jit(solution)/shard_map/ppermute | solution.py:384
  46.1 1.4 %collective-permute-start.22 = (bf16[96,8,128]{2,1,0:T(8,128)(2,1)S(1)}, bf16[96,8,128]{2,1,0:T(8,128)(2,1)S(1)}, u32[]{:S(2)}, u32[]{:S(2)}) collective-permute-start(bf16[96,8,128]{2,1,0:T(8,128)(2,1)S(1)} %collective-permute-done.17.refs_5_), channel_id=1, source_target_pairs={{0,1},{1,0},{2,3},{3,2},{4,5},{5,4},{6,7},{7,6},{8,9},{9,8},{10,11... | collective-permute-start | bytes 589832 | tf_op jit(solution)/shard_map/ppermute | solution.py:384
  46.1 1.7 %collective-permute-start.23 = (bf16[96,8,128]{2,1,0:T(8,128)(2,1)S(1)}, bf16[96,8,128]{2,1,0:T(8,128)(2,1)S(1)}, u32[]{:S(2)}, u32[]{:S(2)}) collective-permute-start(bf16[96,8,128]{2,1,0:T(8,128)(2,1)S(1)} %collective-permute-done.18.refs_6_), channel_id=1, source_target_pairs={{0,1},{1,0},{2,3},{3,2},{4,5},{5,4},{6,7},{7,6},{8,9},{9,8},{10,11... | collective-permute-start | bytes 589832 | tf_op jit(solution)/shard_map/ppermute | solution.py:384
